TPU v7x, 32 devices: a whole 2x2x4 slice. The times are simulated.
32 devices in a mesh: section: 2 (over x), dp: 16 (over z, y, core).
Axes of the slice: x: 2, y: 2, z: 4, core: 2. Of those that a mesh axis runs over, the one named last changes fastest.
Arguments:
- tokens: bfloat16 [8192, 768], P('dp'), may hold values from -6 to 6
- cotangent: bfloat16 [8192, 768], P('dp'), may hold values from -6 to 6
- heights: int32 [32], P('dp'), may hold values from 12 to 16
- widths: int32 [32], P('dp'), may hold values from 12 to 16
- qkv_weight: bfloat16 [2, 768, 2304], P('section', 'dp'), may hold values from -0.21875 to 0.21875
- out_weight: bfloat16 [2, 768, 768], P('section', 'dp'), may hold values from -0.875 to 0.875
- up_weight: bfloat16 [2, 768, 3072], P('section', 'dp'), may hold values from -0.21875 to 0.21875
- down_weight: bfloat16 [2, 3072, 768], P('section', 'dp'), may hold values from -0.109375 to 0.109375
- q_bias: bfloat16 [2, 768], P('section', 'dp'), may hold values from -1.5 to 1.5
- v_bias: bfloat16 [2, 768], P('section', 'dp'), may hold values from -1.5 to 1.5
- out_bias: bfloat16 [2, 768], P('section', 'dp'), may hold values from -1.5 to 1.5
- up_bias: bfloat16 [2, 3072], P('section', 'dp'), may hold values from -1.5 to 1.5
- down_bias: bfloat16 [2, 768], P('section', 'dp'), may hold values from -1.5 to 1.5
- gain_one: bfloat16 [2, 768], P('section', 'dp'), may hold values from 0.25 to 1.75
- shift_one: bfloat16 [2, 768], P('section', 'dp'), may hold values from -1.5 to 1.5
- gain_two: bfloat16 [2, 768], P('section', 'dp'), may hold values from 0.25 to 1.75
- shift_two: bfloat16 [2, 768], P('section', 'dp'), may hold values from -1.5 to 1.5
Outputs:
- layer_outputs: bfloat16 [2, 8192, 768], P('section', 'dp')
- input_grads: float32 [2, 8192, 768], P('section', 'dp')
- grad_qkv_weight: float32 [2, 768, 2304], P('section', 'dp')
- grad_out_weight: float32 [2, 768, 768], P('section', 'dp')
- grad_up_weight: float32 [2, 768, 3072], P('section', 'dp')
- grad_down_weight: float32 [2, 3072, 768], P('section', 'dp')
- grad_q_bias: float32 [2, 768], P('section', 'dp')
- grad_v_bias: float32 [2, 768], P('section', 'dp')
- grad_out_bias: float32 [2, 768], P('section', 'dp')
- grad_up_bias: float32 [2, 3072], P('section', 'dp')
- grad_down_bias: float32 [2, 768], P('section', 'dp')
- grad_gain_one: float32 [2, 768], P('section', 'dp')
- grad_shift_one: float32 [2, 768], P('section', 'dp')
- grad_gain_two: float32 [2, 768], P('section', 'dp')
- grad_shift_two: float32 [2, 768], P('section', 'dp')
All inputs are finite; a program needn't handle non-finite values.
Results may differ from a plain program's by a relative error of at most 0.014.
Values may be sent and summed in bfloat16 or wider, within the bound.
No kernel may reach another device: no remote copies, remote signals or barrier semaphores. Data moves between devices by JAX's collectives and lax.ppermute only.
A program may use at most 256 MiB of HBM per device.

v0:
```python
import jax
import jax.numpy as jnp
from jax import lax
from jax.sharding import PartitionSpec as P

H = 16
GRID = 16
MICRO = 2


eps_norm = 1e-05


def passed_along(block, axis, distance):
    devices = range(lax.axis_size(axis))
    route = [(i - distance, i) for i in devices if i - distance in devices]
    return lax.ppermute(block, axis, route)


def layer_norm(values_in, gain_vec, offset_vec):
    average = jnp.mean(values_in, axis=-1, keepdims=True)
    centred = values_in - average
    variance = jnp.mean(centred * centred, axis=-1, keepdims=True)
    return centred * lax.rsqrt(variance + eps_norm) * gain_vec + offset_vec


def gelu_exact(values_in):
    return jax.nn.gelu(values_in, approximate=False)


def product(first_mat, second_mat):
    return jnp.dot(first_mat, second_mat, preferred_element_type=jnp.float32)


def outer_sum(first_mat, second_mat):
    return lax.dot_general(
        first_mat, second_mat, (((0,), (0,)), ((), ())), preferred_element_type=jnp.float32
    )


def back_product(first_mat, second_mat):
    return lax.dot_general(
        first_mat, second_mat, (((1,), (1,)), ((), ())), preferred_element_type=jnp.float32
    )


def head_split(matrix, valid_mask):
    images, slots = valid_mask.shape
    return matrix.reshape(images, slots, H, matrix.shape[1] // H)


def attend(queries, key_rows, values, valid_mask):
    images, slots = valid_mask.shape
    score_scale = (queries.shape[1] // H) ** (-0.5)
    query_four = head_split(queries, valid_mask)
    key_four = head_split(key_rows, valid_mask)
    value_four = head_split(values, valid_mask)
    scores = (
        jnp.einsum("iqhd,ikhd->ihqk", query_four, key_four, preferred_element_type=jnp.float32)
        * score_scale
    )
    scores = jnp.where(valid_mask[:, None, None, :], scores, -1e30)
    largest = jnp.max(scores, axis=-1, keepdims=True)
    exponent = jnp.exp(scores - largest)
    denominator = jnp.sum(exponent, axis=-1, keepdims=True)
    soft_weights = (exponent / denominator).astype(jnp.bfloat16)
    attended = jnp.einsum(
        "ihqk,ikhd->iqhd", soft_weights, value_four, preferred_element_type=jnp.float32
    )
    log_total = (largest + jnp.log(denominator))[..., 0]
    return (attended.reshape(images * slots, -1).astype(jnp.bfloat16), log_total)


def attend_back(queries, key_rows, values, log_total, valid_mask, grad_attended):
    images, slots = valid_mask.shape
    score_scale = (queries.shape[1] // H) ** (-0.5)
    query_four = head_split(queries, valid_mask)
    key_four = head_split(key_rows, valid_mask)
    value_four = head_split(values, valid_mask)
    grad_four = head_split(grad_attended, valid_mask)
    scores = (
        jnp.einsum("iqhd,ikhd->ihqk", query_four, key_four, preferred_element_type=jnp.float32)
        * score_scale
    )
    scores = jnp.where(valid_mask[:, None, None, :], scores, -1e30)
    soft_full = jnp.exp(scores - log_total[..., None])
    grad_soft = jnp.einsum(
        "iqhd,ikhd->ihqk", grad_four, value_four, preferred_element_type=jnp.float32
    )
    grad_value = jnp.einsum(
        "ihqk,iqhd->ikhd",
        soft_full.astype(jnp.bfloat16),
        grad_four,
        preferred_element_type=jnp.float32,
    )
    row_terms = jnp.sum(soft_full * grad_soft, axis=-1, keepdims=True)
    grad_scores = (soft_full * (grad_soft - row_terms)).astype(jnp.bfloat16)
    grad_query = (
        jnp.einsum("ihqk,ikhd->iqhd", grad_scores, key_four, preferred_element_type=jnp.float32)
        * score_scale
    )
    grad_key = (
        jnp.einsum("ihqk,iqhd->ikhd", grad_scores, query_four, preferred_element_type=jnp.float32)
        * score_scale
    )
    row_count = images * slots
    return (
        grad_query.reshape(row_count, -1),
        grad_key.reshape(row_count, -1),
        grad_value.reshape(row_count, -1),
    )


def forward_layer(params, layer_input, valid_mask):
    (
        qkv_w,
        out_w,
        up_w,
        down_w,
        bias_q,
        bias_v,
        bias_out,
        bias_up,
        bias_down,
        gain_a,
        offset_a,
        gain_b,
        offset_b,
    ) = params
    model_width = qkv_w.shape[0]
    normed = layer_norm(
        layer_input, gain_a.astype(jnp.float32), offset_a.astype(jnp.float32)
    ).astype(jnp.bfloat16)
    projected = product(normed, qkv_w)
    queries = (projected[:, :model_width] + bias_q.astype(jnp.float32)).astype(jnp.bfloat16)
    key_rows = projected[:, model_width : 2 * model_width].astype(jnp.bfloat16)
    values = (projected[:, 2 * model_width :] + bias_v.astype(jnp.float32)).astype(jnp.bfloat16)
    attended, log_total = attend(queries, key_rows, values, valid_mask)
    middle = layer_input + (product(attended, out_w) + bias_out.astype(jnp.float32))
    second = layer_norm(middle, gain_b.astype(jnp.float32), offset_b.astype(jnp.float32)).astype(
        jnp.bfloat16
    )
    hidden_pre = product(second, up_w) + bias_up.astype(jnp.float32)
    activated = gelu_exact(hidden_pre).astype(jnp.bfloat16)
    result = middle + (product(activated, down_w) + bias_down.astype(jnp.float32))
    saved = (
        layer_input,
        normed,
        queries,
        key_rows,
        values,
        log_total,
        attended,
        middle,
        second,
        hidden_pre,
        activated,
    )
    return (result, saved)


def blank_forward(params, layer_input, valid_mask):
    row_count, model_width = layer_input.shape
    hidden_width = params[2].shape[1]
    images, slots = valid_mask.shape
    zero_wide = jnp.zeros((row_count, model_width), jnp.float32)
    zero_narrow = jnp.zeros((row_count, model_width), jnp.bfloat16)
    saved = (
        zero_wide,
        zero_narrow,
        zero_narrow,
        zero_narrow,
        zero_narrow,
        jnp.zeros((images, H, slots), jnp.float32),
        zero_narrow,
        zero_wide,
        zero_narrow,
        jnp.zeros((row_count, hidden_width), jnp.float32),
        jnp.zeros((row_count, hidden_width), jnp.bfloat16),
    )
    return (zero_wide, saved)


def blank_grads(arrays):
    return tuple((jnp.zeros(array.shape, jnp.float32) for array in arrays))


def mlp_params(params):
    return (params[2], params[3], params[7], params[8], params[11], params[12])


def attn_params(params):
    return (params[0], params[1], params[4], params[5], params[6], params[9], params[10])


def backward_mlp(params, saved, upstream):
    down_w = params[3]
    up_w = params[2]
    middle, second, hidden_pre, activated = (saved[7], saved[8], saved[9], saved[10])
    grad_result = upstream.astype(jnp.bfloat16)
    grad_down = outer_sum(activated, grad_result)
    grad_down_bias = jnp.sum(grad_result.astype(jnp.float32), axis=0)
    grad_act = back_product(grad_result, down_w)
    grad_pre = jax.vjp(gelu_exact, hidden_pre)[1](grad_act)[0].astype(jnp.bfloat16)
    grad_up = outer_sum(second, grad_pre)
    grad_up_bias = jnp.sum(grad_pre.astype(jnp.float32), axis=0)
    grad_second = back_product(grad_pre, up_w)
    pullback = jax.vjp(
        layer_norm, middle, params[11].astype(jnp.float32), params[12].astype(jnp.float32)
    )[1]
    grad_mid, grad_gain, grad_offset = pullback(grad_second)
    return (
        upstream + grad_mid,
        (grad_up, grad_down, grad_up_bias, grad_down_bias, grad_gain, grad_offset),
    )


def backward_attn(params, saved, valid_mask, grad_middle):
    qkv_w, out_w = (params[0], params[1])
    layer_input, normed, queries, key_rows, values, log_total, attended = saved[:7]
    grad_branch = grad_middle.astype(jnp.bfloat16)
    grad_out = outer_sum(attended, grad_branch)
    grad_out_bias = jnp.sum(grad_branch.astype(jnp.float32), axis=0)
    grad_attended = back_product(grad_branch, out_w).astype(jnp.bfloat16)
    grad_query, grad_key, grad_value = attend_back(
        queries, key_rows, values, log_total, valid_mask, grad_attended
    )
    query_low = grad_query.astype(jnp.bfloat16)
    value_low = grad_value.astype(jnp.bfloat16)
    grad_joint = jnp.concatenate([query_low, grad_key.astype(jnp.bfloat16), value_low], axis=1)
    grad_qkv = outer_sum(normed, grad_joint)
    grad_q_bias = jnp.sum(query_low.astype(jnp.float32), axis=0)
    grad_v_bias = jnp.sum(value_low.astype(jnp.float32), axis=0)
    grad_normed = back_product(grad_joint, qkv_w)
    pullback = jax.vjp(
        layer_norm, layer_input, params[9].astype(jnp.float32), params[10].astype(jnp.float32)
    )[1]
    grad_in, grad_gain, grad_offset = pullback(grad_normed)
    return (
        grad_middle + grad_in,
        (grad_qkv, grad_out, grad_q_bias, grad_v_bias, grad_out_bias, grad_gain, grad_offset),
    )


def piece_of(array, index, size):
    return lax.slice_in_dim(array, index * size, (index + 1) * size, axis=0)


def shards(
    tokens,
    cotangent,
    heights,
    widths,
    qkv_weight,
    out_weight,
    up_weight,
    down_weight,
    q_bias,
    v_bias,
    out_bias,
    up_bias,
    down_bias,
    gain_one,
    shift_one,
    gain_two,
    shift_two,
):
    leading = lax.axis_index("section") == 0
    gathered = (
        lax.all_gather(qkv_weight, "dp", axis=1, tiled=True),
        lax.all_gather(out_weight, "dp", axis=1, tiled=True),
        lax.all_gather(up_weight, "dp", axis=1, tiled=True),
        lax.all_gather(down_weight, "dp", axis=1, tiled=True),
        lax.all_gather(q_bias, "dp", axis=1, tiled=True),
        lax.all_gather(v_bias, "dp", axis=1, tiled=True),
        lax.all_gather(out_bias, "dp", axis=1, tiled=True),
        lax.all_gather(up_bias, "dp", axis=1, tiled=True),
        lax.all_gather(down_bias, "dp", axis=1, tiled=True),
        lax.all_gather(gain_one, "dp", axis=1, tiled=True),
        lax.all_gather(shift_one, "dp", axis=1, tiled=True),
        lax.all_gather(gain_two, "dp", axis=1, tiled=True),
        lax.all_gather(shift_two, "dp", axis=1, tiled=True),
    )
    params = tuple((piece[0] for piece in gathered))
    position = jnp.arange(GRID * GRID, dtype=jnp.int32)
    valid = ((position // GRID)[None, :] < heights[:, None]) & (
        (position % GRID)[None, :] < widths[:, None]
    )
    micro_count = MICRO
    row_count = tokens.shape[0] // micro_count
    image_count = valid.shape[0] // micro_count
    model_width = tokens.shape[1]
    received = jnp.zeros((row_count, model_width), jnp.bfloat16)
    saved_moments = []
    out_moments = []
    for moment in range(micro_count + 1):
        lead_index = min(moment, micro_count - 1)
        lag_index = max(moment - 1, 0)
        layer_input = jnp.where(leading, piece_of(tokens, lead_index, row_count), received).astype(
            jnp.float32
        )
        valid_mask = jnp.where(
            leading,
            piece_of(valid, lead_index, image_count),
            piece_of(valid, lag_index, image_count),
        )
        active = jnp.where(leading, moment < micro_count, moment >= 1)
        result, saved = lax.cond(
            active,
            lambda: forward_layer(params, layer_input, valid_mask),
            lambda: blank_forward(params, layer_input, valid_mask),
        )
        outgoing = result.astype(jnp.bfloat16)
        saved_moments.append((saved, valid_mask))
        out_moments.append(outgoing)
        if moment < micro_count:
            received = passed_along(outgoing, "section", 1)
    mlp_totals = blank_grads(mlp_params(params))
    attn_totals = blank_grads(attn_params(params))
    arriving = jnp.zeros((row_count, model_width), jnp.bfloat16)
    grad_moments = []
    for moment in range(micro_count + 1):
        saved, valid_mask = saved_moments[micro_count - moment]
        seed_index = max(micro_count - 1 - moment, 0)
        upstream = jnp.where(
            leading,
            arriving.astype(jnp.float32),
            piece_of(cotangent, seed_index, row_count).astype(jnp.float32),
        )
        active = jnp.where(leading, moment >= 1, moment < micro_count)
        grad_middle, mlp_grads = lax.cond(
            active,
            lambda: backward_mlp(params, saved, upstream),
            lambda: (jnp.zeros_like(upstream), blank_grads(mlp_params(params))),
        )
        mlp_totals = tuple((total + grad for total, grad in zip(mlp_totals, mlp_grads)))
        grad_input, attn_grads = lax.cond(
            active,
            lambda: backward_attn(params, saved, valid_mask, grad_middle),
            lambda: (jnp.zeros_like(grad_middle), blank_grads(attn_params(params))),
        )
        attn_totals = tuple((total + grad for total, grad in zip(attn_totals, attn_grads)))
        grad_moments.append(grad_input)
        if moment < micro_count:
            arriving = passed_along(grad_input.astype(jnp.bfloat16), "section", -1)
    summed = (
        lax.psum_scatter(attn_totals[0][None], "dp", scatter_dimension=1, tiled=True),
        lax.psum_scatter(attn_totals[1][None], "dp", scatter_dimension=1, tiled=True),
        lax.psum_scatter(mlp_totals[0][None], "dp", scatter_dimension=1, tiled=True),
        lax.psum_scatter(mlp_totals[1][None], "dp", scatter_dimension=1, tiled=True),
        lax.psum_scatter(attn_totals[2][None], "dp", scatter_dimension=1, tiled=True),
        lax.psum_scatter(attn_totals[3][None], "dp", scatter_dimension=1, tiled=True),
        lax.psum_scatter(attn_totals[4][None], "dp", scatter_dimension=1, tiled=True),
        lax.psum_scatter(mlp_totals[2][None], "dp", scatter_dimension=1, tiled=True),
        lax.psum_scatter(mlp_totals[3][None], "dp", scatter_dimension=1, tiled=True),
        lax.psum_scatter(attn_totals[5][None], "dp", scatter_dimension=1, tiled=True),
        lax.psum_scatter(attn_totals[6][None], "dp", scatter_dimension=1, tiled=True),
        lax.psum_scatter(mlp_totals[4][None], "dp", scatter_dimension=1, tiled=True),
        lax.psum_scatter(mlp_totals[5][None], "dp", scatter_dimension=1, tiled=True),
    )
    (
        grad_qkv_w,
        grad_out_w,
        grad_up_w,
        grad_down_w,
        grad_q_b,
        grad_v_b,
        grad_out_b,
        grad_up_b,
        grad_down_b,
        grad_gain_a,
        grad_offset_a,
        grad_gain_b,
        grad_offset_b,
    ) = summed
    layer_outputs = jnp.concatenate(
        [
            jnp.where(leading, out_moments[index], out_moments[index + 1])
            for index in range(micro_count)
        ],
        axis=0,
    )
    input_grads = jnp.concatenate(
        [
            jnp.where(
                leading, grad_moments[micro_count - index], grad_moments[micro_count - 1 - index]
            )
            for index in range(micro_count)
        ],
        axis=0,
    )
    return (
        layer_outputs[None],
        input_grads[None],
        grad_qkv_w,
        grad_out_w,
        grad_up_w,
        grad_down_w,
        grad_q_b,
        grad_v_b,
        grad_out_b,
        grad_up_b,
        grad_down_b,
        grad_gain_a,
        grad_offset_a,
        grad_gain_b,
        grad_offset_b,
    )


def solution(mesh):
    in_specs = (
        P("dp", None),
        P("dp", None),
        P("dp"),
        P("dp"),
        P("section", "dp", None),
        P("section", "dp", None),
        P("section", "dp", None),
        P("section", "dp", None),
        P("section", "dp"),
        P("section", "dp"),
        P("section", "dp"),
        P("section", "dp"),
        P("section", "dp"),
        P("section", "dp"),
        P("section", "dp"),
        P("section", "dp"),
        P("section", "dp"),
    )
    out_specs = (
        P("section", "dp", None),
        P("section", "dp", None),
        P("section", "dp", None),
        P("section", "dp", None),
        P("section", "dp", None),
        P("section", "dp", None),
        P("section", "dp"),
        P("section", "dp"),
        P("section", "dp"),
        P("section", "dp"),
        P("section", "dp"),
        P("section", "dp"),
        P("section", "dp"),
        P("section", "dp"),
        P("section", "dp"),
    )
    return jax.shard_map(shards, mesh=mesh, in_specs=in_specs, out_specs=out_specs, check_vma=False)
```

profile of v0, /device:TPU:0, one launch (start us, length us, event | category | flops | bytes accessed | tf_op | source)
XLA Modules:
  0.0 1464.3 jit_solution(4428403294134835281)
XLA Ops:
  20.2 63.6 %all-reduce.9 = (bf16[768]{0:T(1024)(128)(2,1)S(1)}, bf16[768]{0:T(1024)(128)(2,1)S(1)}, bf16[768]{0:T(1024)(128)(2,1)S(1)}, bf16[768]{0:T(1024)(128)(2,1)S(1)},...) all-reduce(bf16[768]{0:T(1024)(128)(2,1)S(1)} %dynamic-update-slice, ...), channel_id=1, replica_groups=mesh['section'=2,'dp'=16] {'dp'}, use_global_device_ids=true, to_apply=%add | all-reduce | flops 9216 | bytes 36864 | tf_op jit(solution)/shard_map/squeeze | solution.py:284
  86.7 13.3 all-gather.5.cloned.1.call-done
  100.0 54.7 %all-gather.9.cloned.1.call-done = bf16[1,768,3072]{2,1,0:T(8,128)(2,1)} async-done(((bf16[1,48,3072]{2,1,0:T(8,128)(2,1)}), bf16[1,768,3072]{2,1,0:T(8,128)(2,1)}) %all-gather.9.cloned.1.call-update) | async-done | bytes 4718608 | tf_op jit(solution)/shard_map/all_gather | solution.py:272
  154.7 54.1 %all-gather.11.cloned.1.call-done = bf16[1,3072,768]{2,1,0:T(8,128)(2,1)} async-done(((bf16[1,192,768]{2,1,0:T(8,128)(2,1)}), bf16[1,3072,768]{2,1,0:T(8,128)(2,1)}) %all-gather.11.cloned.1.call-update) | async-done | bytes 4718608 | tf_op jit(solution)/shard_map/all_gather | solution.py:273
  208.9 33.0 %conditional.6 = (f32[256,768]{1,0:T(8,128)S(1)}, bf16[256,768]{1,0:T(8,128)(2,1)S(1)}, bf16[256,768]{1,0:T(8,128)(2,1)}, bf16[256,768]{1,0:T(8,128)(2,1)}, bf16...) conditional(s32[]{:T(128)} %convert_element_type.550, () %tuple.69, ...), branch_computations={%region_0.1_spmd, %region_1.8_spmd} | conditional | flops 3895203328 | bytes 93927192 | solution.py:308
  212.7 3.2 fusion.183
  227.7 10.4 fusion.31
  238.1 3.9 fusion.43
  264.1 11.1 multiply_convert_fusion.3
  277.4 5.0 collective-permute-start.1
  283.8 6.5 collective-permute-done.1
  290.3 8.9 conditional.7
  300.1 11.6 conditional.8
  302.5 4.2 broadcast.1059.clone
  306.8 4.8 broadcast.1058.clone
  311.8 8.1 conditional.9
  316.4 3.3 broadcast.1098.clone
  319.9 8.6 collective-permute-start.2
  329.3 120.2 %collective-permute-done.2 = bf16[256,768]{1,0:T(8,128)(2,1)S(1)} collective-permute-done((bf16[256,768]{1,0:T(8,128)(2,1)S(1)}, bf16[256,768]{1,0:T(8,128)(2,1)S(1)}, u32[]{:S(2)}, u32[]{:S(2)}) %collective-permute-start.2) | collective-permute-done | bytes 393248 | tf_op jit(solution)/shard_map/ppermute | solution.py:17
  451.4 7.0 convert_reduce_fusion.10
  477.9 8.5 collective-permute-done.3
  487.4 52.9 %conditional.10 = (f32[256,768]{1,0:T(8,128)S(1)}, f32[3072]{0:T(1024)}, f32[768]{0:T(1024)}, f32[768]{0:T(1024)}, f32[768]{0:T(1024)}, /*index=5*/f32[768,3072]{1,0:T(8,128)}, f32[3072,768]{1,0:T(8,128)}) conditional(s32[]{:T(128)} %convert_element_type.550, () %tuple.74, (pred[]{:T(512)}, f32[256,768]{1,0:T(8,128)}, f32[256,768]{1,0:T(8,128)}, ...), branch_computations={%region_49.50_spmd, %region_50.0_spmd} | conditional | flops 4894946304 | bytes 109366976 | solution.py:331
  491.9 11.1 convert_reduce_fusion.2
  503.1 3.6 multiply_reduce_fusion.3
  508.3 6.1 convolution_bitcast_fusion.3
  514.4 9.6 copy.197
  524.0 6.6 convolution_bitcast_fusion.2
  530.6 9.7 copy.199
  545.4 48.4 %conditional.11 = (f32[256,768]{1,0:T(8,128)}, f32[768,768]{1,0:T(8,128)}, f32[768]{0:T(1024)}, f32[768]{0:T(1024)}, f32[768]{0:T(1024)}, /*index=5*/f32[768]{0:T(1024)}, f32[768]{0:T(1024)}, f32[768,2304]{1,0:T(8,128)}) conditional(s32[]{:T(128)} %convert_element_type.550, () %tuple.73, (pred[1,256]{1,0:T(4,128)(4,1)}, ...), branch_computations={%region_59.60_spmd, %region_60.71_spmd} | conditional | flops 2949114624 | bytes 121419000 | solution.py:337
  568.3 4.0 multiply_reduce_fusion.14
  575.8 4.0 multiply_reduce_fusion.15
  581.8 4.0 convolution_bitcast_fusion.5
  585.8 8.1 copy.201
  605.0 4.5 add_bitcast_fusion.5
  609.8 9.4 add_bitcast_fusion.4
  622.5 10.8 add_bitcast_fusion.3
  636.2 11.0 add_bitcast_fusion.2
  655.5 56.3 %reduce-scatter.56.cloned.1.call-done = f32[48,1]{1,0:T(8,128)} async-done(((f32[768,1]{1,0:T(8,128)}), f32[48,1]{1,0:T(8,128)}) %reduce-scatter.56.cloned.1.call-update) | async-done | bytes 208
  713.1 57.2 %reduce-scatter.40.cloned.1.call-done = f32[48,1]{1,0:T(8,128)} async-done(((f32[768,1]{1,0:T(8,128)}), f32[48,1]{1,0:T(8,128)}) %reduce-scatter.40.cloned.1.call-update) | async-done | bytes 208
  771.7 56.8 %reduce-scatter.42.cloned.1.call-done = f32[48,1]{1,0:T(8,128)} async-done(((f32[768,1]{1,0:T(8,128)}), f32[48,1]{1,0:T(8,128)}) %reduce-scatter.42.cloned.1.call-update) | async-done | bytes 208
  829.8 57.0 %reduce-scatter.44.cloned.1.call-done = f32[48,1]{1,0:T(8,128)} async-done(((f32[768,1]{1,0:T(8,128)}), f32[48,1]{1,0:T(8,128)}) %reduce-scatter.44.cloned.1.call-update) | async-done | bytes 208
  888.1 56.9 %reduce-scatter.50.cloned.1.call-done = f32[48,1]{1,0:T(8,128)} async-done(((f32[768,1]{1,0:T(8,128)}), f32[48,1]{1,0:T(8,128)}) %reduce-scatter.50.cloned.1.call-update) | async-done | bytes 208
  946.3 57.1 %reduce-scatter.52.cloned.1.call-done = f32[48,1]{1,0:T(8,128)} async-done(((f32[768,1]{1,0:T(8,128)}), f32[48,1]{1,0:T(8,128)}) %reduce-scatter.52.cloned.1.call-update) | async-done | bytes 208
  1004.7 60.9 %reduce-scatter.46.cloned.1.call-done = f32[192,1]{1,0:T(8,128)} async-done(((f32[3072,1]{1,0:T(8,128)}), f32[192,1]{1,0:T(8,128)}) %reduce-scatter.46.cloned.1.call-update) | async-done | bytes 784
  1067.1 65.2 %reduce-scatter.34.cloned.1.call-done = f32[1,48,768]{2,1,0:T(8,128)} async-done(((f32[1,768,768]{2,1,0:T(8,128)}), f32[1,48,768]{2,1,0:T(8,128)}) %reduce-scatter.34.cloned.1.call-update) | async-done | bytes 147472 | tf_op jit(solution)/shard_map/reduce_scatter | solution.py:348
  1132.3 93.5 %reduce-scatter.32.cloned.1.call-done = f32[1,48,2304]{2,1,0:T(8,128)} async-done(((f32[1,768,2304]{2,1,0:T(8,128)}), f32[1,48,2304]{2,1,0:T(8,128)}) %reduce-scatter.32.cloned.1.call-update) | async-done | bytes 442384 | tf_op jit(solution)/shard_map/reduce_scatter | solution.py:347
  1225.8 116.0 %reduce-scatter.36.cloned.1.call-done = f32[1,48,3072]{2,1,0:T(8,128)} async-done(((f32[1,768,3072]{2,1,0:T(8,128)}), f32[1,48,3072]{2,1,0:T(8,128)}) %reduce-scatter.36.cloned.1.call-update) | async-done | bytes 589840 | tf_op jit(solution)/shard_map/reduce_scatter | solution.py:349
  1341.9 115.7 %reduce-scatter.38.cloned.1.call-done = f32[1,192,768]{2,1,0:T(8,128)} async-done(((f32[1,3072,768]{2,1,0:T(8,128)}), f32[1,192,768]{2,1,0:T(8,128)}) %reduce-scatter.38.cloned.1.call-update) | async-done | bytes 589840 | tf_op jit(solution)/shard_map/reduce_scatter | solution.py:350
  (504 shorter events, 168.4 us)
Async XLA Ops:
  7.2 79.6 %all-gather.7.cloned.1.call-start = ((), (), s32[]{:S(2)}) async-start(), calls=%async_computation.14 | async-start | bytes 1253376 | tf_op jit(solution)/shard_map/all_gather | solution.py:271
  7.9 92.1 %all-gather.5.cloned.1.call-start = ((), (), s32[]{:S(2)}) async-start(), calls=%async_computation.13 | async-start | bytes 3760128 | tf_op jit(solution)/shard_map/all_gather | solution.py:270
  8.7 146.0 %all-gather.9.cloned.1.call-start = ((), (), s32[]{:S(2)}) async-start(), calls=%async_computation.15 | async-start | bytes 5013504 | tf_op jit(solution)/shard_map/all_gather | solution.py:272
  9.4 199.4 %all-gather.11.cloned.1.call-start = ((), (), s32[]{:S(2)}) async-start(), calls=%async_computation.16 | async-start | bytes 5013504 | tf_op jit(solution)/shard_map/all_gather | solution.py:273
  10.0 642.9 %reduce-scatter.48.cloned.1.call-start = ((), (), s32[]{:S(2)}) async-start(), calls=%async_computation.25 | async-start | bytes 417792
  83.8 125.1 %copy-start.96 = (bf16[3072]{0:T(1024)(128)(2,1)}, bf16[3072]{0:T(1024)(128)(2,1)S(1)}, u32[]{:S(2)}) copy-start(bf16[3072]{0:T(1024)(128)(2,1)S(1)} %get-tuple-element.596) | copy-start | bytes 18436
  83.8 125.1 %copy-start.97 = (bf16[768]{0:T(1024)(128)(2,1)}, bf16[768]{0:T(1024)(128)(2,1)S(1)}, u32[]{:S(2)}) copy-start(bf16[768]{0:T(1024)(128)(2,1)S(1)} %get-tuple-element.589) | copy-start | bytes 4612
  83.8 125.1 %copy-start.98 = (bf16[768]{0:T(1024)(128)(2,1)}, bf16[768]{0:T(1024)(128)(2,1)S(1)}, u32[]{:S(2)}) copy-start(bf16[768]{0:T(1024)(128)(2,1)S(1)} %get-tuple-element.594) | copy-start | bytes 4612
  83.8 125.1 %copy-start.105 = (bf16[768]{0:T(1024)(128)(2,1)}, bf16[768]{0:T(1024)(128)(2,1)S(1)}, u32[]{:S(2)}) copy-start(bf16[768]{0:T(1024)(128)(2,1)S(1)} %get-tuple-element.590) | copy-start | bytes 4612
  83.8 125.1 %copy-start.106 = (bf16[768]{0:T(1024)(128)(2,1)}, bf16[768]{0:T(1024)(128)(2,1)S(1)}, u32[]{:S(2)}) copy-start(bf16[768]{0:T(1024)(128)(2,1)S(1)} %get-tuple-element.591) | copy-start | bytes 4612
  83.8 125.1 %copy-start.107 = (bf16[768]{0:T(1024)(128)(2,1)}, bf16[768]{0:T(1024)(128)(2,1)S(1)}, u32[]{:S(2)}) copy-start(bf16[768]{0:T(1024)(128)(2,1)S(1)} %get-tuple-element.592) | copy-start | bytes 4612
  83.8 125.1 %copy-start.108 = (bf16[768]{0:T(1024)(128)(2,1)}, bf16[768]{0:T(1024)(128)(2,1)S(1)}, u32[]{:S(2)}) copy-start(bf16[768]{0:T(1024)(128)(2,1)S(1)} %get-tuple-element.593) | copy-start | bytes 4612
  83.8 125.1 %copy-start.109 = (bf16[768]{0:T(1024)(128)(2,1)}, bf16[768]{0:T(1024)(128)(2,1)S(1)}, u32[]{:S(2)}) copy-start(bf16[768]{0:T(1024)(128)(2,1)S(1)} %get-tuple-element.595) | copy-start | bytes 4612
  83.8 125.1 %copy-start.110 = (bf16[768]{0:T(1024)(128)(2,1)}, bf16[768]{0:T(1024)(128)(2,1)S(1)}, u32[]{:S(2)}) copy-start(bf16[768]{0:T(1024)(128)(2,1)S(1)} %get-tuple-element.597) | copy-start | bytes 4612
  85.7 123.2 %copy-start.143 = (pred[1,256]{1,0:T(4,128)(4,1)}, pred[1,256]{1,0:T(4,128)(4,1)S(1)}, u32[]{:S(2)}) copy-start(pred[1,256]{1,0:T(4,128)(4,1)S(1)} %get-tuple-element.674) | copy-start | bytes 772
  224.0 14.0 slice-start.14
  241.9 15.4 %copy-start.2 = (f32[256,768]{1,0:T(8,128)}, f32[256,768]{1,0:T(8,128)S(1)}, u32[]{:S(2)}) copy-start(f32[256,768]{1,0:T(8,128)S(1)} %get-tuple-element.390) | copy-start | bytes 2359300
  241.9 15.4 %copy-start.26 = (bf16[256,768]{1,0:T(8,128)(2,1)}, bf16[256,768]{1,0:T(8,128)(2,1)S(1)}, u32[]{:S(2)}) copy-start(bf16[256,768]{1,0:T(8,128)(2,1)S(1)} %get-tuple-element.391) | copy-start | bytes 1179652
  241.9 10.7 collective-permute-start
  244.2 13.1 copy-start.93
  244.9 19.1 %copy-start.84 = (f32[768]{0:T(1024)}, f32[768]{0:T(1024)S(1)}, u32[]{:S(2)}) copy-start(f32[768]{0:T(1024)S(1)} %convert_element_type.566) | copy-start | bytes 9220
  245.5 11.8 copy-start.125
  246.1 17.9 %copy-start.90 = (f32[768]{0:T(1024)}, f32[768]{0:T(1024)S(1)}, u32[]{:S(2)}) copy-start(f32[768]{0:T(1024)S(1)} %convert_element_type.567) | copy-start | bytes 9220
  263.1 12.0 slice-start.12
  263.7 197.1 %copy-start.13 = (f32[256,768]{1,0:T(8,128)}, f32[256,768]{1,0:T(8,128)S(1)}, u32[]{:S(2)}) copy-start(f32[256,768]{1,0:T(8,128)S(1)} %get-tuple-element.678) | copy-start | bytes 2359300
  263.7 11.4 copy-start.102
  275.2 15.1 %copy-start.52 = (bf16[512,768]{1,0:T(8,128)(2,1)S(1)}, bf16[512,768]{1,0:T(8,128)(2,1)}, u32[]{:S(2)}) copy-start(bf16[512,768]{1,0:T(8,128)(2,1)} %param.29) | copy-start | bytes 2359300
  277.4 12.9 collective-permute-start.1
  319.9 138.6 %copy-start.17 = (f32[256,768]{1,0:T(8,128)}, f32[256,768]{1,0:T(8,128)S(1)}, u32[]{:S(2)}) copy-start(f32[256,768]{1,0:T(8,128)S(1)} %get-tuple-element.383) | copy-start | bytes 2359300
  319.9 129.6 %collective-permute-start.2 = (bf16[256,768]{1,0:T(8,128)(2,1)S(1)}, bf16[256,768]{1,0:T(8,128)(2,1)S(1)}, u32[]{:S(2)}, u32[]{:S(2)}) collective-permute-start(bf16[256,768]{1,0:T(8,128)(2,1)S(1)} %convert_element_type.576), channel_id=1, source_target_pairs={{16,0},{17,1},{18,2},{19,3},{20,4},{21,5},{22,6},{23,7},{24,8},{25... | collective-permute-start | bytes 1179656 | tf_op jit(solution)/shard_map/ppermute | solution.py:17
  449.5 11.6 copy-start.45
  475.3 11.1 collective-permute-start.3
  487.4 58.0 %copy-start.3 = (f32[256,768]{1,0:T(8,128)S(1)}, f32[256,768]{1,0:T(8,128)}, u32[]{:S(2)}) copy-start(f32[256,768]{1,0:T(8,128)} %copy-done.2) | copy-start | bytes 2359300
  487.4 58.0 %copy-start.27 = (bf16[256,768]{1,0:T(8,128)(2,1)S(1)}, bf16[256,768]{1,0:T(8,128)(2,1)}, u32[]{:S(2)}) copy-start(bf16[256,768]{1,0:T(8,128)(2,1)} %copy-done.26) | copy-start | bytes 1179652
  487.4 58.0 %copy-start.89 = (f32[1,16,256]{2,1,0:T(8,128)S(1)}, f32[1,16,256]{2,1,0:T(8,128)}, u32[]{:S(2)}) copy-start(f32[1,16,256]{2,1,0:T(8,128)} %copy-done.88) | copy-start | bytes 49156
  489.6 13.5 slice-start.10
  541.9 112.2 %reduce-scatter.54.cloned.1.call-start = ((), (), s32[]{:S(2)}) async-start(), calls=%async_computation.28 | async-start | bytes 417792
  543.7 168.1 %reduce-scatter.56.cloned.1.call-start = ((), (), s32[]{:S(2)}) async-start(), calls=%async_computation.29 | async-start | bytes 417792
  545.3 225.0 %reduce-scatter.40.cloned.1.call-start = ((), (), s32[]{:S(2)}) async-start(), calls=%async_computation.21 | async-start | bytes 417792
  595.5 232.9 %reduce-scatter.42.cloned.1.call-start = ((), (), s32[]{:S(2)}) async-start(), calls=%async_computation.22 | async-start | bytes 417792
  597.3 289.6 %reduce-scatter.44.cloned.1.call-start = ((), (), s32[]{:S(2)}) async-start(), calls=%async_computation.23 | async-start | bytes 417792
  598.9 346.1 %reduce-scatter.50.cloned.1.call-start = ((), (), s32[]{:S(2)}) async-start(), calls=%async_computation.26 | async-start | bytes 417792
  600.7 402.7 %reduce-scatter.52.cloned.1.call-start = ((), (), s32[]{:S(2)}) async-start(), calls=%async_computation.27 | async-start | bytes 417792
  602.4 463.2 %reduce-scatter.46.cloned.1.call-start = ((), (), s32[]{:S(2)}) async-start(), calls=%async_computation.24 | async-start | bytes 1671168
  604.8 527.5 %reduce-scatter.34.cloned.1.call-start = ((), (), s32[]{:S(2)}) async-start(), calls=%async_computation.18 | async-start | bytes 2506752 | tf_op jit(solution)/shard_map/reduce_scatter | solution.py:348
  609.5 616.4 %reduce-scatter.32.cloned.1.call-start = ((), (), s32[]{:S(2)}) async-start(), calls=%async_computation.17 | async-start | bytes 7520256 | tf_op jit(solution)/shard_map/reduce_scatter | solution.py:347
  619.3 722.6 %reduce-scatter.36.cloned.1.call-start = ((), (), s32[]{:S(2)}) async-start(), calls=%async_computation.19 | async-start | bytes 10027008 | tf_op jit(solution)/shard_map/reduce_scatter | solution.py:349
  633.3 824.3 %reduce-scatter.38.cloned.1.call-start = ((), (), s32[]{:S(2)}) async-start(), calls=%async_computation.20 | async-start | bytes 10027008 | tf_op jit(solution)/shard_map/reduce_scatter | solution.py:350
  (105 other events, 413.0 us)
Sparse Core Ops, SparseCore 0:
  10.3 41.2 all-gather.6
  53.9 46.0 all-gather.4
  102.3 52.3 all-gather.8
  156.8 51.9 all-gather.10
  542.1 53.1 reduce-scatter.47
  599.0 54.6 reduce-scatter.53
  657.2 54.5 reduce-scatter.55
  715.7 54.6 reduce-scatter.39
  773.8 54.5 reduce-scatter.41
  832.2 54.5 reduce-scatter.43
  890.3 54.6 reduce-scatter.49
  948.8 54.5 reduce-scatter.51
  1007.1 58.4 reduce-scatter.45
  1070.2 62.0 reduce-scatter.33
  1136.7 89.0 reduce-scatter.31
  1230.9 110.8 reduce-scatter.35
  1346.4 111.1 reduce-scatter.37
where the time goes:
time: 1470 us; the launch traced here: 1460 us
  waiting for transfers between devices  1060 us (72%)
  matrix products  124 us (8%)
  local copies, waits for them, and re-layouts  109 us (7%)
  other arithmetic  77 us (5%)
  blocking collectives  63.6 us (4%)
  starting transfers between devices  17.4 us (1%)
  between operations  16.8 us (1%)
    unnamed x26, waiting for transfers between devices  405 us
    ppermute x4, waiting for transfers between devices, passed_along(): return lax.ppermute(block, axis, route)  138 us
    reduce_scatter x1, waiting for transfers between devices, shards(): lax.psum_scatter(mlp_totals[0][None], 'dp', scatter_dimension=1, tiled=True)  116 us
    reduce_scatter x1, waiting for transfers between devices, shards(): lax.psum_scatter(mlp_totals[1][None], 'dp', scatter_dimension=1, tiled=True)  116 us
    reduce_scatter x1, waiting for transfers between devices, shards(): lax.psum_scatter(attn_totals[0][None], 'dp', scatter_dimension=1, tiled=T...  93.5 us
    reduce_scatter x1, waiting for transfers between devices, shards(): lax.psum_scatter(attn_totals[1][None], 'dp', scatter_dimension=1, tiled=T...  65.2 us
    squeeze x1, blocking collectives, shards(): params = tuple((piece[0] for piece in gathered))  63.6 us
    all_gather x1, waiting for transfers between devices, shards(): lax.all_gather(up_weight, 'dp', axis=1, tiled=True)  54.7 us
  transfers between devices with their start and end apart: 21, of which 18 were waited for; matrix products, arithmetic and copies ran while one was open for 9% of the time, Pallas kernels for 0%

commit v1 on v0

v1 whole, which is shorter than its diff:
```python
import functools

import jax
import jax.numpy as jnp
from jax import lax
from jax.experimental import pallas as pl
from jax.experimental.pallas import tpu as pltpu
from jax.sharding import PartitionSpec as P

H = 16
GRID = 16
LEAD = 16
RING = 8
VEC_ROWS = 16

f32 = jnp.float32
bf16 = jnp.bfloat16
eps_norm = 1e-05


def layer_norm(values_in, gain_vec, offset_vec):
    average = jnp.mean(values_in, axis=-1, keepdims=True)
    centred = values_in - average
    variance = jnp.mean(centred * centred, axis=-1, keepdims=True)
    return centred * lax.rsqrt(variance + eps_norm) * gain_vec + offset_vec


def gelu_exact(values_in):
    return jax.nn.gelu(values_in, approximate=False)


def product(first_mat, second_mat):
    return jnp.dot(first_mat, second_mat, preferred_element_type=f32)


def outer_sum(first_mat, second_mat):
    return lax.dot_general(
        first_mat, second_mat, (((0,), (0,)), ((), ())), preferred_element_type=f32
    )


def back_product(first_mat, second_mat):
    return lax.dot_general(
        first_mat, second_mat, (((1,), (1,)), ((), ())), preferred_element_type=f32
    )


def chip_at(place):
    if isinstance(place, int):
        return 2 * place if place < 4 else 2 * (7 - place) + 1
    return jnp.where(place < 4, 2 * place, 2 * (7 - place) + 1)


def place_of(chip):
    if isinstance(chip, int):
        return chip // 2 if chip % 2 == 0 else 7 - chip // 2
    return jnp.where(chip % 2 == 0, chip // 2, 7 - chip // 2)


def ring_route(step):
    return [
        (2 * chip_at(place) + core, 2 * chip_at((place + step) % RING) + core)
        for place in range(RING)
        for core in range(2)
    ]


CORE_ROUTE = [(index, index ^ 1) for index in range(2 * RING)]


def onward(block):
    return lax.ppermute(block, "dp", ring_route(1))


def backward(block):
    return lax.ppermute(block, "dp", ring_route(-1))


def across(block):
    return lax.ppermute(block, "dp", CORE_ROUTE)


def ring_gather(shard):
    half = shard.shape[0] // 2
    here = {0: shard}
    up, down = shard, shard
    for step in range(1, RING // 2):
        up, down = onward(up), backward(down)
        here[RING - step], here[step] = up, down
    far = (onward(up[:half]), backward(down[half:]))
    blocks = []
    for place in range(RING):
        if place == RING // 2:
            blocks += [far[0], far[1], across(far[0]), across(far[1])]
        else:
            blocks += [here[place], across(here[place])]
    return blocks


def assemble(blocks):
    rows, width = blocks[0].shape
    half = rows // 2
    count = len(blocks)

    def kernel(*refs):
        blocks_in, out, sems = refs[:count], refs[count], refs[count + 1]
        me = lax.axis_index("dp")
        core, place = lax.rem(me, 2), place_of(lax.div(me, 2))
        copies = []
        at = 0
        for step in range(RING):
            chip = chip_at(lax.rem(place + step, RING))
            parts = ((0, half), (half, half)) if step == RING // 2 else ((0, rows),)
            for owner in (2 * chip + core, 2 * chip + 1 - core):
                for start, size in parts:
                    copies.append(
                        pltpu.make_async_copy(
                            blocks_in[at], out.at[owner, pl.ds(start, size)], sems.at[at]
                        )
                    )
                    at += 1
        for copy in copies:
            copy.start()
        for copy in copies:
            copy.wait()

    return pl.pallas_call(
        kernel,
        out_shape=jax.ShapeDtypeStruct((2 * RING, rows, width), blocks[0].dtype),
        in_specs=[pl.BlockSpec(memory_space=pl.ANY)] * count,
        out_specs=pl.BlockSpec(memory_space=pl.ANY),
        scratch_shapes=[pltpu.SemaphoreType.DMA((count,))],
        name="assemble",
    )(*blocks)


def dispatch(whole):
    count, rows, width = whole.shape

    def kernel(whole_ref, own_ref, peer_ref, sems):
        me = lax.axis_index("dp")
        core, place = lax.rem(me, 2), place_of(lax.div(me, 2))
        copies = []
        for step in range(RING):
            chip = chip_at(lax.rem(place + step, RING))
            copies.append(
                pltpu.make_async_copy(whole_ref.at[2 * chip + core], own_ref.at[step], sems.at[2 * step])
            )
            copies.append(
                pltpu.make_async_copy(
                    whole_ref.at[2 * chip + 1 - core], peer_ref.at[step], sems.at[2 * step + 1]
                )
            )
        for copy in copies:
            copy.start()
        for copy in copies:
            copy.wait()

    return pl.pallas_call(
        kernel,
        out_shape=[jax.ShapeDtypeStruct((RING, rows, width), whole.dtype)] * 2,
        in_specs=[pl.BlockSpec(memory_space=pl.ANY)],
        out_specs=[pl.BlockSpec(memory_space=pl.ANY)] * 2,
        scratch_shapes=[pltpu.SemaphoreType.DMA((2 * RING,))],
        name="dispatch",
    )(whole)


def ring_scatter(own, peer):
    rows = own.shape[1]
    half = rows // 2
    arrived = across(peer)

    def local(step, start=0, size=rows):
        return own[step, start : start + size].astype(f32) + arrived[step, start : start + size].astype(f32)

    far = RING // 2
    up = onward(local(far, 0, half).astype(bf16))
    down = backward(local(far, half, half).astype(bf16))
    joint_up = jnp.concatenate([local(far - 1, 0, half) + up.astype(f32), local(far - 1, half, half)], 0)
    joint_down = jnp.concatenate([local(far + 1, 0, half), local(far + 1, half, half) + down.astype(f32)], 0)
    up, down = onward(joint_up.astype(bf16)), backward(joint_down.astype(bf16))
    for step in range(far - 2, 0, -1):
        up = onward((local(step) + up.astype(f32)).astype(bf16))
        down = backward((local(RING - step) + down.astype(f32)).astype(bf16))
    return local(0) + up.astype(f32) + down.astype(f32)


def head_split(matrix, valid_mask):
    images, slots = valid_mask.shape
    return matrix.reshape(images, slots, H, matrix.shape[1] // H)


def attn_forward(layer_input, attn_w, vecs, valid_mask):
    width = layer_input.shape[1]
    images, slots = valid_mask.shape
    rows = width // LEAD
    w_of = lambda c: attn_w[:, c * rows : (c + 1) * rows].reshape(width, width)
    normed = layer_norm(layer_input, vecs["gain_one"], vecs["shift_one"]).astype(bf16)
    queries = (product(normed, w_of(0)) + vecs["q_bias"]).astype(bf16)
    key_rows = product(normed, w_of(1)).astype(bf16)
    values = (product(normed, w_of(2)) + vecs["v_bias"]).astype(bf16)
    scale = (width // H) ** (-0.5)
    q4, k4, v4 = (head_split(a, valid_mask) for a in (queries, key_rows, values))
    scores = jnp.einsum("iqhd,ikhd->ihqk", q4, k4, preferred_element_type=f32) * scale
    scores = jnp.where(valid_mask[:, None, None, :], scores, -1e30)
    exponent = jnp.exp(scores - jnp.max(scores, axis=-1, keepdims=True))
    probs = (exponent / jnp.sum(exponent, axis=-1, keepdims=True)).astype(bf16)
    attended = jnp.einsum("ihqk,ikhd->iqhd", probs, v4, preferred_element_type=f32)
    attended = attended.reshape(images * slots, -1).astype(bf16)
    middle = layer_input + (product(attended, w_of(3)) + vecs["out_bias"])
    second = layer_norm(middle, vecs["gain_two"], vecs["shift_two"]).astype(bf16)
    return middle, second, (normed, queries, key_rows, values, probs, attended)


def mlp_forward(middle, second, up_w, down_w, vecs):
    width = middle.shape[1]
    rows = width // LEAD
    chunks = up_w.shape[1] // rows
    up = jnp.concatenate([up_w[:, c * rows : (c + 1) * rows].reshape(width, width) for c in range(chunks)], 1)
    hidden_pre = product(second, up) + vecs["up_bias"]
    activated = gelu_exact(hidden_pre).astype(bf16)
    result = middle + (product(activated, down_w.reshape(-1, width)) + vecs["down_bias"])
    return result.astype(bf16), activated, hidden_pre


def mlp_backward(upstream, middle, hidden_pre, up_w, down_w, vecs):
    width = middle.shape[1]
    rows = width // LEAD
    chunks = up_w.shape[1] // rows
    up = jnp.concatenate([up_w[:, c * rows : (c + 1) * rows].reshape(width, width) for c in range(chunks)], 1)
    grad_act = back_product(upstream, down_w.reshape(-1, width))
    grad_pre = jax.vjp(gelu_exact, hidden_pre)[1](grad_act)[0].astype(bf16)
    grad_second = back_product(grad_pre, up)
    grad_mid, grad_gain, grad_offset = jax.vjp(layer_norm, middle, vecs["gain_two"], vecs["shift_two"])[1](
        grad_second
    )
    sums = {
        "down_bias": jnp.sum(upstream.astype(f32), axis=0),
        "up_bias": jnp.sum(grad_pre.astype(f32), axis=0),
        "gain_two": grad_gain,
        "shift_two": grad_offset,
    }
    return upstream.astype(f32) + grad_mid, grad_pre, sums


def attn_backward(grad_middle, layer_input, saved, attn_w, vecs, valid_mask):
    normed, queries, key_rows, values, probs, attended = saved
    width = layer_input.shape[1]
    images, slots = valid_mask.shape
    rows = width // LEAD
    w_of = lambda c: attn_w[:, c * rows : (c + 1) * rows].reshape(width, width)
    scale = (width // H) ** (-0.5)
    grad_branch = grad_middle.astype(bf16)
    grad_attended = back_product(grad_branch, w_of(3)).astype(bf16)
    q4, k4, v4, g4 = (head_split(a, valid_mask) for a in (queries, key_rows, values, grad_attended))
    grad_probs = jnp.einsum("iqhd,ikhd->ihqk", g4, v4, preferred_element_type=f32)
    grad_value = jnp.einsum("ihqk,iqhd->ikhd", probs, g4, preferred_element_type=f32)
    soft = probs.astype(f32)
    terms = jnp.sum(soft * grad_probs, axis=-1, keepdims=True)
    grad_scores = (soft * (grad_probs - terms)).astype(bf16)
    grad_query = jnp.einsum("ihqk,ikhd->iqhd", grad_scores, k4, preferred_element_type=f32) * scale
    grad_key = jnp.einsum("ihqk,iqhd->ikhd", grad_scores, q4, preferred_element_type=f32) * scale
    parts = [a.reshape(images * slots, -1).astype(bf16) for a in (grad_query, grad_key, grad_value)]
    grad_normed = sum(back_product(part, w_of(c)) for c, part in enumerate(parts))
    grad_in, grad_gain, grad_offset = jax.vjp(layer_norm, layer_input, vecs["gain_one"], vecs["shift_one"])[1](
        grad_normed
    )
    sums = {
        "out_bias": jnp.sum(grad_branch.astype(f32), axis=0),
        "q_bias": jnp.sum(parts[0].astype(f32), axis=0),
        "v_bias": jnp.sum(parts[2].astype(f32), axis=0),
        "gain_one": grad_gain,
        "shift_one": grad_offset,
    }
    return grad_middle + grad_in, grad_branch, parts, sums


VECS = ("q_bias", "v_bias", "out_bias", "down_bias", "gain_one", "shift_one", "gain_two", "shift_two", "up_bias")


def by_columns(weight, width):
    rows, columns = weight.shape
    return jnp.concatenate([weight[:, at : at + width] for at in range(0, columns, width)], 0)


def solution(mesh):
    dp_size = mesh.shape["dp"]
    ringed = dp_size == 2 * RING

    def gather_weights(qkv, out, up, down, vectors):
        width = out.shape[1]
        if ringed:
            vec_row = jnp.concatenate([vectors[name] for name in VECS])
            vec_count = vec_row.shape[0]
            vec_block = jnp.zeros((VEC_ROWS, width), bf16).at[0, :vec_count].set(vec_row)
            first = assemble(ring_gather(jnp.concatenate([by_columns(qkv, width), out, vec_block], 0)))
            up_w = assemble(ring_gather(by_columns(up, width)))
            down_w = assemble(ring_gather(down))
            vec_rows = first[:, first.shape[1] - VEC_ROWS, :vec_count]
            vecs, at = {}, 0
            for name in VECS:
                size = vectors[name].shape[0]
                vecs[name] = vec_rows[:, at : at + size].reshape(1, -1).astype(f32)
                at += size
            return first, up_w, down_w, vecs
        gathered = [lax.all_gather(w, "dp", axis=0, tiled=True) for w in (qkv, out, up, down)]
        blocked = [w.reshape(LEAD, -1, w.shape[1]) for w in gathered]
        fold = lambda w: w.reshape(LEAD, w.shape[1], -1, width).transpose(0, 2, 1, 3).reshape(LEAD, -1, width)
        first = jnp.concatenate([fold(blocked[0]), blocked[1], jnp.zeros((LEAD, VEC_ROWS, width), bf16)], 1)
        vecs = {
            name: lax.all_gather(vectors[name], "dp", axis=0, tiled=True).reshape(1, -1).astype(f32)
            for name in VECS
        }
        return first, fold(blocked[2]), blocked[3], vecs

    def scatter_gradients(grad_down, grad_up, grad_first, sums):
        width = grad_down.shape[2]
        rows = width // LEAD
        if ringed:
            row = jnp.concatenate([sums[name].reshape(LEAD, -1) for name in VECS], 1).astype(bf16)
            vec_count = row.shape[1]
            vec_block = jnp.zeros((LEAD, VEC_ROWS, width), bf16).at[:, 0, :vec_count].set(row)
            down = ring_scatter(*dispatch(grad_down))
            up = ring_scatter(*dispatch(grad_up))
            first = ring_scatter(*dispatch(jnp.concatenate([grad_first, vec_block], 1)))
            vec_row, at, vecs = first[4 * rows], 0, {}
            for name in VECS:
                size = sums[name].size // dp_size
                vecs[name] = vec_row[at : at + size]
                at += size
            unfold = lambda block: jnp.concatenate(
                [block[at : at + rows] for at in range(0, block.shape[0], rows)], 1
            )
            return unfold(first[: 3 * rows]), first[3 * rows : 4 * rows], unfold(up), down, vecs
        scatter = lambda a: lax.psum_scatter(a, "dp", scatter_dimension=0, tiled=True)
        unfold = lambda w: w.reshape(LEAD, -1, rows, width).transpose(0, 2, 1, 3).reshape(LEAD * rows, -1)
        vecs = {name: scatter(sums[name].reshape(-1)) for name in VECS}
        return (
            scatter(unfold(grad_first[:, : 3 * rows]).astype(f32)),
            scatter(grad_first[:, 3 * rows :].reshape(width, width).astype(f32)),
            scatter(unfold(grad_up).astype(f32)),
            scatter(grad_down.reshape(-1, width).astype(f32)),
            vecs,
        )

    def shards(
        tokens, cotangent, heights, widths, qkv_weight, out_weight, up_weight, down_weight,
        q_bias, v_bias, out_bias, up_bias, down_bias, gain_one, shift_one, gain_two, shift_two,
    ):
        leading = lax.axis_index("section") == 0
        vectors = dict(
            q_bias=q_bias[0], v_bias=v_bias[0], out_bias=out_bias[0], up_bias=up_bias[0], down_bias=down_bias[0],
            gain_one=gain_one[0], shift_one=shift_one[0], gain_two=gain_two[0], shift_two=shift_two[0],
        )
        attn_w, up_w, down_w, vecs = gather_weights(
            qkv_weight[0], out_weight[0], up_weight[0], down_weight[0], vectors
        )
        position = jnp.arange(GRID * GRID, dtype=jnp.int32)
        valid = ((position // GRID)[None, :] < heights[:, None]) & (
            (position % GRID)[None, :] < widths[:, None]
        )

        middle, second, _ = attn_forward(tokens.astype(f32), attn_w, vecs, valid)
        sent, _, _ = mlp_forward(middle, second, up_w, down_w, vecs)
        received = lax.ppermute(sent, "section", [(0, 1)])
        layer_input = jnp.where(leading, tokens, received).astype(f32)
        middle, second, saved = attn_forward(layer_input, attn_w, vecs, valid)
        result, activated, hidden_pre = mlp_forward(middle, second, up_w, down_w, vecs)

        grad_middle, _, _ = mlp_backward(cotangent, middle, hidden_pre, up_w, down_w, vecs)
        grad_input, _, _, _ = attn_backward(grad_middle, layer_input, saved, attn_w, vecs, valid)
        arriving = lax.ppermute(grad_input.astype(bf16), "section", [(1, 0)])
        upstream = jnp.where(leading, arriving, cotangent)
        grad_down = outer_sum(activated, upstream).astype(bf16)
        grad_middle, grad_pre, sums = mlp_backward(upstream, middle, hidden_pre, up_w, down_w, vecs)
        grad_up = outer_sum(second, grad_pre).astype(bf16)
        grad_input, grad_branch, parts, more = attn_backward(
            grad_middle, layer_input, saved, attn_w, vecs, valid
        )
        normed, attended = saved[0], saved[5]
        first = [outer_sum(normed, part) for part in parts] + [outer_sum(attended, grad_branch)]
        width = tokens.shape[1]
        grad_first = jnp.concatenate([g.reshape(LEAD, -1, width) for g in first], 1).astype(bf16)
        chunks = grad_up.shape[1] // width
        grad_up = jnp.concatenate(
            [grad_up[:, c * width : (c + 1) * width].reshape(LEAD, -1, width) for c in range(chunks)], 1
        )
        g_qkv, g_out, g_up, g_down, g_vecs = scatter_gradients(
            grad_down.reshape(LEAD, -1, width), grad_up, grad_first, {**sums, **more}
        )
        return (
            result[None], grad_input[None], g_qkv[None], g_out[None], g_up[None], g_down[None],
            *(
                g_vecs[name][None]
                for name in (
                    "q_bias", "v_bias", "out_bias", "up_bias", "down_bias",
                    "gain_one", "shift_one", "gain_two", "shift_two",
                )
            ),
        )

    rows = P("dp", None)
    three, two = P("section", "dp", None), P("section", "dp")
    return jax.shard_map(
        shards,
        mesh=mesh,
        in_specs=(rows, rows, P("dp"), P("dp")) + (three,) * 4 + (two,) * 9,
        out_specs=(three,) * 6 + (two,) * 9,
        check_vma=False,
    )
```

time: 1470 us -> 1360 us (0.925)
  waiting for transfers between devices: 1060 us -> 112 us
  Pallas kernels: 0 us -> 889 us
  blocking collectives: 63.6 us -> 0 us
  starting transfers between devices: 17.4 us -> 73.2 us
  other arithmetic: 77 us -> 39.1 us
  matrix products: 124 us -> 158 us
  local copies, waits for them, and re-layouts: 109 us -> 75.7 us
    pallas_call x0 -> x6, Pallas kernels: none -> 889 us  [the longest x3 445 us: assemble(): pl.pallas_call(kernel, out_shape=jax.ShapeDtypeStruct((2 * RING, rows, wi...]
    unnamed x26 -> x0, waiting for transfers between devices: 405 us -> none
    reduce_scatter x4 -> x0, waiting for transfers between devices: 390 us -> none  [the longest x1 116 us: shards(): lax.psum_scatter(mlp_totals[0][None], 'dp', scatter_dimension=1, tiled=True)]
    all_gather x4 -> x0, waiting for transfers between devices: 122 us -> none  [the longest x1 54.7 us: shards(): lax.all_gather(up_weight, 'dp', axis=1, tiled=True)]
    squeeze x1 -> x0, blocking collectives: 63.6 us -> none  [shards(): params = tuple((piece[0] for piece in gathered))]
    ppermute x4 -> x80, starting transfers between devices: 16.4 us -> 73.2 us  [the longest x24 31.8 us: backward(): return lax.ppermute(block, 'dp', ring_route(-1))]
    dot_general x21, matrix products: 55.8 us -> 90.8 us  [the longest x11 65.6 us: product(): return jnp.dot(first_mat, second_mat, preferred_element_type=f32)]
    another operation x30 -> x1, local copies, waits for them, and re-layouts: 32.1 us -> 0.01 us
  transfers between devices with their start and end apart: 21 -> 80, of which waited for: 18 -> 32; matrix products, arithmetic and copies ran while one was open for 9% -> 5% of each run, Pallas kernels for 0% -> 44%
where the time goes in v1:
time: 1360 us; the launch traced here: 1350 us
  Pallas kernels  889 us (65%)
  matrix products  158 us (12%)
  waiting for transfers between devices  112 us (8%)
  local copies, waits for them, and re-layouts  75.7 us (6%)
  starting transfers between devices  73.2 us (5%)
  other arithmetic  39.1 us (3%)
    pallas_call x3, Pallas kernels, assemble(): pl.pallas_call(kernel, out_shape=jax.ShapeDtypeStruct((2 * RING, rows, wi...  445 us
    pallas_call x3, Pallas kernels, dispatch(): pl.pallas_call(kernel, out_shape=[jax.ShapeDtypeStruct((RING, rows, width...  444 us
    dot_general x11, matrix products, product(): return jnp.dot(first_mat, second_mat, preferred_element_type=f32)  65.6 us
    ppermute x24, waiting for transfers between devices, onward(): return lax.ppermute(block, 'dp', ring_route(1))  56.3 us
    dot_general x11, matrix products, back_product(): lax.dot_general(first_mat, second_mat, (((1,), (1,)), ((), ())), preferre...  34.2 us
    ppermute x24, starting transfers between devices, backward(): return lax.ppermute(block, 'dp', ring_route(-1))  31.8 us
    ppermute x24, starting transfers between devices, onward(): return lax.ppermute(block, 'dp', ring_route(1))  29.6 us
  transfers between devices with their start and end apart: 80, of which 32 were waited for; matrix products, arithmetic and copies ran while one was open for 5% of the time, Pallas kernels for 44%

profile of v1, /device:TPU:0, one launch (start us, length us, event | category | flops | bytes accessed | tf_op | source)
XLA Modules:
  0.0 1350.0 jit_solution(4100169904472361610)
XLA Ops:
  1.8 3.1 collective-permute-start.24
  9.6 3.2 collective-permute-done.24.refs_16_
  14.4 5.4 concatenate.85
  24.4 6.0 collective-permute-done.7.refs_16_
  40.1 2.9 collective-permute-done.42.refs_14_
  78.6 3.5 collective-permute-done.10.refs_8_
  86.0 144.2 %assemble.4 = bf16[16,192,768]{2,1,0:T(8,128)(2,1)} custom-call(bf16[192,768]{1,0:T(8,128)(2,1)} %copy-done.47, bf16[192,768]{1,0:T(8,128)(2,1)} %collective-permute-done.17.refs_1_, bf16[192,768]{1,0:T(8,128)(2,1)} %collective-permute-done.18.refs_2_, bf16[192,768]{1,0:T(8,128)(2,1)} %copy-done.84, bf16[192,768]{1,0:T(8,128)(2,1)} %copy-done.83, ...), custom_call_target="tpu_custom_call" | custom-call | tf_op jit(solution)/shard_map/assemble/pallas_call | solution.py:127
  231.8 4.5 fusion.228
  236.3 144.2 %assemble.5 = bf16[16,192,768]{2,1,0:T(8,128)(2,1)} custom-call(bf16[192,768]{1,0:T(8,128)(2,1)} %bitcast.390, bf16[192,768]{1,0:T(8,128)(2,1)} %copy-done.77, bf16[192,768]{1,0:T(8,128)(2,1)} %copy-done.76, bf16[192,768]{1,0:T(8,128)(2,1)} %copy-done.80, bf16[192,768]{1,0:T(8,128)(2,1)} %copy-done.79, bf16[192,768]{1,0:T(8,128)(2,1)} %copy-done.86, ...), custom_call_target="tpu_custom_call" | custom-call | tf_op jit(solution)/shard_map/assemble/pallas_call | solution.py:127
  382.2 156.1 %assemble.3 = bf16[16,208,768]{2,1,0:T(8,128)(2,1)} custom-call(bf16[208,768]{1,0:T(8,128)(2,1)} %copy-done.63, bf16[208,768]{1,0:T(8,128)(2,1)} %copy-done.66, bf16[208,768]{1,0:T(8,128)(2,1)} %copy-done.65, bf16[208,768]{1,0:T(8,128)(2,1)} %copy-done.70, bf16[208,768]{1,0:T(8,128)(2,1)} %copy-done.68, bf16[208,768]{1,0:T(8,128)(2,1)} %copy-done.72, ...), custom_call_target="tpu_custom_call" | custom-call | tf_op jit(solution)/shard_map/assemble/pallas_call | solution.py:127
  539.3 4.2 fusion.226
  548.1 3.1 add_convert_fusion.8
  553.7 3.1 convolution_convert_fusion.9
  559.2 8.2 fusion.232
  567.5 4.2 fusion.70
  578.3 22.3 %add_convert_fusion.6 = bf16[512,768]{1,0:T(8,128)(2,1)} fusion(f32[512,768]{1,0:T(8,128)} %copy-done.28, bf16[3072,768]{1,0:T(8,128)(2,1)} %bitcast.329, f32[3072]{0:T(1024)S(1)} %reshape.750, f32[768]{0:T(1024)S(1)} %reshape.751, f32[768]{0:T(1024)S(1)} %reshape.749, f32[768]{0:T(1024)S(1)} %reshape.748, f32[512]{0:T(512)S(1)} %add_rsqrt_fusion, ...), kind=kOutput, calls=%fused_computation.126 | convolution fusion | flops 4957667328 | bytes 11822080 | tf_op jit(solution)/shard_map/dot_general | solution.py:33
  600.6 4.3 collective-permute-start.51
  604.8 16.5 %collective-permute-done.51 = bf16[512,768]{1,0:T(8,128)(2,1)} collective-permute-done((bf16[512,768]{1,0:T(8,128)(2,1)}, bf16[512,768]{1,0:T(8,128)(2,1)}, u32[]{:S(2)}, u32[]{:S(2)}) %collective-permute-start.51) | collective-permute-done | bytes 786464 | tf_op jit(solution)/shard_map/ppermute | solution.py:366
  632.1 5.5 fusion.242
  637.6 4.4 divide_convert_fusion
  647.7 21.1 %multiply_convert_fusion = (bf16[512,3072]{1,0:T(8,128)(2,1)}, f32[512,3072]{1,0:T(8,128)}, f32[512,3072]{1,0:T(8,128)}) fusion(f32[3072]{0:T(1024)S(1)} %reshape.750, bf16[768,768]{1,0:T(8,128)(2,1)S(1)} %bitcast.361, bf16[768,768]{1,0:T(8,128)(2,1)S(1)} %bitcast.365, bf16[768,768]{1,0:T(8,128)(2,1)S(1)} %bitcast.369, bf16[768,768]{1,0:T(8,128)(2,1)S(1)} %bitcast.357, ...), kind=kOutput, calls=%fused_computation.34 | convolution fusion | flops 2540568576 | bytes 22042624 | tf_op jit(solution)/shard_map/dot_general | solution.py:33
  668.9 14.0 %multiply_reduce_fusion.2 = (f32[512]{0:T(512)S(1)}, f32[512,768]{1,0:T(8,128)}) fusion(f32[512,768]{1,0:T(8,128)S(1)} %get-tuple-element.148, f32[512]{0:T(512)S(1)} %broadcast_multiply_fusion, f32[768]{0:T(1024)S(1)} %reshape.748, bf16[768,768]{1,0:T(8,128)(2,1)} %bitcast.360, bf16[768,768]{1,0:T(8,128)(2,1)} %bitcast.364, ...), kind=kOutput, calls=%fused_computation.120 | convolution fusion | flops 4875877888 | bytes 25971712 | tf_op jit(solution)/shard_map/dot_general | solution.py:43
  690.2 2.9 reshape.736
  693.1 3.9 fusion.68
  697.0 2.8 fusion.2
  713.9 20.6 %collective-permute-done.52 = bf16[512,768]{1,0:T(8,128)(2,1)S(1)} collective-permute-done((bf16[512,768]{1,0:T(8,128)(2,1)S(1)}, bf16[512,768]{1,0:T(8,128)(2,1)S(1)}, u32[]{:S(2)}, u32[]{:S(2)}) %collective-permute-start.52) | collective-permute-done | bytes 786464 | tf_op jit(solution)/shard_map/ppermute | solution.py:373
  734.8 8.1 fusion.219
  742.9 4.9 convolution_convert_fusion.1
  747.8 2.9 multiply_reduce_fusion
  757.8 2.9 reshape.737
  760.7 4.8 fusion.253
  765.5 2.8 fusion.4
  774.9 4.3 convolution_convert_fusion
  779.2 144.2 %dispatch.5 = (bf16[8,192,768]{2,1,0:T(8,128)(2,1)}, bf16[8,192,768]{2,1,0:T(8,128)(2,1)}) custom-call(bf16[16,192,768]{2,1,0:T(8,128)(2,1)} %bitcast.335), custom_call_target="tpu_custom_call" | custom-call | tf_op jit(solution)/shard_map/dispatch/pallas_call | solution.py:159
  928.7 144.2 %dispatch.4 = (bf16[8,192,768]{2,1,0:T(8,128)(2,1)}, bf16[8,192,768]{2,1,0:T(8,128)(2,1)}) custom-call(bf16[16,192,768]{2,1,0:T(8,128)(2,1)} %pad_maximum_fusion.1.whole_ref), custom_call_target="tpu_custom_call" | custom-call | tf_op jit(solution)/shard_map/dispatch/pallas_call | solution.py:159
  1086.6 3.3 fusion.64
  1092.7 3.1 fusion.62
  1098.4 156.1 %dispatch.3 = (bf16[8,208,768]{2,1,0:T(8,128)(2,1)}, bf16[8,208,768]{2,1,0:T(8,128)(2,1)}) custom-call(bf16[16,208,768]{2,1,0:T(8,128)(2,1)} %pad_dynamic-update-slice_fusion.whole_ref), custom_call_target="tpu_custom_call" | custom-call | tf_op jit(solution)/shard_map/dispatch/pallas_call | solution.py:159
  1254.7 7.1 fusion.71
  1278.1 6.0 collective-permute-done.54
  1286.4 4.9 collective-permute-done.64
  1295.1 6.7 collective-permute-done.55
  1303.5 4.6 collective-permute-done.65
  1310.9 3.4 collective-permute-done.74
  1318.2 3.0 collective-permute-done.56
  1328.3 4.2 collective-permute-done.60
  1335.7 3.2 collective-permute-done.70
  1340.0 3.6 collective-permute-done.79
  (527 shorter events, 204.9 us)
Async XLA Ops:
  1.8 11.0 collective-permute-start.24
  4.9 14.9 %collective-permute-start.18 = (bf16[192,768]{1,0:T(8,128)(2,1)S(1)}, bf16[192,768]{1,0:T(8,128)(2,1)}, u32[]{:S(2)}, u32[]{:S(2)}) collective-permute-start(bf16[192,768]{1,0:T(8,128)(2,1)S(1)} %pad_maximum_fusion.4.refs_0_), channel_id=1, source_target_pairs={{0,2},{1,3},{4,0},{5,1},{8,4},{9,5},{12,8},{13,9},{14,12},{15,13},... | collective-permute-start | bytes 884744 | tf_op jit(solution)/shard_map/ppermute | solution.py:76
  4.9 17.1 %collective-permute-start.17 = (bf16[192,768]{1,0:T(8,128)(2,1)S(1)}, bf16[192,768]{1,0:T(8,128)(2,1)}, u32[]{:S(2)}, u32[]{:S(2)}) collective-permute-start(bf16[192,768]{1,0:T(8,128)(2,1)S(1)} %pad_maximum_fusion.4.refs_0_), channel_id=1, source_target_pairs={{0,1},{1,0},{2,3},{3,2},{4,5},{5,4},{6,7},{7,6},{8,9},{9,8},{10,11... | collective-permute-start | bytes 884744 | tf_op jit(solution)/shard_map/ppermute | solution.py:80
  4.9 17.1 %collective-permute-start.41 = (bf16[192,768]{1,0:T(8,128)(2,1)}, bf16[192,768]{1,0:T(8,128)(2,1)S(1)}, u32[]{:S(2)}, u32[]{:S(2)}) collective-permute-start(bf16[192,768]{1,0:T(8,128)(2,1)} %bitcast.387), channel_id=1, source_target_pairs={{0,4},{1,5},{4,8},{5,9},{8,12},{9,13},{12,14},{13,15},{14,10},{15,... | collective-permute-start | bytes 884744 | tf_op jit(solution)/shard_map/ppermute | solution.py:72
  6.9 15.4 %collective-permute-start.35 = (bf16[192,768]{1,0:T(8,128)(2,1)}, bf16[192,768]{1,0:T(8,128)(2,1)S(1)}, u32[]{:S(2)}, u32[]{:S(2)}) collective-permute-start(bf16[192,768]{1,0:T(8,128)(2,1)} %bitcast.388), channel_id=1, source_target_pairs={{0,2},{1,3},{4,0},{5,1},{8,4},{9,5},{12,8},{13,9},{14,12},{15,13},... | collective-permute-start | bytes 884744 | tf_op jit(solution)/shard_map/ppermute | solution.py:76
  12.8 11.3 collective-permute-start.34
  19.8 10.5 collective-permute-start.7
  22.0 10.4 collective-permute-start.1
  22.0 10.4 collective-permute-start
  22.3 14.3 %collective-permute-start.25 = (bf16[192,768]{1,0:T(8,128)(2,1)}, bf16[192,768]{1,0:T(8,128)(2,1)S(1)}, u32[]{:S(2)}, u32[]{:S(2)}) collective-permute-start(bf16[192,768]{1,0:T(8,128)(2,1)} %collective-permute-done.24.refs_16_), channel_id=1, source_target_pairs={{0,4},{1,5},{4,8},{5,9},{8,12},{9,13},{12,14},{13,15},{14,10},{15,... | collective-permute-start | bytes 884744 | tf_op jit(solution)/shard_map/ppermute | solution.py:72
  24.1 14.5 %collective-permute-start.20 = (bf16[192,768]{1,0:T(8,128)(2,1)}, bf16[192,768]{1,0:T(8,128)(2,1)S(1)}, u32[]{:S(2)}, u32[]{:S(2)}) collective-permute-start(bf16[192,768]{1,0:T(8,128)(2,1)} %collective-permute-done.18.refs_2_), channel_id=1, source_target_pairs={{0,2},{1,3},{4,0},{5,1},{8,4},{9,5},{12,8},{13,9},{14,12},{15,13},... | collective-permute-start | bytes 884744 | tf_op jit(solution)/shard_map/ppermute | solution.py:76
  32.4 10.6 collective-permute-start.42
  39.1 10.7 collective-permute-start.8
  59.0 10.5 collective-permute-start.9
  62.7 10.5 collective-permute-start.5
  64.8 10.6 collective-permute-start.15
  64.9 10.6 collective-permute-start.27
  82.1 149.2 %collective-permute-start.40 = (bf16[192,768]{1,0:T(8,128)(2,1)S(1)}, bf16[192,768]{1,0:T(8,128)(2,1)}, u32[]{:S(2)}, u32[]{:S(2)}) collective-permute-start(bf16[192,768]{1,0:T(8,128)(2,1)S(1)} %collective-permute-done.39.refs_6_), channel_id=1, source_target_pairs={{0,1},{1,0},{2,3},{3,2},{4,5},{5,4},{6,7},{7,6},{8,9},{9,8},{10,11... | collective-permute-start | bytes 884744 | tf_op jit(solution)/shard_map/ppermute | solution.py:80
  82.1 149.2 %collective-permute-start.48 = (bf16[192,768]{1,0:T(8,128)(2,1)S(1)}, bf16[192,768]{1,0:T(8,128)(2,1)}, u32[]{:S(2)}, u32[]{:S(2)}) collective-permute-start(bf16[192,768]{1,0:T(8,128)(2,1)S(1)} %collective-permute-done.43.refs_12_), channel_id=1, source_target_pairs={{0,1},{1,0},{2,3},{3,2},{4,5},{5,4},{6,7},{7,6},{8,9},{9,8},{10,11... | collective-permute-start | bytes 884744 | tf_op jit(solution)/shard_map/ppermute | solution.py:80
  83.3 146.9 %collective-permute-start.11 = (bf16[104,768]{1,0:T(8,128)(2,1)}, bf16[104,768]{1,0:T(8,128)(2,1)}, u32[]{:S(2)}, u32[]{:S(2)}) collective-permute-start(bf16[104,768]{1,0:T(8,128)(2,1)} %slice.562), channel_id=1, source_target_pairs={{0,2},{1,3},{4,0},{5,1},{8,4},{9,5},{12,8},{13,9},{14,12},{15,13},... | collective-permute-start | bytes 479240 | tf_op jit(solution)/shard_map/ppermute | solution.py:76
  85.0 145.7 %collective-permute-start.46 = (bf16[96,768]{1,0:T(8,128)(2,1)}, bf16[96,768]{1,0:T(8,128)(2,1)}, u32[]{:S(2)}, u32[]{:S(2)}) collective-permute-start(bf16[96,768]{1,0:T(8,128)(2,1)} %collective-permute-done.44.refs_8_), channel_id=1, source_target_pairs={{0,1},{1,0},{2,3},{3,2},{4,5},{5,4},{6,7},{7,6},{8,9},{9,8},{10,11... | collective-permute-start | bytes 442376 | tf_op jit(solution)/shard_map/ppermute | solution.py:80
  85.1 145.8 %collective-permute-start.47 = (bf16[96,768]{1,0:T(8,128)(2,1)}, bf16[96,768]{1,0:T(8,128)(2,1)}, u32[]{:S(2)}, u32[]{:S(2)}) collective-permute-start(bf16[96,768]{1,0:T(8,128)(2,1)} %collective-permute-done.45.refs_9_), channel_id=1, source_target_pairs={{0,1},{1,0},{2,3},{3,2},{4,5},{5,4},{6,7},{7,6},{8,9},{9,8},{10,11... | collective-permute-start | bytes 442376 | tf_op jit(solution)/shard_map/ppermute | solution.py:80
  230.2 150.2 %collective-permute-start.4 = (bf16[208,768]{1,0:T(8,128)(2,1)}, bf16[208,768]{1,0:T(8,128)(2,1)S(1)}, u32[]{:S(2)}, u32[]{:S(2)}) collective-permute-start(bf16[208,768]{1,0:T(8,128)(2,1)} %copy-done.68), channel_id=1, source_target_pairs={{0,1},{1,0},{2,3},{3,2},{4,5},{5,4},{6,7},{7,6},{8,9},{9,8},{10,11... | collective-permute-start | bytes 958472 | tf_op jit(solution)/shard_map/ppermute | solution.py:80
  230.7 149.8 %collective-permute-start.14 = (bf16[208,768]{1,0:T(8,128)(2,1)S(1)}, bf16[208,768]{1,0:T(8,128)(2,1)S(1)}, u32[]{:S(2)}, u32[]{:S(2)}) collective-permute-start(bf16[208,768]{1,0:T(8,128)(2,1)S(1)} %collective-permute-done.9.refs_12_), channel_id=1, source_target_pairs={{0,1},{1,0},{2,3},{3,2},{4,5},{5,4},{6,7},{7,6},{8,9},{9,8},{10,11... | collective-permute-start | bytes 958472 | tf_op jit(solution)/shard_map/ppermute | solution.py:80
  230.8 149.7 %collective-permute-start.6 = (bf16[208,768]{1,0:T(8,128)(2,1)S(1)}, bf16[208,768]{1,0:T(8,128)(2,1)S(1)}, u32[]{:S(2)}, u32[]{:S(2)}) collective-permute-start(bf16[208,768]{1,0:T(8,128)(2,1)S(1)} %collective-permute-done.5.refs_6_), channel_id=1, source_target_pairs={{0,1},{1,0},{2,3},{3,2},{4,5},{5,4},{6,7},{7,6},{8,9},{9,8},{10,11... | collective-permute-start | bytes 958472 | tf_op jit(solution)/shard_map/ppermute | solution.py:80
  231.2 149.3 %collective-permute-start.12 = (bf16[104,768]{1,0:T(8,128)(2,1)S(1)}, bf16[104,768]{1,0:T(8,128)(2,1)S(1)}, u32[]{:S(2)}, u32[]{:S(2)}) collective-permute-start(bf16[104,768]{1,0:T(8,128)(2,1)S(1)} %collective-permute-done.10.refs_8_), channel_id=1, source_target_pairs={{0,1},{1,0},{2,3},{3,2},{4,5},{5,4},{6,7},{7,6},{8,9},{9,8},{10,11... | collective-permute-start | bytes 479240 | tf_op jit(solution)/shard_map/ppermute | solution.py:80
  231.4 149.2 %collective-permute-start.13 = (bf16[104,768]{1,0:T(8,128)(2,1)}, bf16[104,768]{1,0:T(8,128)(2,1)S(1)}, u32[]{:S(2)}, u32[]{:S(2)}) collective-permute-start(bf16[104,768]{1,0:T(8,128)(2,1)} %collective-permute-done.11.refs_9_), channel_id=1, source_target_pairs={{0,1},{1,0},{2,3},{3,2},{4,5},{5,4},{6,7},{7,6},{8,9},{9,8},{10,11... | collective-permute-start | bytes 479240 | tf_op jit(solution)/shard_map/ppermute | solution.py:80
  600.6 20.8 %collective-permute-start.51 = (bf16[512,768]{1,0:T(8,128)(2,1)}, bf16[512,768]{1,0:T(8,128)(2,1)}, u32[]{:S(2)}, u32[]{:S(2)}) collective-permute-start(bf16[512,768]{1,0:T(8,128)(2,1)} %add_convert_fusion.6), channel_id=1, source_target_pairs={{0,16},{1,17},{2,18},{3,19},{4,20},{5,21},{6,22},{7,23},{8,24},{9,... | collective-permute-start | bytes 2359304 | tf_op jit(solution)/shard_map/ppermute | solution.py:366
  712.6 21.9 %collective-permute-start.52 = (bf16[512,768]{1,0:T(8,128)(2,1)S(1)}, bf16[512,768]{1,0:T(8,128)(2,1)S(1)}, u32[]{:S(2)}, u32[]{:S(2)}) collective-permute-start(bf16[512,768]{1,0:T(8,128)(2,1)S(1)} %add_convert_fusion.1), channel_id=1, source_target_pairs={{16,0},{17,1},{18,2},{19,3},{20,4},{21,5},{22,6},{23,7},{24,8},{25... | collective-permute-start | bytes 2359304 | tf_op jit(solution)/shard_map/ppermute | solution.py:373
  923.4 338.4 %collective-permute-start.71 = (bf16[8,192,768]{2,1,0:T(8,128)(2,1)}, bf16[8,192,768]{2,1,0:T(8,128)(2,1)}, u32[]{:S(2)}, u32[]{:S(2)}) collective-permute-start(bf16[8,192,768]{2,1,0:T(8,128)(2,1)} %get-tuple-element.50), channel_id=1, source_target_pairs={{0,1},{1,0},{2,3},{3,2},{4,5},{5,4},{6,7},{7,6},{8,9},{9,8},{10,11... | collective-permute-start | bytes 7077896 | tf_op jit(solution)/shard_map/ppermute | solution.py:80
  1072.9 192.2 %collective-permute-start.62 = (bf16[8,192,768]{2,1,0:T(8,128)(2,1)}, bf16[8,192,768]{2,1,0:T(8,128)(2,1)}, u32[]{:S(2)}, u32[]{:S(2)}) collective-permute-start(bf16[8,192,768]{2,1,0:T(8,128)(2,1)} %get-tuple-element.48), channel_id=1, source_target_pairs={{0,1},{1,0},{2,3},{3,2},{4,5},{5,4},{6,7},{7,6},{8,9},{9,8},{10,11... | collective-permute-start | bytes 7077896 | tf_op jit(solution)/shard_map/ppermute | solution.py:80
  1254.5 19.6 %collective-permute-start.53 = (bf16[8,208,768]{2,1,0:T(8,128)(2,1)}, bf16[8,208,768]{2,1,0:T(8,128)(2,1)S(1)}, u32[]{:S(2)}, u32[]{:S(2)}) collective-permute-start(bf16[8,208,768]{2,1,0:T(8,128)(2,1)} %get-tuple-element.46), channel_id=1, source_target_pairs={{0,1},{1,0},{2,3},{3,2},{4,5},{5,4},{6,7},{7,6},{8,9},{9,8},{10,11... | collective-permute-start | bytes 7667720 | tf_op jit(solution)/shard_map/ppermute | solution.py:80
  1270.9 40.1 %collective-permute-start.77 = (bf16[192,768]{1,0:T(8,128)(2,1)S(1)}, bf16[192,768]{1,0:T(8,128)(2,1)S(1)}, u32[]{:S(2)}, u32[]{:S(2)}) collective-permute-start(bf16[192,768]{1,0:T(8,128)(2,1)S(1)} %pad_maximum_fusion.8), channel_id=1, source_target_pairs={{0,2},{1,3},{4,0},{5,1},{8,4},{9,5},{12,8},{13,9},{14,12},{15,13},... | collective-permute-start | bytes 884744 | tf_op jit(solution)/shard_map/ppermute | solution.py:76
  1272.5 20.3 %collective-permute-start.73 = (bf16[192,768]{1,0:T(8,128)(2,1)S(1)}, bf16[192,768]{1,0:T(8,128)(2,1)S(1)}, u32[]{:S(2)}, u32[]{:S(2)}) collective-permute-start(bf16[192,768]{1,0:T(8,128)(2,1)S(1)} %pad_maximum_fusion.7), channel_id=1, source_target_pairs={{0,4},{1,5},{4,8},{5,9},{8,12},{9,13},{12,14},{13,15},{14,10},{15,... | collective-permute-start | bytes 884744 | tf_op jit(solution)/shard_map/ppermute | solution.py:72
  1276.4 25.9 %collective-permute-start.68 = (bf16[192,768]{1,0:T(8,128)(2,1)S(1)}, bf16[192,768]{1,0:T(8,128)(2,1)S(1)}, u32[]{:S(2)}, u32[]{:S(2)}) collective-permute-start(bf16[192,768]{1,0:T(8,128)(2,1)S(1)} %pad_maximum_fusion.6), channel_id=1, source_target_pairs={{0,2},{1,3},{4,0},{5,1},{8,4},{9,5},{12,8},{13,9},{14,12},{15,13},... | collective-permute-start | bytes 884744 | tf_op jit(solution)/shard_map/ppermute | solution.py:76
  1284.7 33.0 %collective-permute-start.59 = (bf16[208,768]{1,0:T(8,128)(2,1)S(1)}, bf16[208,768]{1,0:T(8,128)(2,1)S(1)}, u32[]{:S(2)}, u32[]{:S(2)}) collective-permute-start(bf16[208,768]{1,0:T(8,128)(2,1)S(1)} %pad_maximum_fusion.3), channel_id=1, source_target_pairs={{0,2},{1,3},{4,0},{5,1},{8,4},{9,5},{12,8},{13,9},{14,12},{15,13},... | collective-permute-start | bytes 958472 | tf_op jit(solution)/shard_map/ppermute | solution.py:76
  1291.3 10.5 collective-permute-start.55
  1292.8 15.2 %collective-permute-start.65 = (bf16[192,768]{1,0:T(8,128)(2,1)S(1)}, bf16[192,768]{1,0:T(8,128)(2,1)S(1)}, u32[]{:S(2)}, u32[]{:S(2)}) collective-permute-start(bf16[192,768]{1,0:T(8,128)(2,1)S(1)} %fusion.130), channel_id=1, source_target_pairs={{0,4},{1,5},{4,8},{5,9},{8,12},{9,13},{12,14},{13,15},{14,10},{15,... | collective-permute-start | bytes 884744 | tf_op jit(solution)/shard_map/ppermute | solution.py:72
  1301.7 12.6 collective-permute-start.74
  1302.3 18.9 %collective-permute-start.56 = (bf16[208,768]{1,0:T(8,128)(2,1)S(1)}, bf16[208,768]{1,0:T(8,128)(2,1)S(1)}, u32[]{:S(2)}, u32[]{:S(2)}) collective-permute-start(bf16[208,768]{1,0:T(8,128)(2,1)S(1)} %fusion.116), channel_id=1, source_target_pairs={{0,4},{1,5},{4,8},{5,9},{8,12},{9,13},{12,14},{13,15},{14,10},{15,... | collective-permute-start | bytes 958472 | tf_op jit(solution)/shard_map/ppermute | solution.py:72
  1309.3 13.7 %collective-permute-start.69 = (bf16[192,768]{1,0:T(8,128)(2,1)S(1)}, bf16[192,768]{1,0:T(8,128)(2,1)S(1)}, u32[]{:S(2)}, u32[]{:S(2)}) collective-permute-start(bf16[192,768]{1,0:T(8,128)(2,1)S(1)} %get-tuple-element.96), channel_id=1, source_target_pairs={{0,2},{1,3},{4,0},{5,1},{8,4},{9,5},{12,8},{13,9},{14,12},{15,13},... | collective-permute-start | bytes 884744 | tf_op jit(solution)/shard_map/ppermute | solution.py:76
  1317.3 22.7 %collective-permute-start.75 = (bf16[192,768]{1,0:T(8,128)(2,1)S(1)}, bf16[192,768]{1,0:T(8,128)(2,1)S(1)}, u32[]{:S(2)}, u32[]{:S(2)}) collective-permute-start(bf16[192,768]{1,0:T(8,128)(2,1)S(1)} %get-tuple-element.87), channel_id=1, source_target_pairs={{0,4},{1,5},{4,8},{5,9},{8,12},{9,13},{12,14},{13,15},{14,10},{15,... | collective-permute-start | bytes 884744 | tf_op jit(solution)/shard_map/ppermute | solution.py:72
  1317.7 16.4 %collective-permute-start.66 = (bf16[192,768]{1,0:T(8,128)(2,1)S(1)}, bf16[192,768]{1,0:T(8,128)(2,1)S(1)}, u32[]{:S(2)}, u32[]{:S(2)}) collective-permute-start(bf16[192,768]{1,0:T(8,128)(2,1)S(1)} %get-tuple-element.95), channel_id=1, source_target_pairs={{0,4},{1,5},{4,8},{5,9},{8,12},{9,13},{12,14},{13,15},{14,10},{15,... | collective-permute-start | bytes 884744 | tf_op jit(solution)/shard_map/ppermute | solution.py:72
  1321.5 11.0 collective-permute-start.60
  1323.1 23.3 %collective-permute-start.57 = (bf16[208,768]{1,0:T(8,128)(2,1)S(1)}, bf16[208,768]{1,0:T(8,128)(2,1)S(1)}, u32[]{:S(2)}, u32[]{:S(2)}) collective-permute-start(bf16[208,768]{1,0:T(8,128)(2,1)S(1)} %get-tuple-element.75), channel_id=1, source_target_pairs={{0,4},{1,5},{4,8},{5,9},{8,12},{9,13},{12,14},{13,15},{14,10},{15,... | collective-permute-start | bytes 958472 | tf_op jit(solution)/shard_map/ppermute | solution.py:72
  1325.7 13.2 collective-permute-start.70
  1332.5 11.0 collective-permute-start.79
  1334.2 12.8 collective-permute-start.61
  (144 other events, 2731.6 us)

commit v2 on v1

v2 whole, which is shorter than its diff:
```python
import jax
import jax.numpy as jnp
from jax import lax
from jax.experimental import pallas as pl
from jax.experimental.pallas import tpu as pltpu
from jax.sharding import PartitionSpec as P

H = 16
GRID = 16
LEAD = 16
RING = 8
VEC_ROWS = 16

f32 = jnp.float32
bf16 = jnp.bfloat16
eps_norm = 1e-05


def chip_at(place):
    if isinstance(place, int):
        return 2 * place if place < 4 else 2 * (7 - place) + 1
    return jnp.where(place < 4, 2 * place, 2 * (7 - place) + 1)


def place_of(chip):
    if isinstance(chip, int):
        return chip // 2 if chip % 2 == 0 else 7 - chip // 2
    return jnp.where(chip % 2 == 0, chip // 2, 7 - chip // 2)


def ring_route(step):
    return [
        (2 * chip_at(place) + core, 2 * chip_at((place + step) % RING) + core)
        for place in range(RING)
        for core in range(2)
    ]


CORE_ROUTE = [(index, index ^ 1) for index in range(2 * RING)]


def onward(block):
    return lax.ppermute(block, "dp", ring_route(1))


def backward(block):
    return lax.ppermute(block, "dp", ring_route(-1))


def across(block):
    return lax.ppermute(block, "dp", CORE_ROUTE)


def ring_gather(shard):
    half = shard.shape[0] // 2
    here = {0: shard}
    up, down = shard, shard
    for step in range(1, RING // 2):
        up, down = onward(up), backward(down)
        here[RING - step], here[step] = up, down
    far = (onward(up[:half]), backward(down[half:]))
    blocks = []
    for place in range(RING):
        if place == RING // 2:
            blocks += [far[0], far[1], across(far[0]), across(far[1])]
        else:
            blocks += [here[place], across(here[place])]
    return blocks


def assemble(blocks):
    rows, width = blocks[0].shape
    half = rows // 2
    count = len(blocks)

    def kernel(*refs):
        blocks_in, out, sems = refs[:count], refs[count], refs[count + 1]
        me = lax.axis_index("dp")
        core, place = lax.rem(me, 2), place_of(lax.div(me, 2))
        copies = []
        at = 0
        for step in range(RING):
            chip = chip_at(lax.rem(place + step, RING))
            parts = ((0, half), (half, half)) if step == RING // 2 else ((0, rows),)
            for owner in (2 * chip + core, 2 * chip + 1 - core):
                for start, size in parts:
                    copies.append(
                        pltpu.make_async_copy(
                            blocks_in[at], out.at[owner, pl.ds(start, size)], sems.at[at]
                        )
                    )
                    at += 1
        for copy in copies:
            copy.start()
        for copy in copies:
            copy.wait()

    return pl.pallas_call(
        kernel,
        out_shape=jax.ShapeDtypeStruct((2 * RING, rows, width), blocks[0].dtype),
        in_specs=[pl.BlockSpec(memory_space=pl.ANY)] * count,
        out_specs=pl.BlockSpec(memory_space=pltpu.VMEM),
        scratch_shapes=[pltpu.SemaphoreType.DMA((count,))],
        compiler_params=pltpu.CompilerParams(vmem_limit_bytes=16 * 2**20),
        name="assemble",
    )(*blocks)


def ring_scatter(own, peer):
    rows = own.shape[1]
    half = rows // 2
    arrived = across(peer)

    def local(step, start=0, size=rows):
        return own[step, start : start + size].astype(f32) + arrived[step, start : start + size].astype(f32)

    far = RING // 2
    up = onward(local(far, 0, half).astype(bf16))
    down = backward(local(far, half, half).astype(bf16))
    joint_up = jnp.concatenate([local(far - 1, 0, half) + up.astype(f32), local(far - 1, half, half)], 0)
    joint_down = jnp.concatenate([local(far + 1, 0, half), local(far + 1, half, half) + down.astype(f32)], 0)
    up, down = onward(joint_up.astype(bf16)), backward(joint_down.astype(bf16))
    for step in range(far - 2, 0, -1):
        up = onward((local(step) + up.astype(f32)).astype(bf16))
        down = backward((local(RING - step) + down.astype(f32)).astype(bf16))
    return local(0) + up.astype(f32) + down.astype(f32)


VMEM_LIMIT = 48 * 2**20
MLP_CHUNK = 32
Q_BIAS, V_BIAS, OUT_BIAS, DOWN_BIAS, GAIN_ONE, SHIFT_ONE, GAIN_TWO, SHIFT_TWO, UP_BIAS = range(9)
NT = (((1,), (1,)), ((), ()))
TN = (((0,), (0,)), ((), ()))


def dot(first_mat, second_mat):
    return jnp.dot(first_mat, second_mat, preferred_element_type=f32)


def dot_nt(first_mat, second_mat):
    return lax.dot_general(first_mat, second_mat, NT, preferred_element_type=f32)


def dot_tn(first_mat, second_mat):
    return lax.dot_general(first_mat, second_mat, TN, preferred_element_type=f32)


def weight_part(w_ref, part):
    width = w_ref.shape[2]
    rows = width // LEAD
    return w_ref[:, part * rows : (part + 1) * rows, :].reshape(width, width)


def norm_parts(rows_in):
    average = jnp.mean(rows_in, axis=-1, keepdims=True)
    centred = rows_in - average
    inverse = lax.rsqrt(jnp.mean(centred * centred, axis=-1, keepdims=True) + eps_norm)
    return centred * inverse, inverse


def norm_back(rows_in, gain_row, grad_rows):
    unit, inverse = norm_parts(rows_in)
    scaled = grad_rows * gain_row
    mean_one = jnp.mean(scaled, axis=-1, keepdims=True)
    mean_two = jnp.mean(scaled * unit, axis=-1, keepdims=True)
    return (scaled - mean_one - unit * mean_two) * inverse, grad_rows * unit


def head_window(head, head_size, width):
    start = min(head * head_size // 128 * 128, width - 256)
    return start, head * head_size - start


def only_head(block, low, head_size):
    lane = lax.broadcasted_iota(jnp.int32, block.shape, 1)
    return jnp.where((lane >= low) & (lane < low + head_size), block, jnp.zeros_like(block))


def column_sum(rows_in):
    return jnp.sum(rows_in, axis=0, keepdims=True)


def attn_forward_kernel(
    heights_ref, widths_ref, x_ref, w_ref, vec_ref,
    middle_ref, second_ref, normed_ref, q_ref, k_ref, v_ref, probs_ref, attended_ref,
    vt_ref, at_ref,
):
    slots, width = x_ref.shape
    head_size = width // H
    step = 64
    for at in range(0, slots, step):
        unit, _ = norm_parts(x_ref[at : at + step, :].astype(f32))
        normed_ref[at : at + step, :] = (
            unit * vec_ref[GAIN_ONE : GAIN_ONE + 1, :] + vec_ref[SHIFT_ONE : SHIFT_ONE + 1, :]
        ).astype(bf16)
    normed = normed_ref[...]
    q_ref[...] = (dot(normed, weight_part(w_ref, 0)) + vec_ref[Q_BIAS : Q_BIAS + 1, :]).astype(bf16)
    k_ref[...] = dot(normed, weight_part(w_ref, 1)).astype(bf16)
    values = dot(normed, weight_part(w_ref, 2)) + vec_ref[V_BIAS : V_BIAS + 1, :]
    v_ref[...] = values.astype(bf16)
    vt_ref[...] = values.astype(bf16).T
    image = pl.program_id(0)
    slot = lax.broadcasted_iota(jnp.int32, (slots, 128), 0)
    valid = (slot // GRID < heights_ref[image]) & (slot % GRID < widths_ref[image])
    mask = jnp.where(valid, 0.0, -1e30).astype(f32)
    scale = head_size ** (-0.5)
    for head in range(H):
        start, low = head_window(head, head_size, width)
        queries = only_head(q_ref[:, start : start + 256], low, head_size)
        scores = dot_nt(k_ref[:, start : start + 256], queries)
        for at in range(0, slots, 128):
            part = scores[:, at : at + 128] * scale + mask
            exponent = jnp.exp(part - jnp.max(part, axis=0, keepdims=True))
            inverse = 1.0 / jnp.sum(exponent, axis=0, keepdims=True)
            probs_ref[head, :, at : at + 128] = (exponent * inverse).astype(bf16)
        here = slice(head * head_size, (head + 1) * head_size)
        at_ref[here, :] = dot(vt_ref[here, :], probs_ref[head])
    attended_ref[...] = at_ref[...].T.astype(bf16)
    branch = dot(attended_ref[...], weight_part(w_ref, 3))
    middle_ref[...] = x_ref[...].astype(f32) + (branch + vec_ref[OUT_BIAS : OUT_BIAS + 1, :])
    for at in range(0, slots, step):
        unit, _ = norm_parts(middle_ref[at : at + step, :])
        second_ref[at : at + step, :] = (
            unit * vec_ref[GAIN_TWO : GAIN_TWO + 1, :] + vec_ref[SHIFT_TWO : SHIFT_TWO + 1, :]
        ).astype(bf16)


def attn_forward(layer_input, attn_w, vecs, heights, widths):
    count, width = layer_input.shape
    images = heights.shape[0]
    slots = count // images
    rows = pl.BlockSpec((slots, width), lambda i, *_: (i, 0))
    wide = jax.ShapeDtypeStruct((count, width), f32)
    low = jax.ShapeDtypeStruct((count, width), bf16)
    flops = 8 * count * width * width + 4 * count * slots * width
    return pl.pallas_call(
        attn_forward_kernel,
        grid_spec=pltpu.PrefetchScalarGridSpec(
            num_scalar_prefetch=2,
            grid=(images,),
            in_specs=[
                rows,
                pl.BlockSpec(attn_w.shape, lambda i, *_: (0, 0, 0), pipeline_mode=pl.Buffered(1)),
                pl.BlockSpec(vecs.shape, lambda i, *_: (0, 0)),
            ],
            out_specs=[rows] * 6
            + [pl.BlockSpec((None, H, slots, slots), lambda i, *_: (i, 0, 0, 0)), rows],
            scratch_shapes=[pltpu.VMEM((width, slots), bf16), pltpu.VMEM((width, slots), f32)],
        ),
        out_shape=[wide, low, low, low, low, low, jax.ShapeDtypeStruct((images, H, slots, slots), bf16), low],
        compiler_params=pltpu.CompilerParams(vmem_limit_bytes=VMEM_LIMIT),
        cost_estimate=pl.CostEstimate(
            flops=flops, bytes_accessed=attn_w.size * 2 + count * width * 20, transcendentals=count * slots * H
        ),
        name="attn_forward",
    )(heights, widths, layer_input, attn_w, vecs)


def mlp_forward_kernel(
    middle_ref, second_ref, up_ref, down_ref, vec_ref, result_ref, act_ref, slope_ref, pre_ref, acc_ref
):
    index = pl.program_id(0)
    count, width = second_ref.shape
    pre_ref[...] = dot(second_ref[...], up_ref[...].reshape(width, width))
    bias = vec_ref[pl.ds(UP_BIAS + index, 1), :]

    def gelu_rows(at, _):
        here = pl.ds(at * MLP_CHUNK, MLP_CHUNK)
        pre = pre_ref[here, :] + bias
        below = 0.5 * (1.0 + lax.erf(pre * (0.5**0.5)))
        act_ref[here, :] = (pre * below).astype(bf16)
        bell = jnp.exp(-0.5 * pre * pre) * (0.5 / jnp.pi) ** 0.5
        slope_ref[here, :] = (below + pre * bell).astype(bf16)
        return 0

    lax.fori_loop(0, count // MLP_CHUNK, gelu_rows, 0)
    added = dot(act_ref[...], down_ref[...].reshape(width, width))

    @pl.when(index == 0)
    def _():
        acc_ref[...] = added

    @pl.when(index > 0)
    def _():
        acc_ref[...] += added

    @pl.when(index == pl.num_programs(0) - 1)
    def _():
        result_ref[...] = (
            middle_ref[...] + (acc_ref[...] + vec_ref[DOWN_BIAS : DOWN_BIAS + 1, :])
        ).astype(bf16)


def mlp_forward(middle, second, up_w, down_w, vecs):
    count, width = middle.shape
    parts = up_w.shape[1] * LEAD // width
    whole = pl.BlockSpec((count, width), lambda j: (0, 0))
    chunk = pl.BlockSpec((count, width), lambda j: (0, j))
    low = jax.ShapeDtypeStruct((count, width), bf16)
    hidden = jax.ShapeDtypeStruct((count, width * parts), bf16)
    return pl.pallas_call(
        mlp_forward_kernel,
        grid=(parts,),
        in_specs=[
            whole,
            whole,
            pl.BlockSpec((LEAD, width // LEAD, width), lambda j: (0, j, 0)),
            pl.BlockSpec((LEAD // parts, down_w.shape[1], width), lambda j: (j, 0, 0)),
            pl.BlockSpec(vecs.shape, lambda j: (0, 0)),
        ],
        out_specs=[whole, chunk, chunk],
        out_shape=[low, hidden, hidden],
        scratch_shapes=[pltpu.VMEM((count, width), f32)] * 2,
        compiler_params=pltpu.CompilerParams(vmem_limit_bytes=VMEM_LIMIT),
        cost_estimate=pl.CostEstimate(
            flops=4 * count * width * width * parts,
            bytes_accessed=up_w.size * 4 + count * width * (8 + 4 * parts),
            transcendentals=2 * count * width * parts,
        ),
        name="mlp_forward",
    )(middle, second, up_w, down_w, vecs)


def mlp_backward_kernel(
    upstream_ref, slope_ref, middle_ref, up_ref, down_ref, vec_ref,
    grad_middle_ref, grad_pre_ref, sums_ref, up_sum_ref, ga_ref, acc_ref,
):
    index = pl.program_id(0)
    count, width = upstream_ref.shape
    ga_ref[...] = dot_nt(upstream_ref[...], down_ref[...].reshape(width, width))
    sums = jnp.zeros((1, width), f32)
    for at in range(0, count, MLP_CHUNK):
        here = slice(at, at + MLP_CHUNK)
        pre = (ga_ref[here, :] * slope_ref[here, :].astype(f32)).astype(bf16)
        grad_pre_ref[here, :] = pre
        sums += column_sum(pre.astype(f32))
    up_sum_ref[0] = sums
    added = dot_nt(grad_pre_ref[...], up_ref[...].reshape(width, width))

    @pl.when(index == 0)
    def _():
        acc_ref[...] = added

    @pl.when(index > 0)
    def _():
        acc_ref[...] += added

    @pl.when(index == pl.num_programs(0) - 1)
    def _():
        gain = vec_ref[GAIN_TWO : GAIN_TWO + 1, :]
        down_sum = jnp.zeros((1, width), f32)
        gain_sum = jnp.zeros((1, width), f32)
        shift_sum = jnp.zeros((1, width), f32)
        for at in range(0, count, MLP_CHUNK):
            here = slice(at, at + MLP_CHUNK)
            upstream = upstream_ref[here, :].astype(f32)
            grad = acc_ref[here, :]
            grad_mid, gain_terms = norm_back(middle_ref[here, :], gain, grad)
            grad_middle_ref[here, :] = upstream + grad_mid
            down_sum += column_sum(upstream)
            gain_sum += column_sum(gain_terms)
            shift_sum += column_sum(grad)
        sums_ref[0:1, :] = down_sum
        sums_ref[1:2, :] = gain_sum
        sums_ref[2:3, :] = shift_sum


def mlp_backward(upstream, slope, middle, up_w, down_w, vecs):
    count, width = middle.shape
    parts = up_w.shape[1] * LEAD // width
    whole = pl.BlockSpec((count, width), lambda j: (0, 0))
    chunk = pl.BlockSpec((count, width), lambda j: (0, j))
    return pl.pallas_call(
        mlp_backward_kernel,
        grid=(parts,),
        in_specs=[
            whole,
            chunk,
            whole,
            pl.BlockSpec((LEAD, width // LEAD, width), lambda j: (0, j, 0)),
            pl.BlockSpec((LEAD // parts, down_w.shape[1], width), lambda j: (j, 0, 0)),
            pl.BlockSpec(vecs.shape, lambda j: (0, 0)),
        ],
        out_specs=[
            whole,
            chunk,
            pl.BlockSpec((8, width), lambda j: (0, 0)),
            pl.BlockSpec((1, 1, width), lambda j: (j, 0, 0)),
        ],
        out_shape=[
            jax.ShapeDtypeStruct((count, width), f32),
            jax.ShapeDtypeStruct((count, width * parts), bf16),
            jax.ShapeDtypeStruct((8, width), f32),
            jax.ShapeDtypeStruct((parts, 1, width), f32),
        ],
        scratch_shapes=[pltpu.VMEM((count, width), f32)] * 2,
        compiler_params=pltpu.CompilerParams(vmem_limit_bytes=VMEM_LIMIT),
        cost_estimate=pl.CostEstimate(
            flops=4 * count * width * width * parts,
            bytes_accessed=up_w.size * 4 + count * width * (10 + 4 * parts),
            transcendentals=0,
        ),
        name="mlp_backward",
    )(upstream, slope, middle, up_w, down_w, vecs)


def attn_backward_kernel(
    grad_middle_ref, x_ref, q_ref, k_ref, v_ref, probs_ref, w_ref, vec_ref,
    grad_in_ref, grad_low_ref, branch_ref, gq_ref, gk_ref, gv_ref, sums_ref,
    ga_ref, gat_ref, qt_ref, kt_ref, gqt_ref, gkt_ref, gvt_ref,
):
    slots, width = x_ref.shape
    head_size = width // H
    scale = head_size ** (-0.5)
    branch_ref[...] = grad_middle_ref[...].astype(bf16)
    ga = dot_nt(branch_ref[...], weight_part(w_ref, 3)).astype(bf16)
    ga_ref[...] = ga
    gat_ref[...] = ga.T
    qt_ref[...] = q_ref[...].T
    kt_ref[...] = k_ref[...].T
    for head in range(H):
        start, low = head_window(head, head_size, width)
        here = slice(head * head_size, (head + 1) * head_size)
        own = only_head(ga_ref[:, start : start + 256], low, head_size)
        grad_probs = dot_nt(v_ref[:, start : start + 256], own)
        pieces = []
        for at in range(0, slots, 128):
            probs = probs_ref[head, :, at : at + 128].astype(f32)
            grad = grad_probs[:, at : at + 128]
            total = jnp.sum(probs * grad, axis=0, keepdims=True)
            pieces.append((probs * (grad - total)).astype(bf16))
        grad_scores = jnp.concatenate(pieces, axis=1)
        gvt_ref[here, :] = dot_nt(gat_ref[here, :], probs_ref[head])
        gqt_ref[here, :] = dot(kt_ref[here, :], grad_scores) * scale
        gkt_ref[here, :] = dot_nt(qt_ref[here, :], grad_scores) * scale
    gq_ref[...] = gqt_ref[...].T.astype(bf16)
    gk_ref[...] = gkt_ref[...].T.astype(bf16)
    gv_ref[...] = gvt_ref[...].T.astype(bf16)
    grad_normed = dot_nt(gq_ref[...], weight_part(w_ref, 0))
    grad_normed += dot_nt(gk_ref[...], weight_part(w_ref, 1))
    grad_normed += dot_nt(gv_ref[...], weight_part(w_ref, 2))
    grad_in_ref[...] = grad_normed
    gain = vec_ref[GAIN_ONE : GAIN_ONE + 1, :]
    sums = [jnp.zeros((1, width), f32)] * 5
    for at in range(0, slots, MLP_CHUNK):
        rows = slice(at, at + MLP_CHUNK)
        grad = grad_in_ref[rows, :]
        grad_norm, gain_terms = norm_back(x_ref[rows, :].astype(f32), gain, grad)
        total = grad_middle_ref[rows, :] + grad_norm
        grad_in_ref[rows, :] = total
        grad_low_ref[rows, :] = total.astype(bf16)
        terms = (
            gq_ref[rows, :].astype(f32), gv_ref[rows, :].astype(f32), branch_ref[rows, :].astype(f32),
            gain_terms, grad,
        )
        sums = [old + column_sum(new) for old, new in zip(sums, terms)]

    first = pl.program_id(0) == 0
    for row, value in enumerate(sums):
        sums_ref[row : row + 1, :] = value + jnp.where(first, 0.0, sums_ref[row : row + 1, :])


def attn_backward(grad_middle, layer_input, saved, attn_w, vecs, images):
    queries, key_rows, values, probs = saved
    count, width = layer_input.shape
    slots = count // images
    rows = pl.BlockSpec((slots, width), lambda i: (i, 0))
    low = jax.ShapeDtypeStruct((count, width), bf16)
    flipped = pltpu.VMEM((width, slots), bf16)
    flipped_wide = pltpu.VMEM((width, slots), f32)
    return pl.pallas_call(
        attn_backward_kernel,
        grid=(images,),
        in_specs=[rows] * 5
        + [
            pl.BlockSpec((None, H, slots, slots), lambda i: (i, 0, 0, 0)),
            pl.BlockSpec(attn_w.shape, lambda i: (0, 0, 0), pipeline_mode=pl.Buffered(1)),
            pl.BlockSpec(vecs.shape, lambda i: (0, 0)),
        ],
        out_specs=[rows] * 6 + [pl.BlockSpec((8, width), lambda i: (0, 0))],
        out_shape=[jax.ShapeDtypeStruct((count, width), f32)] + [low] * 5 + [jax.ShapeDtypeStruct((8, width), f32)],
        scratch_shapes=[pltpu.VMEM((slots, width), bf16)] + [flipped] * 3 + [flipped_wide] * 3,
        compiler_params=pltpu.CompilerParams(vmem_limit_bytes=VMEM_LIMIT),
        cost_estimate=pl.CostEstimate(
            flops=8 * count * width * width + 8 * count * slots * width,
            bytes_accessed=attn_w.size * 2 + count * width * 30,
            transcendentals=0,
        ),
        name="attn_backward",
    )(grad_middle, layer_input, queries, key_rows, values, probs, attn_w, vecs)


def ring_slot(owner, me):
    there, here = place_of(lax.div(owner, 2)), place_of(lax.div(me, 2))
    return lax.rem(there - here + RING, RING)


def store_block(own_ref, peer_ref, owner, core, rows, value):
    me = lax.axis_index("dp")
    slot = ring_slot(owner, me)

    @pl.when(lax.rem(me, 2) == core)
    def _():
        own_ref[slot, rows, :] = value

    @pl.when(lax.rem(me, 2) != core)
    def _():
        peer_ref[slot, rows, :] = value


def scatter_shapes(rows, width):
    return [jax.ShapeDtypeStruct((RING, rows, width), bf16)] * 2


def grad_down_kernel(act_ref, upstream_ref, own_ref, peer_ref):
    index = pl.program_id(0)
    rows = own_ref.shape[1]
    value = dot_tn(act_ref[...], upstream_ref[...]).astype(bf16)
    for at in range(value.shape[0] // rows):
        owner = index * (value.shape[0] // rows) + at
        store_block(own_ref, peer_ref, owner, at % 2, slice(None), value[at * rows : (at + 1) * rows])


def grad_down_blocks(activated, upstream):
    count, width = upstream.shape
    hidden = activated.shape[1]
    parts = hidden // width
    rows = hidden // LEAD
    return pl.pallas_call(
        grad_down_kernel,
        grid=(parts,),
        in_specs=[
            pl.BlockSpec((count, width), lambda j: (0, j)),
            pl.BlockSpec((count, width), lambda j: (0, 0)),
        ],
        out_specs=[pl.BlockSpec((RING, rows, width), lambda j: (0, 0, 0))] * 2,
        out_shape=scatter_shapes(rows, width),
        compiler_params=pltpu.CompilerParams(vmem_limit_bytes=VMEM_LIMIT),
        cost_estimate=pl.CostEstimate(
            flops=2 * count * width * hidden, bytes_accessed=count * hidden * 2 + hidden * width * 2, transcendentals=0
        ),
        name="grad_down",
    )(activated, upstream)


def grad_up_kernel(second_ref, pre_ref, own_ref, peer_ref, flip_ref):
    index = pl.program_id(0)
    width = second_ref.shape[1]
    rows = width // LEAD

    @pl.when(index == 0)
    def _():
        flip_ref[...] = second_ref[...].T

    value = dot(flip_ref[...], pre_ref[...]).astype(bf16)
    for owner in range(LEAD):
        here = pl.ds(pl.multiple_of(index * rows, rows), rows)
        store_block(own_ref, peer_ref, owner, owner % 2, here, value[owner * rows : (owner + 1) * rows])


def grad_up_blocks(second, grad_pre):
    count, width = second.shape
    hidden = grad_pre.shape[1]
    parts = hidden // width
    rows = hidden // LEAD
    return pl.pallas_call(
        grad_up_kernel,
        grid=(parts,),
        in_specs=[
            pl.BlockSpec((count, width), lambda j: (0, 0)),
            pl.BlockSpec((count, width), lambda j: (0, j)),
        ],
        out_specs=[pl.BlockSpec((RING, rows, width), lambda j: (0, 0, 0))] * 2,
        out_shape=scatter_shapes(rows, width),
        scratch_shapes=[pltpu.VMEM((width, count), bf16)],
        compiler_params=pltpu.CompilerParams(vmem_limit_bytes=VMEM_LIMIT),
        cost_estimate=pl.CostEstimate(
            flops=2 * count * width * hidden, bytes_accessed=count * hidden * 2 + hidden * width * 2, transcendentals=0
        ),
        name="grad_up",
    )(second, grad_pre)


def grad_first_kernel(
    normed_ref, attended_ref, gq_ref, gk_ref, gv_ref, branch_ref, vec_ref, own_ref, peer_ref, flip_ref
):
    width = normed_ref.shape[1]
    rows = width // LEAD
    flip_ref[...] = normed_ref[...].T
    for part, right in enumerate((gq_ref, gk_ref, gv_ref, branch_ref)):
        if part == 3:
            flip_ref[...] = attended_ref[...].T
        value = dot(flip_ref[...], right[...]).astype(bf16)
        for owner in range(LEAD):
            here = slice(part * rows, (part + 1) * rows)
            store_block(own_ref, peer_ref, owner, owner % 2, here, value[owner * rows : (owner + 1) * rows])
    for owner in range(LEAD):
        here = slice(4 * rows, 4 * rows + VEC_ROWS)
        store_block(own_ref, peer_ref, owner, owner % 2, here, vec_ref[owner])


def grad_first_blocks(normed, attended, gq, gk, gv, branch, vec_block):
    count, width = normed.shape
    rows = 4 * width // LEAD + VEC_ROWS
    return pl.pallas_call(
        grad_first_kernel,
        in_specs=[pl.BlockSpec(memory_space=pltpu.VMEM)] * 7,
        out_specs=[pl.BlockSpec(memory_space=pltpu.VMEM)] * 2,
        out_shape=scatter_shapes(rows, width),
        scratch_shapes=[pltpu.VMEM((width, count), bf16)],
        compiler_params=pltpu.CompilerParams(vmem_limit_bytes=VMEM_LIMIT),
        cost_estimate=pl.CostEstimate(
            flops=8 * count * width * width, bytes_accessed=count * width * 12 + 8 * width * width, transcendentals=0
        ),
        name="grad_first",
    )(normed, attended, gq, gk, gv, branch, vec_block)


VECS = ("q_bias", "v_bias", "out_bias", "down_bias", "gain_one", "shift_one", "gain_two", "shift_two")


def by_columns(weight, width):
    columns = weight.shape[1]
    return jnp.concatenate([weight[:, at : at + width] for at in range(0, columns, width)], 0)


def back_by_columns(block, rows):
    return jnp.concatenate([block[at : at + rows] for at in range(0, block.shape[0], rows)], 1)


def solution(mesh):
    dp_size = mesh.shape["dp"]
    ringed = dp_size == 2 * RING

    def gather_weights(qkv, out, up, down, vectors):
        width = out.shape[1]
        if ringed:
            rows = out.shape[0]
            vec_rows = jnp.concatenate([jnp.stack([vectors[name] for name in VECS]), vectors["up_bias"].reshape(-1, rows)])
            vec_block = jnp.pad(vec_rows, ((0, VEC_ROWS - vec_rows.shape[0]), (0, width - rows)))
            first = assemble(ring_gather(jnp.concatenate([by_columns(qkv, width), out, vec_block], 0)))
            up_w = assemble(ring_gather(by_columns(up, width)))
            down_w = assemble(ring_gather(down))
            vec_all = first[:, first.shape[1] - VEC_ROWS :, :rows]
            count = len(VECS)
            vecs = vec_all[:, :count].transpose(1, 0, 2).reshape(count, width)
            ups = vec_all[:, count : vec_rows.shape[0]].reshape(-1, width)
        else:
            gathered = [lax.all_gather(w, "dp", axis=0, tiled=True) for w in (qkv, out, up, down)]
            blocked = [w.reshape(LEAD, -1, w.shape[1]) for w in gathered]
            fold = lambda w: w.reshape(LEAD, w.shape[1], -1, width).transpose(0, 2, 1, 3).reshape(LEAD, -1, width)
            first = jnp.concatenate([fold(blocked[0]), blocked[1], jnp.zeros((LEAD, VEC_ROWS, width), bf16)], 1)
            up_w, down_w = fold(blocked[2]), blocked[3]
            whole = lambda name: lax.all_gather(vectors[name], "dp", axis=0, tiled=True)
            vecs = jnp.stack([whole(name) for name in VECS])
            ups = whole("up_bias").reshape(-1, width)
        vecs = jnp.concatenate([vecs, ups], 0).astype(f32)
        return first, up_w, down_w, jnp.pad(vecs, ((0, VEC_ROWS - vecs.shape[0]), (0, 0)))

    def shards(
        tokens, cotangent, heights, widths, qkv_weight, out_weight, up_weight, down_weight,
        q_bias, v_bias, out_bias, up_bias, down_bias, gain_one, shift_one, gain_two, shift_two,
    ):
        leading = lax.axis_index("section") == 0
        width = tokens.shape[1]
        images = heights.shape[0]
        rows = width // LEAD
        vectors = dict(
            q_bias=q_bias[0], v_bias=v_bias[0], out_bias=out_bias[0], up_bias=up_bias[0], down_bias=down_bias[0],
            gain_one=gain_one[0], shift_one=shift_one[0], gain_two=gain_two[0], shift_two=shift_two[0],
        )
        attn_w, up_w, down_w, vecs = gather_weights(
            qkv_weight[0], out_weight[0], up_weight[0], down_weight[0], vectors
        )

        middle, second = attn_forward(tokens, attn_w, vecs, heights, widths)[:2]
        sent = mlp_forward(middle, second, up_w, down_w, vecs)[0]
        received = lax.ppermute(sent, "section", [(0, 1)])
        layer_input = jnp.where(leading, tokens, received)
        middle, second, normed, queries, key_rows, values, probs, attended = attn_forward(
            layer_input, attn_w, vecs, heights, widths
        )
        result, activated, slope = mlp_forward(middle, second, up_w, down_w, vecs)

        saved = (queries, key_rows, values, probs)
        grad_middle = mlp_backward(cotangent, slope, middle, up_w, down_w, vecs)[0]
        to_send = attn_backward(grad_middle, layer_input, saved, attn_w, vecs, images)[1]
        arriving = lax.ppermute(to_send, "section", [(1, 0)])
        upstream = jnp.where(leading, arriving, cotangent)
        if ringed:
            g_down = ring_scatter(*grad_down_blocks(activated, upstream))
        grad_middle, grad_pre, mlp_sums, up_sums = mlp_backward(upstream, slope, middle, up_w, down_w, vecs)
        if ringed:
            g_up = back_by_columns(ring_scatter(*grad_up_blocks(second, grad_pre)), rows)
        grad_input, _, branch, gq, gk, gv, attn_sums = attn_backward(
            grad_middle, layer_input, saved, attn_w, vecs, images
        )
        sums = jnp.concatenate([attn_sums[:3], mlp_sums[:1], attn_sums[3:5], mlp_sums[1:3]], 0)
        count = len(VECS)
        if ringed:
            parts = up_sums.shape[0]
            blocks = jnp.concatenate(
                [sums.reshape(count, LEAD, rows).transpose(1, 0, 2), up_sums.reshape(LEAD, parts, rows)], 1
            )
            blocks = jnp.pad(blocks, ((0, 0), (0, VEC_ROWS - count - parts), (0, width - rows))).astype(bf16)
            g_first = ring_scatter(*grad_first_blocks(normed, attended, gq, gk, gv, branch, blocks))
            g_qkv = back_by_columns(g_first[: 3 * rows], rows)
            g_out = g_first[3 * rows : 4 * rows]
            vec_rows = g_first[4 * rows :, :rows]
            g_vecs = {name: vec_rows[at] for at, name in enumerate(VECS)}
            g_vecs["up_bias"] = vec_rows[count : count + parts].reshape(-1)
        else:
            scatter = lambda a: lax.psum_scatter(a, "dp", scatter_dimension=0, tiled=True)
            outer = lambda a, b: lax.dot_general(a, b, TN, preferred_element_type=f32)
            g_down = scatter(outer(activated, upstream))
            g_up = scatter(outer(second, grad_pre))
            g_qkv = scatter(outer(normed, jnp.concatenate([gq, gk, gv], 1)))
            g_out = scatter(outer(attended, branch))
            g_vecs = {name: scatter(sums[at]) for at, name in enumerate(VECS)}
            g_vecs["up_bias"] = scatter(up_sums.reshape(-1))
        return (
            result[None], grad_input[None], g_qkv[None], g_out[None], g_up[None], g_down[None],
            *(
                g_vecs[name][None]
                for name in (
                    "q_bias", "v_bias", "out_bias", "up_bias", "down_bias",
                    "gain_one", "shift_one", "gain_two", "shift_two",
                )
            ),
        )

    rows_spec = P("dp", None)
    three, two = P("section", "dp", None), P("section", "dp")
    return jax.shard_map(
        shards,
        mesh=mesh,
        in_specs=(rows_spec, rows_spec, P("dp"), P("dp")) + (three,) * 4 + (two,) * 9,
        out_specs=(three,) * 6 + (two,) * 9,
        check_vma=False,
    )
```

time: 1360 us -> 399 us (0.29)
  Pallas kernels: 889 us -> 152 us
  matrix products: 158 us -> 0 us
  local copies, waits for them, and re-layouts: 75.7 us -> 34.8 us
  other arithmetic: 39.1 us -> 18.4 us
    pallas_call x3, Pallas kernels: 445 us -> 6.82 us  [assemble(): pl.pallas_call(kernel, out_shape=jax.ShapeDtypeStruct((2 * RING, rows, wi...]
    pallas_call x3 -> x11, Pallas kernels: 444 us -> 146 us  [the longest x2 38.3 us: attn_backward(): pl.pallas_call(attn_backward_kernel, grid=(images,), in_specs=[rows] * 5...]
    dot_general x38 -> x0, matrix products: 144 us -> none  [the longest x11 65.6 us: product(): return jnp.dot(first_mat, second_mat, preferred_element_type=f32)]
    convert_element_type x25 -> x0, local copies, waits for them, and re-layouts: 20.3 us -> none  [the longest x6 5.99 us: attn_backward(): a.reshape(images * slots, -1).astype(bf16)]
    sub x2 -> x0, matrix products: 13.7 us -> none  [attn_forward(): exponent = jnp.exp(scores - jnp.max(scores, axis=-1, keepdims=True))]
    unnamed x237 -> x62, local copies, waits for them, and re-layouts: 19.2 us -> 30.4 us
  transfers between devices with their start and end apart: 80 -> 80, of which waited for: 32 -> 35; matrix products, arithmetic and copies ran while one was open for 5% -> 6% of each run, Pallas kernels for 44% -> 10%
where the time goes in v2:
time: 399 us; the launch traced here: 395 us
  Pallas kernels  152 us (38%)
  waiting for transfers between devices  118 us (30%)
  starting transfers between devices  69.6 us (17%)
  local copies, waits for them, and re-layouts  34.8 us (9%)
  other arithmetic  18.4 us (5%)
    ppermute x24, waiting for transfers between devices, onward(): return lax.ppermute(block, 'dp', ring_route(1))  50.1 us
    pallas_call x2, Pallas kernels, attn_backward(): pl.pallas_call(attn_backward_kernel, grid=(images,), in_specs=[rows] * 5...  38.3 us
    ppermute x24, starting transfers between devices, onward(): return lax.ppermute(block, 'dp', ring_route(1))  38.3 us
    pallas_call x2, Pallas kernels, attn_forward(): pl.pallas_call(attn_forward_kernel, grid_spec=pltpu.PrefetchScalarGridSpe...  32.4 us
    unnamed x62, local copies, waits for them, and re-layouts  30.4 us
    pallas_call x2, Pallas kernels, mlp_forward(): pl.pallas_call(mlp_forward_kernel, grid=(parts,), in_specs=[whole, whole,...  30.2 us
    ppermute x24, waiting for transfers between devices, backward(): return lax.ppermute(block, 'dp', ring_route(-1))  29.8 us
    pallas_call x2, Pallas kernels, mlp_backward(): pl.pallas_call(mlp_backward_kernel, grid=(parts,), in_specs=[whole, chunk...  23.5 us
  transfers between devices with their start and end apart: 80, of which 35 were waited for; matrix products, arithmetic and copies ran while one was open for 6% of the time, Pallas kernels for 10%

profile of v2, /device:TPU:0, one launch (start us, length us, event | category | flops | bytes accessed | tf_op | source)
XLA Modules:
  0.0 394.6 jit_solution(12195272875450587822)
XLA Ops:
  1.7 3.1 collective-permute-start.24
  4.8 2.0 collective-permute-start.41
  12.6 2.1 collective-permute-done.18.refs_2_
  16.7 2.1 collective-permute-done.41.refs_16_
  18.9 2.1 collective-permute-done.35.refs_2_
  22.6 3.0 collective-permute-done.7.refs_16_
  25.6 2.2 collective-permute-start.20
  28.5 2.9 collective-permute-done.25.refs_14_
  31.4 1.9 collective-permute-start.37
  35.1 3.1 collective-permute-done.42.refs_14_
  41.6 3.4 collective-permute-done.8.refs_14_
  45.0 2.1 collective-permute-start.9
  52.9 4.1 %collective-permute-done.22.refs_6_ = bf16[192,768]{1,0:T(8,128)(2,1)S(1)} collective-permute-done((bf16[192,768]{1,0:T(8,128)(2,1)S(1)}, bf16[192,768]{1,0:T(8,128)(2,1)S(1)}, u32[]{:S(2)}, u32[]{:S(2)}) %collective-permute-start.22) | collective-permute-done | bytes 294944 | tf_op jit(solution)/shard_map/ppermute | solution.py:47
  57.0 6.8 %collective-permute-done.43.refs_12_ = bf16[192,768]{1,0:T(8,128)(2,1)S(1)} collective-permute-done((bf16[192,768]{1,0:T(8,128)(2,1)S(1)}, bf16[192,768]{1,0:T(8,128)(2,1)S(1)}, u32[]{:S(2)}, u32[]{:S(2)}) %collective-permute-start.43) | collective-permute-done | bytes 294944 | tf_op jit(solution)/shard_map/ppermute | solution.py:43
  64.5 2.7 collective-permute-done.5.refs_6_
  75.7 2.1 collective-permute-done.44.refs_8_
  83.2 2.1 assemble.4.up_ref
  85.3 2.2 copy-done.1
  87.5 2.1 assemble.5.down_ref
  89.5 2.1 copy-done.2
  91.7 2.7 assemble.3.w_ref
  94.4 2.3 copy-done
  97.0 16.5 %attn_forward.2 = (f32[512,768]{1,0:T(8,128)}, bf16[512,768]{1,0:T(8,128)(2,1)S(1)}, bf16[512,768]{1,0:T(8,128)(2,1)}, bf16[512,768]{1,0:T(8,128)(2,1)}, bf16[51...) custom-call(s32[2]{0:T(128)S(1)} %copy-done.18, ...), custom_call_target="tpu_custom_call" | custom-call | flops 2818572288 | bytes 12976128 | tf_op jit(solution)/shard_map/attn_forward/pallas_call | solution.py:236
  114.9 15.0 %mlp_forward.2 = (bf16[512,768]{1,0:T(8,128)(2,1)S(1)}, bf16[512,3072]{1,0:T(8,128)(2,1)}, bf16[512,3072]{1,0:T(8,128)(2,1)}) custom-call(f32[512,768]{1,0:T(8,128)S(1)} %copy-done.23, bf16[512,768]{1,0:T(8,128)(2,1)S(1)} %get-tuple-element.48.second_ref, bf16[16,192,768]{2,1,0:T(8,128)(2,1)} %copy-done.1, bf16[16,192,768]{2,1,0:T(8,128)(2,1)} %copy-done.2, ...), custom_call_target="tpu_custom_call" | custom-call | flops 4831838208 | bytes 18874368 | tf_op jit(solution)/shard_map/mlp_forward/pallas_call | solution.py:301
  129.9 4.0 %collective-permute-start.51 = (bf16[512,768]{1,0:T(8,128)(2,1)S(1)}, bf16[512,768]{1,0:T(8,128)(2,1)S(1)}, u32[]{:S(2)}, u32[]{:S(2)}) collective-permute-start(bf16[512,768]{1,0:T(8,128)(2,1)S(1)} %get-tuple-element.49), channel_id=1, source_target_pairs={{0,16},{1,17},{2,18},{3,19},{4,20},{5,21},{6,22},{7,23},{8,24},{9,... | collective-permute-start | bytes 2359304 | tf_op jit(solution)/shard_map/ppermute | solution.py:678
  133.9 16.8 %collective-permute-done.51 = bf16[512,768]{1,0:T(8,128)(2,1)S(1)} collective-permute-done((bf16[512,768]{1,0:T(8,128)(2,1)S(1)}, bf16[512,768]{1,0:T(8,128)(2,1)S(1)}, u32[]{:S(2)}, u32[]{:S(2)}) %collective-permute-start.51) | collective-permute-done | bytes 786464 | tf_op jit(solution)/shard_map/ppermute | solution.py:678
  150.8 16.0 %attn_forward.3 = (f32[512,768]{1,0:T(8,128)}, bf16[512,768]{1,0:T(8,128)(2,1)S(1)}, bf16[512,768]{1,0:T(8,128)(2,1)S(1)}, bf16[512,768]{1,0:T(8,128)(2,1)S(1)},...) custom-call(s32[2]{0:T(128)S(1)} %copy-done.18, ...), custom_call_target="tpu_custom_call" | custom-call | flops 2818572288 | bytes 12976128 | tf_op jit(solution)/shard_map/attn_forward/pallas_call | solution.py:236
  171.8 15.2 %mlp_forward.3 = (bf16[512,768]{1,0:T(8,128)(2,1)}, bf16[512,3072]{1,0:T(8,128)(2,1)S(1)}, bf16[512,3072]{1,0:T(8,128)(2,1)}) custom-call(f32[512,768]{1,0:T(8,128)S(1)} %copy-done.20, bf16[512,768]{1,0:T(8,128)(2,1)S(1)} %get-tuple-element.51.second_ref, bf16[16,192,768]{2,1,0:T(8,128)(2,1)} %copy-done.1, bf16[16,192,768]{2,1,0:T(8,128)(2,1)} %copy-done.2, ...), custom_call_target="tpu_custom_call" | custom-call | flops 4831838208 | bytes 18874368 | tf_op jit(solution)/shard_map/mlp_forward/pallas_call | solution.py:301
  188.7 11.7 %mlp_backward.2 = (f32[512,768]{1,0:T(8,128)S(1)}, bf16[512,3072]{1,0:T(8,128)(2,1)}, f32[8,768]{1,0:T(8,128)}, f32[4,1,768]{2,1,0:T(1,128)}) custom-call(bf16[512,768]{1,0:T(8,128)(2,1)S(1)} %copy-done.10, bf16[512,3072]{1,0:T(8,128)(2,1)} %get-tuple-element.53.slope_ref, f32[512,768]{1,0:T(8,128)S(1)} %copy-done.20, bf16[16,192,768]{2,1,0:T(8,128)(2,1)} %copy-done.1, ...), custom_call_target="tpu_custom_call" | custom-call | flops 4831838208 | bytes 19660800 | tf_op jit(solution)/shard_map/mlp_backward/pallas_call | solution.py:373
  201.5 19.1 %attn_backward.2 = (f32[512,768]{1,0:T(8,128)}, bf16[512,768]{1,0:T(8,128)(2,1)S(1)}, bf16[512,768]{1,0:T(8,128)(2,1)}, bf16[512,768]{1,0:T(8,128)(2,1)}, bf16[5...) custom-call(f32[512,768]{1,0:T(8,128)} %copy-done.8, ...), custom_call_target="tpu_custom_call" | custom-call | flops 3221225472 | bytes 16908288 | tf_op jit(solution)/shard_map/attn_backward/pallas_call | solution.py:471
  222.1 19.7 %collective-permute-done.52 = bf16[512,768]{1,0:T(8,128)(2,1)S(1)} collective-permute-done((bf16[512,768]{1,0:T(8,128)(2,1)S(1)}, bf16[512,768]{1,0:T(8,128)(2,1)S(1)}, u32[]{:S(2)}, u32[]{:S(2)}) %collective-permute-start.52) | collective-permute-done | bytes 786464 | tf_op jit(solution)/shard_map/ppermute | solution.py:688
  241.9 11.8 %mlp_backward.3 = (f32[512,768]{1,0:T(8,128)S(1)}, bf16[512,3072]{1,0:T(8,128)(2,1)}, f32[8,768]{1,0:T(8,128)S(1)}, f32[4,1,768]{2,1,0:T(1,128)S(1)}) custom-call(bf16[512,768]{1,0:T(8,128)(2,1)S(1)} %broadcast_select_fusion.upstream_ref, bf16[512,3072]{1,0:T(8,128)(2,1)} %get-tuple-element.53.slope_ref, f32[512,768]{1,0:T(8,128)S(1)} %copy-done.21, ...), custom_call_target="tpu_custom_call" | custom-call | flops 4831838208 | bytes 19660800 | tf_op jit(solution)/shard_map/mlp_backward/pallas_call | solution.py:373
  254.9 6.7 %grad_down.1 = (bf16[8,192,768]{2,1,0:T(8,128)(2,1)S(1)}, bf16[8,192,768]{2,1,0:T(8,128)(2,1)}) custom-call(bf16[512,3072]{1,0:T(8,128)(2,1)} %copy-done.22, bf16[512,768]{1,0:T(8,128)(2,1)S(1)} %broadcast_select_fusion.upstream_ref), custom_call_target="tpu_custom_call" | custom-call | flops 2415919104 | bytes 7864320 | tf_op jit(solution)/shard_map/grad_down/pallas_call | solution.py:529
  261.6 7.0 %grad_up.1 = (bf16[8,192,768]{2,1,0:T(8,128)(2,1)S(1)}, bf16[8,192,768]{2,1,0:T(8,128)(2,1)}) custom-call(bf16[512,768]{1,0:T(8,128)(2,1)S(1)} %get-tuple-element.51.second_ref, bf16[512,3072]{1,0:T(8,128)(2,1)} %get-tuple-element.73.pre_ref), custom_call_target="tpu_custom_call" | custom-call | flops 2415919104 | bytes 7864320 | tf_op jit(solution)/shard_map/grad_up/pallas_call | solution.py:566
  270.6 19.1 %attn_backward.3 = (f32[512,768]{1,0:T(8,128)}, bf16[512,768]{1,0:T(8,128)(2,1)}, bf16[512,768]{1,0:T(8,128)(2,1)S(1)}, bf16[512,768]{1,0:T(8,128)(2,1)S(1)}, bf...) custom-call(f32[512,768]{1,0:T(8,128)} %copy-done.7, ...), custom_call_target="tpu_custom_call" | custom-call | flops 3221225472 | bytes 16908288 | tf_op jit(solution)/shard_map/attn_backward/pallas_call | solution.py:471
  298.4 7.4 %grad_first.1 = (bf16[8,208,768]{2,1,0:T(8,128)(2,1)}, bf16[8,208,768]{2,1,0:T(8,128)(2,1)}) custom-call(bf16[512,768]{1,0:T(8,128)(2,1)S(1)} %copy-done.25, bf16[512,768]{1,0:T(8,128)(2,1)S(1)} %copy-done.27, bf16[512,768]{1,0:T(8,128)(2,1)S(1)} %copy-done.13, bf16[512,768]{1,0:T(8,128)(2,1)S(1)} %copy-done.15, bf16[512,768]{1,0:T(8,128)(2,1)S(1)} %copy-done.17, ...), custom_call_target="tpu_custom_call" | custom-call | flops 2415919104 | bytes 9437184 | tf_op jit(solution)/shard_map/grad_first/pallas_call | solution.py:605
  322.0 5.8 %collective-permute-done.54 = bf16[104,768]{1,0:T(8,128)(2,1)S(1)} collective-permute-done((bf16[104,768]{1,0:T(8,128)(2,1)S(1)}, bf16[104,768]{1,0:T(8,128)(2,1)S(1)}, u32[]{:S(2)}, u32[]{:S(2)}) %collective-permute-start.54) | collective-permute-done | bytes 159776 | tf_op jit(solution)/shard_map/ppermute | solution.py:43
  330.1 4.7 %collective-permute-done.64 = bf16[192,768]{1,0:T(8,128)(2,1)S(1)} collective-permute-done((bf16[192,768]{1,0:T(8,128)(2,1)S(1)}, bf16[192,768]{1,0:T(8,128)(2,1)S(1)}, u32[]{:S(2)}, u32[]{:S(2)}) %collective-permute-start.64) | collective-permute-done | bytes 294944 | tf_op jit(solution)/shard_map/ppermute | solution.py:43
  340.2 5.0 %collective-permute-done.55 = bf16[208,768]{1,0:T(8,128)(2,1)S(1)} collective-permute-done((bf16[208,768]{1,0:T(8,128)(2,1)S(1)}, bf16[208,768]{1,0:T(8,128)(2,1)S(1)}, u32[]{:S(2)}, u32[]{:S(2)}) %collective-permute-start.55) | collective-permute-done | bytes 319520 | tf_op jit(solution)/shard_map/ppermute | solution.py:43
  348.7 2.9 collective-permute-done.65
  352.9 1.8 collective-permute-start.69
  354.7 3.2 collective-permute-done.74
  368.1 2.8 collective-permute-done.78
  372.3 5.5 %collective-permute-done.60 = bf16[208,768]{1,0:T(8,128)(2,1)S(1)} collective-permute-done((bf16[208,768]{1,0:T(8,128)(2,1)S(1)}, bf16[208,768]{1,0:T(8,128)(2,1)S(1)}, u32[]{:S(2)}, u32[]{:S(2)}) %collective-permute-start.60) | collective-permute-done | bytes 319520 | tf_op jit(solution)/shard_map/ppermute | solution.py:47
  378.2 1.8 collective-permute-start.61
  380.0 4.1 %collective-permute-done.70 = bf16[192,768]{1,0:T(8,128)(2,1)S(1)} collective-permute-done((bf16[192,768]{1,0:T(8,128)(2,1)S(1)}, bf16[192,768]{1,0:T(8,128)(2,1)S(1)}, u32[]{:S(2)}, u32[]{:S(2)}) %collective-permute-start.70) | collective-permute-done | bytes 294944 | tf_op jit(solution)/shard_map/ppermute | solution.py:47
  385.2 2.8 collective-permute-done.79
  388.1 1.9 fusion.15
  (251 shorter events, 105.5 us)
Async XLA Ops:
  1.7 10.9 %collective-permute-start.24 = (bf16[192,768]{1,0:T(8,128)(2,1)S(1)}, bf16[192,768]{1,0:T(8,128)(2,1)S(1)}, u32[]{:S(2)}, u32[]{:S(2)}) collective-permute-start(bf16[192,768]{1,0:T(8,128)(2,1)S(1)} %pad_maximum_fusion.2.refs_0_), channel_id=1, source_target_pairs={{0,4},{1,5},{4,8},{5,9},{8,12},{9,13},{12,14},{13,15},{14,10},{15,... | collective-permute-start | bytes 884744 | tf_op jit(solution)/shard_map/ppermute | solution.py:43
  4.8 9.9 %collective-permute-start.18 = (bf16[192,768]{1,0:T(8,128)(2,1)S(1)}, bf16[192,768]{1,0:T(8,128)(2,1)S(1)}, u32[]{:S(2)}, u32[]{:S(2)}) collective-permute-start(bf16[192,768]{1,0:T(8,128)(2,1)S(1)} %pad_maximum_fusion.2.refs_0_), channel_id=1, source_target_pairs={{0,2},{1,3},{4,0},{5,1},{8,4},{9,5},{12,8},{13,9},{14,12},{15,13},... | collective-permute-start | bytes 884744 | tf_op jit(solution)/shard_map/ppermute | solution.py:47
  4.8 11.5 %collective-permute-start.17 = (bf16[192,768]{1,0:T(8,128)(2,1)S(1)}, bf16[192,768]{1,0:T(8,128)(2,1)S(1)}, u32[]{:S(2)}, u32[]{:S(2)}) collective-permute-start(bf16[192,768]{1,0:T(8,128)(2,1)S(1)} %pad_maximum_fusion.2.refs_0_), channel_id=1, source_target_pairs={{0,1},{1,0},{2,3},{3,2},{4,5},{5,4},{6,7},{7,6},{8,9},{9,8},{10,11... | collective-permute-start | bytes 884744 | tf_op jit(solution)/shard_map/ppermute | solution.py:51
  4.8 14.1 %collective-permute-start.41 = (bf16[192,768]{1,0:T(8,128)(2,1)}, bf16[192,768]{1,0:T(8,128)(2,1)S(1)}, u32[]{:S(2)}, u32[]{:S(2)}) collective-permute-start(bf16[192,768]{1,0:T(8,128)(2,1)} %bitcast.130), channel_id=1, source_target_pairs={{0,4},{1,5},{4,8},{5,9},{8,12},{9,13},{12,14},{13,15},{14,10},{15,... | collective-permute-start | bytes 884744 | tf_op jit(solution)/shard_map/ppermute | solution.py:43
  6.8 14.2 %collective-permute-start.35 = (bf16[192,768]{1,0:T(8,128)(2,1)}, bf16[192,768]{1,0:T(8,128)(2,1)S(1)}, u32[]{:S(2)}, u32[]{:S(2)}) collective-permute-start(bf16[192,768]{1,0:T(8,128)(2,1)} %bitcast.131), channel_id=1, source_target_pairs={{0,2},{1,3},{4,0},{5,1},{8,4},{9,5},{12,8},{13,9},{14,12},{15,13},... | collective-permute-start | bytes 884744 | tf_op jit(solution)/shard_map/ppermute | solution.py:47
  14.7 10.9 %collective-permute-start.7 = (bf16[208,768]{1,0:T(8,128)(2,1)S(1)}, bf16[208,768]{1,0:T(8,128)(2,1)S(1)}, u32[]{:S(2)}, u32[]{:S(2)}) collective-permute-start(bf16[208,768]{1,0:T(8,128)(2,1)S(1)} %pad_dynamic-update-slice_fusion.refs_0_), channel_id=1, source_target_pairs={{0,4},{1,5},{4,8},{5,9},{8,12},{9,13},{12,14},{13,15},{14,10},{15,... | collective-permute-start | bytes 958472 | tf_op jit(solution)/shard_map/ppermute | solution.py:43
  16.3 11.5 %collective-permute-start.1 = (bf16[208,768]{1,0:T(8,128)(2,1)S(1)}, bf16[208,768]{1,0:T(8,128)(2,1)S(1)}, u32[]{:S(2)}, u32[]{:S(2)}) collective-permute-start(bf16[208,768]{1,0:T(8,128)(2,1)S(1)} %pad_dynamic-update-slice_fusion.refs_0_), channel_id=1, source_target_pairs={{0,2},{1,3},{4,0},{5,1},{8,4},{9,5},{12,8},{13,9},{14,12},{15,13},... | collective-permute-start | bytes 958472 | tf_op jit(solution)/shard_map/ppermute | solution.py:47
  18.9 8.9 %collective-permute-start = (bf16[208,768]{1,0:T(8,128)(2,1)S(1)}, bf16[208,768]{1,0:T(8,128)(2,1)S(1)}, u32[]{:S(2)}, u32[]{:S(2)}) collective-permute-start(bf16[208,768]{1,0:T(8,128)(2,1)S(1)} %pad_dynamic-update-slice_fusion.refs_0_), channel_id=1, source_target_pairs={{0,1},{1,0},{2,3},{3,2},{4,5},{5,4},{6,7},{7,6},{8,9},{9,8},{10,11... | collective-permute-start | bytes 958472 | tf_op jit(solution)/shard_map/ppermute | solution.py:51
  21.0 10.4 %collective-permute-start.25 = (bf16[192,768]{1,0:T(8,128)(2,1)S(1)}, bf16[192,768]{1,0:T(8,128)(2,1)S(1)}, u32[]{:S(2)}, u32[]{:S(2)}) collective-permute-start(bf16[192,768]{1,0:T(8,128)(2,1)S(1)} %collective-permute-done.24.refs_16_), channel_id=1, source_target_pairs={{0,4},{1,5},{4,8},{5,9},{8,12},{9,13},{12,14},{13,15},{14,10},{15,... | collective-permute-start | bytes 884744 | tf_op jit(solution)/shard_map/ppermute | solution.py:43
  28.3 9.9 %collective-permute-start.42 = (bf16[192,768]{1,0:T(8,128)(2,1)S(1)}, bf16[192,768]{1,0:T(8,128)(2,1)S(1)}, u32[]{:S(2)}, u32[]{:S(2)}) collective-permute-start(bf16[192,768]{1,0:T(8,128)(2,1)S(1)} %collective-permute-done.41.refs_16_), channel_id=1, source_target_pairs={{0,4},{1,5},{4,8},{5,9},{8,12},{9,13},{12,14},{13,15},{14,10},{15,... | collective-permute-start | bytes 884744 | tf_op jit(solution)/shard_map/ppermute | solution.py:43
  33.8 11.2 %collective-permute-start.8 = (bf16[208,768]{1,0:T(8,128)(2,1)S(1)}, bf16[208,768]{1,0:T(8,128)(2,1)S(1)}, u32[]{:S(2)}, u32[]{:S(2)}) collective-permute-start(bf16[208,768]{1,0:T(8,128)(2,1)S(1)} %collective-permute-done.7.refs_16_), channel_id=1, source_target_pairs={{0,4},{1,5},{4,8},{5,9},{8,12},{9,13},{12,14},{13,15},{14,10},{15,... | collective-permute-start | bytes 958472 | tf_op jit(solution)/shard_map/ppermute | solution.py:43
  38.2 8.9 %collective-permute-start.3 = (bf16[208,768]{1,0:T(8,128)(2,1)S(1)}, bf16[208,768]{1,0:T(8,128)(2,1)S(1)}, u32[]{:S(2)}, u32[]{:S(2)}) collective-permute-start(bf16[208,768]{1,0:T(8,128)(2,1)S(1)} %collective-permute-done.1.refs_2_), channel_id=1, source_target_pairs={{0,2},{1,3},{4,0},{5,1},{8,4},{9,5},{12,8},{13,9},{14,12},{15,13},... | collective-permute-start | bytes 958472 | tf_op jit(solution)/shard_map/ppermute | solution.py:47
  39.8 9.4 %collective-permute-start.32 = (bf16[192,768]{1,0:T(8,128)(2,1)S(1)}, bf16[192,768]{1,0:T(8,128)(2,1)S(1)}, u32[]{:S(2)}, u32[]{:S(2)}) collective-permute-start(bf16[192,768]{1,0:T(8,128)(2,1)S(1)} %collective-permute-done.25.refs_14_), channel_id=1, source_target_pairs={{0,1},{1,0},{2,3},{3,2},{4,5},{5,4},{6,7},{7,6},{8,9},{9,8},{10,11... | collective-permute-start | bytes 884744 | tf_op jit(solution)/shard_map/ppermute | solution.py:51
  40.3 11.1 %collective-permute-start.26 = (bf16[192,768]{1,0:T(8,128)(2,1)S(1)}, bf16[192,768]{1,0:T(8,128)(2,1)S(1)}, u32[]{:S(2)}, u32[]{:S(2)}) collective-permute-start(bf16[192,768]{1,0:T(8,128)(2,1)S(1)} %collective-permute-done.25.refs_14_), channel_id=1, source_target_pairs={{0,4},{1,5},{4,8},{5,9},{8,12},{9,13},{12,14},{13,15},{14,10},{15,... | collective-permute-start | bytes 884744 | tf_op jit(solution)/shard_map/ppermute | solution.py:43
  45.0 19.4 %collective-permute-start.9 = (bf16[208,768]{1,0:T(8,128)(2,1)S(1)}, bf16[208,768]{1,0:T(8,128)(2,1)S(1)}, u32[]{:S(2)}, u32[]{:S(2)}) collective-permute-start(bf16[208,768]{1,0:T(8,128)(2,1)S(1)} %collective-permute-done.8.refs_14_), channel_id=1, source_target_pairs={{0,4},{1,5},{4,8},{5,9},{8,12},{9,13},{12,14},{13,15},{14,10},{15,... | collective-permute-start | bytes 958472 | tf_op jit(solution)/shard_map/ppermute | solution.py:43
  47.1 9.9 %collective-permute-start.22 = (bf16[192,768]{1,0:T(8,128)(2,1)S(1)}, bf16[192,768]{1,0:T(8,128)(2,1)S(1)}, u32[]{:S(2)}, u32[]{:S(2)}) collective-permute-start(bf16[192,768]{1,0:T(8,128)(2,1)S(1)} %collective-permute-done.20.refs_4_), channel_id=1, source_target_pairs={{0,2},{1,3},{4,0},{5,1},{8,4},{9,5},{12,8},{13,9},{14,12},{15,13},... | collective-permute-start | bytes 884744 | tf_op jit(solution)/shard_map/ppermute | solution.py:47
  48.3 15.5 %collective-permute-start.43 = (bf16[192,768]{1,0:T(8,128)(2,1)S(1)}, bf16[192,768]{1,0:T(8,128)(2,1)S(1)}, u32[]{:S(2)}, u32[]{:S(2)}) collective-permute-start(bf16[192,768]{1,0:T(8,128)(2,1)S(1)} %collective-permute-done.42.refs_14_), channel_id=1, source_target_pairs={{0,4},{1,5},{4,8},{5,9},{8,12},{9,13},{12,14},{13,15},{14,10},{15,... | collective-permute-start | bytes 884744 | tf_op jit(solution)/shard_map/ppermute | solution.py:43
  49.1 14.8 %collective-permute-start.39 = (bf16[192,768]{1,0:T(8,128)(2,1)S(1)}, bf16[192,768]{1,0:T(8,128)(2,1)S(1)}, u32[]{:S(2)}, u32[]{:S(2)}) collective-permute-start(bf16[192,768]{1,0:T(8,128)(2,1)S(1)} %collective-permute-done.37.refs_4_), channel_id=1, source_target_pairs={{0,2},{1,3},{4,0},{5,1},{8,4},{9,5},{12,8},{13,9},{14,12},{15,13},... | collective-permute-start | bytes 884744 | tf_op jit(solution)/shard_map/ppermute | solution.py:47
  51.3 15.8 %collective-permute-start.5 = (bf16[208,768]{1,0:T(8,128)(2,1)S(1)}, bf16[208,768]{1,0:T(8,128)(2,1)S(1)}, u32[]{:S(2)}, u32[]{:S(2)}) collective-permute-start(bf16[208,768]{1,0:T(8,128)(2,1)S(1)} %collective-permute-done.3.refs_4_), channel_id=1, source_target_pairs={{0,2},{1,3},{4,0},{5,1},{8,4},{9,5},{12,8},{13,9},{14,12},{15,13},... | collective-permute-start | bytes 958472 | tf_op jit(solution)/shard_map/ppermute | solution.py:47
  57.0 14.4 %collective-permute-start.15 = (bf16[208,768]{1,0:T(8,128)(2,1)S(1)}, bf16[208,768]{1,0:T(8,128)(2,1)S(1)}, u32[]{:S(2)}, u32[]{:S(2)}) collective-permute-start(bf16[208,768]{1,0:T(8,128)(2,1)S(1)} %collective-permute-done.8.refs_14_), channel_id=1, source_target_pairs={{0,1},{1,0},{2,3},{3,2},{4,5},{5,4},{6,7},{7,6},{8,9},{9,8},{10,11... | collective-permute-start | bytes 958472 | tf_op jit(solution)/shard_map/ppermute | solution.py:51
  69.4 9.9 %collective-permute-start.10 = (bf16[104,768]{1,0:T(8,128)(2,1)S(1)}, bf16[104,768]{1,0:T(8,128)(2,1)S(1)}, u32[]{:S(2)}, u32[]{:S(2)}) collective-permute-start(bf16[104,768]{1,0:T(8,128)(2,1)S(1)} %slice.432), channel_id=1, source_target_pairs={{0,4},{1,5},{4,8},{5,9},{8,12},{9,13},{12,14},{13,15},{14,10},{15,... | collective-permute-start | bytes 479240 | tf_op jit(solution)/shard_map/ppermute | solution.py:43
  71.0 8.8 %collective-permute-start.11 = (bf16[104,768]{1,0:T(8,128)(2,1)S(1)}, bf16[104,768]{1,0:T(8,128)(2,1)S(1)}, u32[]{:S(2)}, u32[]{:S(2)}) collective-permute-start(bf16[104,768]{1,0:T(8,128)(2,1)S(1)} %slice.433), channel_id=1, source_target_pairs={{0,2},{1,3},{4,0},{5,1},{8,4},{9,5},{12,8},{13,9},{14,12},{15,13},... | collective-permute-start | bytes 479240 | tf_op jit(solution)/shard_map/ppermute | solution.py:47
  81.6 10.1 %collective-permute-start.4 = (bf16[208,768]{1,0:T(8,128)(2,1)S(1)}, bf16[208,768]{1,0:T(8,128)(2,1)S(1)}, u32[]{:S(2)}, u32[]{:S(2)}) collective-permute-start(bf16[208,768]{1,0:T(8,128)(2,1)S(1)} %collective-permute-done.3.refs_4_), channel_id=1, source_target_pairs={{0,1},{1,0},{2,3},{3,2},{4,5},{5,4},{6,7},{7,6},{8,9},{9,8},{10,11... | collective-permute-start | bytes 958472 | tf_op jit(solution)/shard_map/ppermute | solution.py:51
  81.8 9.9 %collective-permute-start.14 = (bf16[208,768]{1,0:T(8,128)(2,1)S(1)}, bf16[208,768]{1,0:T(8,128)(2,1)S(1)}, u32[]{:S(2)}, u32[]{:S(2)}) collective-permute-start(bf16[208,768]{1,0:T(8,128)(2,1)S(1)} %collective-permute-done.9.refs_12_), channel_id=1, source_target_pairs={{0,1},{1,0},{2,3},{3,2},{4,5},{5,4},{6,7},{7,6},{8,9},{9,8},{10,11... | collective-permute-start | bytes 958472 | tf_op jit(solution)/shard_map/ppermute | solution.py:51
  82.1 9.6 %collective-permute-start.6 = (bf16[208,768]{1,0:T(8,128)(2,1)S(1)}, bf16[208,768]{1,0:T(8,128)(2,1)S(1)}, u32[]{:S(2)}, u32[]{:S(2)}) collective-permute-start(bf16[208,768]{1,0:T(8,128)(2,1)S(1)} %collective-permute-done.5.refs_6_), channel_id=1, source_target_pairs={{0,1},{1,0},{2,3},{3,2},{4,5},{5,4},{6,7},{7,6},{8,9},{9,8},{10,11... | collective-permute-start | bytes 958472 | tf_op jit(solution)/shard_map/ppermute | solution.py:51
  82.6 9.0 %collective-permute-start.12 = (bf16[104,768]{1,0:T(8,128)(2,1)S(1)}, bf16[104,768]{1,0:T(8,128)(2,1)S(1)}, u32[]{:S(2)}, u32[]{:S(2)}) collective-permute-start(bf16[104,768]{1,0:T(8,128)(2,1)S(1)} %collective-permute-done.10.refs_8_), channel_id=1, source_target_pairs={{0,1},{1,0},{2,3},{3,2},{4,5},{5,4},{6,7},{7,6},{8,9},{9,8},{10,11... | collective-permute-start | bytes 479240 | tf_op jit(solution)/shard_map/ppermute | solution.py:51
  129.9 20.8 %collective-permute-start.51 = (bf16[512,768]{1,0:T(8,128)(2,1)S(1)}, bf16[512,768]{1,0:T(8,128)(2,1)S(1)}, u32[]{:S(2)}, u32[]{:S(2)}) collective-permute-start(bf16[512,768]{1,0:T(8,128)(2,1)S(1)} %get-tuple-element.49), channel_id=1, source_target_pairs={{0,16},{1,17},{2,18},{3,19},{4,20},{5,21},{6,22},{7,23},{8,24},{9,... | collective-permute-start | bytes 2359304 | tf_op jit(solution)/shard_map/ppermute | solution.py:678
  220.7 21.1 %collective-permute-start.52 = (bf16[512,768]{1,0:T(8,128)(2,1)S(1)}, bf16[512,768]{1,0:T(8,128)(2,1)S(1)}, u32[]{:S(2)}, u32[]{:S(2)}) collective-permute-start(bf16[512,768]{1,0:T(8,128)(2,1)S(1)} %get-tuple-element.59), channel_id=1, source_target_pairs={{16,0},{17,1},{18,2},{19,3},{20,4},{21,5},{22,6},{23,7},{24,8},{25... | collective-permute-start | bytes 2359304 | tf_op jit(solution)/shard_map/ppermute | solution.py:688
  261.6 44.2 %collective-permute-start.71 = (bf16[8,192,768]{2,1,0:T(8,128)(2,1)}, bf16[8,192,768]{2,1,0:T(8,128)(2,1)}, u32[]{:S(2)}, u32[]{:S(2)}) collective-permute-start(bf16[8,192,768]{2,1,0:T(8,128)(2,1)} %get-tuple-element.78), channel_id=1, source_target_pairs={{0,1},{1,0},{2,3},{3,2},{4,5},{5,4},{6,7},{7,6},{8,9},{9,8},{10,11... | collective-permute-start | bytes 7077896 | tf_op jit(solution)/shard_map/ppermute | solution.py:51
  270.1 39.1 %collective-permute-start.62 = (bf16[8,192,768]{2,1,0:T(8,128)(2,1)}, bf16[8,192,768]{2,1,0:T(8,128)(2,1)}, u32[]{:S(2)}, u32[]{:S(2)}) collective-permute-start(bf16[8,192,768]{2,1,0:T(8,128)(2,1)} %get-tuple-element.75), channel_id=1, source_target_pairs={{0,1},{1,0},{2,3},{3,2},{4,5},{5,4},{6,7},{7,6},{8,9},{9,8},{10,11... | collective-permute-start | bytes 7077896 | tf_op jit(solution)/shard_map/ppermute | solution.py:51
  305.8 13.3 %collective-permute-start.53 = (bf16[8,208,768]{2,1,0:T(8,128)(2,1)}, bf16[8,208,768]{2,1,0:T(8,128)(2,1)S(1)}, u32[]{:S(2)}, u32[]{:S(2)}) collective-permute-start(bf16[8,208,768]{2,1,0:T(8,128)(2,1)} %get-tuple-element.72), channel_id=1, source_target_pairs={{0,1},{1,0},{2,3},{3,2},{4,5},{5,4},{6,7},{7,6},{8,9},{9,8},{10,11... | collective-permute-start | bytes 7667720 | tf_op jit(solution)/shard_map/ppermute | solution.py:51
  315.9 38.8 %collective-permute-start.77 = (bf16[192,768]{1,0:T(8,128)(2,1)S(1)}, bf16[192,768]{1,0:T(8,128)(2,1)S(1)}, u32[]{:S(2)}, u32[]{:S(2)}) collective-permute-start(bf16[192,768]{1,0:T(8,128)(2,1)S(1)} %pad_maximum_fusion.6), channel_id=1, source_target_pairs={{0,2},{1,3},{4,0},{5,1},{8,4},{9,5},{12,8},{13,9},{14,12},{15,13},... | collective-permute-start | bytes 884744 | tf_op jit(solution)/shard_map/ppermute | solution.py:47
  316.5 21.1 %collective-permute-start.73 = (bf16[192,768]{1,0:T(8,128)(2,1)S(1)}, bf16[192,768]{1,0:T(8,128)(2,1)S(1)}, u32[]{:S(2)}, u32[]{:S(2)}) collective-permute-start(bf16[192,768]{1,0:T(8,128)(2,1)S(1)} %pad_maximum_fusion.5), channel_id=1, source_target_pairs={{0,4},{1,5},{4,8},{5,9},{8,12},{9,13},{12,14},{13,15},{14,10},{15,... | collective-permute-start | bytes 884744 | tf_op jit(solution)/shard_map/ppermute | solution.py:43
  321.4 25.7 %collective-permute-start.68 = (bf16[192,768]{1,0:T(8,128)(2,1)S(1)}, bf16[192,768]{1,0:T(8,128)(2,1)S(1)}, u32[]{:S(2)}, u32[]{:S(2)}) collective-permute-start(bf16[192,768]{1,0:T(8,128)(2,1)S(1)} %pad_maximum_fusion.4), channel_id=1, source_target_pairs={{0,2},{1,3},{4,0},{5,1},{8,4},{9,5},{12,8},{13,9},{14,12},{15,13},... | collective-permute-start | bytes 884744 | tf_op jit(solution)/shard_map/ppermute | solution.py:47
  329.5 31.8 %collective-permute-start.59 = (bf16[208,768]{1,0:T(8,128)(2,1)S(1)}, bf16[208,768]{1,0:T(8,128)(2,1)S(1)}, u32[]{:S(2)}, u32[]{:S(2)}) collective-permute-start(bf16[208,768]{1,0:T(8,128)(2,1)S(1)} %pad_maximum_fusion.1), channel_id=1, source_target_pairs={{0,2},{1,3},{4,0},{5,1},{8,4},{9,5},{12,8},{13,9},{14,12},{15,13},... | collective-permute-start | bytes 958472 | tf_op jit(solution)/shard_map/ppermute | solution.py:47
  334.8 10.5 %collective-permute-start.55 = (bf16[208,768]{1,0:T(8,128)(2,1)S(1)}, bf16[208,768]{1,0:T(8,128)(2,1)S(1)}, u32[]{:S(2)}, u32[]{:S(2)}) collective-permute-start(bf16[208,768]{1,0:T(8,128)(2,1)S(1)} %pad_maximum_fusion), channel_id=1, source_target_pairs={{0,4},{1,5},{4,8},{5,9},{8,12},{9,13},{12,14},{13,15},{14,10},{15,... | collective-permute-start | bytes 958472 | tf_op jit(solution)/shard_map/ppermute | solution.py:43
  337.6 14.0 %collective-permute-start.65 = (bf16[192,768]{1,0:T(8,128)(2,1)S(1)}, bf16[192,768]{1,0:T(8,128)(2,1)S(1)}, u32[]{:S(2)}, u32[]{:S(2)}) collective-permute-start(bf16[192,768]{1,0:T(8,128)(2,1)S(1)} %fusion.18), channel_id=1, source_target_pairs={{0,4},{1,5},{4,8},{5,9},{8,12},{9,13},{12,14},{13,15},{14,10},{15,... | collective-permute-start | bytes 884744 | tf_op jit(solution)/shard_map/ppermute | solution.py:43
  345.2 12.6 %collective-permute-start.74 = (bf16[192,768]{1,0:T(8,128)(2,1)S(1)}, bf16[192,768]{1,0:T(8,128)(2,1)S(1)}, u32[]{:S(2)}, u32[]{:S(2)}) collective-permute-start(bf16[192,768]{1,0:T(8,128)(2,1)S(1)} %fusion.12), channel_id=1, source_target_pairs={{0,4},{1,5},{4,8},{5,9},{8,12},{9,13},{12,14},{13,15},{14,10},{15,... | collective-permute-start | bytes 884744 | tf_op jit(solution)/shard_map/ppermute | solution.py:43
  347.1 17.6 %collective-permute-start.56 = (bf16[208,768]{1,0:T(8,128)(2,1)S(1)}, bf16[208,768]{1,0:T(8,128)(2,1)S(1)}, u32[]{:S(2)}, u32[]{:S(2)}) collective-permute-start(bf16[208,768]{1,0:T(8,128)(2,1)S(1)} %fusion.5), channel_id=1, source_target_pairs={{0,4},{1,5},{4,8},{5,9},{8,12},{9,13},{12,14},{13,15},{14,10},{15,... | collective-permute-start | bytes 958472 | tf_op jit(solution)/shard_map/ppermute | solution.py:43
  352.9 13.9 %collective-permute-start.69 = (bf16[192,768]{1,0:T(8,128)(2,1)S(1)}, bf16[192,768]{1,0:T(8,128)(2,1)S(1)}, u32[]{:S(2)}, u32[]{:S(2)}) collective-permute-start(bf16[192,768]{1,0:T(8,128)(2,1)S(1)} %get-tuple-element.96), channel_id=1, source_target_pairs={{0,2},{1,3},{4,0},{5,1},{8,4},{9,5},{12,8},{13,9},{14,12},{15,13},... | collective-permute-start | bytes 884744 | tf_op jit(solution)/shard_map/ppermute | solution.py:47
  359.2 26.1 %collective-permute-start.75 = (bf16[192,768]{1,0:T(8,128)(2,1)S(1)}, bf16[192,768]{1,0:T(8,128)(2,1)S(1)}, u32[]{:S(2)}, u32[]{:S(2)}) collective-permute-start(bf16[192,768]{1,0:T(8,128)(2,1)S(1)} %get-tuple-element.87), channel_id=1, source_target_pairs={{0,4},{1,5},{4,8},{5,9},{8,12},{9,13},{12,14},{13,15},{14,10},{15,... | collective-permute-start | bytes 884744 | tf_op jit(solution)/shard_map/ppermute | solution.py:43
  361.0 10.0 %collective-permute-start.78 = (bf16[192,768]{1,0:T(8,128)(2,1)S(1)}, bf16[192,768]{1,0:T(8,128)(2,1)S(1)}, u32[]{:S(2)}, u32[]{:S(2)}) collective-permute-start(bf16[192,768]{1,0:T(8,128)(2,1)S(1)} %get-tuple-element.88), channel_id=1, source_target_pairs={{0,2},{1,3},{4,0},{5,1},{8,4},{9,5},{12,8},{13,9},{14,12},{15,13},... | collective-permute-start | bytes 884744 | tf_op jit(solution)/shard_map/ppermute | solution.py:47
  361.3 16.9 %collective-permute-start.66 = (bf16[192,768]{1,0:T(8,128)(2,1)S(1)}, bf16[192,768]{1,0:T(8,128)(2,1)S(1)}, u32[]{:S(2)}, u32[]{:S(2)}) collective-permute-start(bf16[192,768]{1,0:T(8,128)(2,1)S(1)} %get-tuple-element.95), channel_id=1, source_target_pairs={{0,4},{1,5},{4,8},{5,9},{8,12},{9,13},{12,14},{13,15},{14,10},{15,... | collective-permute-start | bytes 884744 | tf_op jit(solution)/shard_map/ppermute | solution.py:43
  365.0 25.9 %collective-permute-start.57 = (bf16[208,768]{1,0:T(8,128)(2,1)S(1)}, bf16[208,768]{1,0:T(8,128)(2,1)S(1)}, u32[]{:S(2)}, u32[]{:S(2)}) collective-permute-start(bf16[208,768]{1,0:T(8,128)(2,1)S(1)} %get-tuple-element.79), channel_id=1, source_target_pairs={{0,4},{1,5},{4,8},{5,9},{8,12},{9,13},{12,14},{13,15},{14,10},{15,... | collective-permute-start | bytes 958472 | tf_op jit(solution)/shard_map/ppermute | solution.py:43
  366.8 11.0 %collective-permute-start.60 = (bf16[208,768]{1,0:T(8,128)(2,1)S(1)}, bf16[208,768]{1,0:T(8,128)(2,1)S(1)}, u32[]{:S(2)}, u32[]{:S(2)}) collective-permute-start(bf16[208,768]{1,0:T(8,128)(2,1)S(1)} %get-tuple-element.80), channel_id=1, source_target_pairs={{0,2},{1,3},{4,0},{5,1},{8,4},{9,5},{12,8},{13,9},{14,12},{15,13},... | collective-permute-start | bytes 958472 | tf_op jit(solution)/shard_map/ppermute | solution.py:47
  370.9 13.2 %collective-permute-start.70 = (bf16[192,768]{1,0:T(8,128)(2,1)S(1)}, bf16[192,768]{1,0:T(8,128)(2,1)S(1)}, u32[]{:S(2)}, u32[]{:S(2)}) collective-permute-start(bf16[192,768]{1,0:T(8,128)(2,1)S(1)} %fusion.17), channel_id=1, source_target_pairs={{0,2},{1,3},{4,0},{5,1},{8,4},{9,5},{12,8},{13,9},{14,12},{15,13},... | collective-permute-start | bytes 884744 | tf_op jit(solution)/shard_map/ppermute | solution.py:47
  377.8 10.3 %collective-permute-start.79 = (bf16[192,768]{1,0:T(8,128)(2,1)S(1)}, bf16[192,768]{1,0:T(8,128)(2,1)S(1)}, u32[]{:S(2)}, u32[]{:S(2)}) collective-permute-start(bf16[192,768]{1,0:T(8,128)(2,1)S(1)} %fusion.11), channel_id=1, source_target_pairs={{0,2},{1,3},{4,0},{5,1},{8,4},{9,5},{12,8},{13,9},{14,12},{15,13},... | collective-permute-start | bytes 884744 | tf_op jit(solution)/shard_map/ppermute | solution.py:47
  378.2 13.3 %collective-permute-start.61 = (bf16[208,768]{1,0:T(8,128)(2,1)S(1)}, bf16[208,768]{1,0:T(8,128)(2,1)S(1)}, u32[]{:S(2)}, u32[]{:S(2)}) collective-permute-start(bf16[208,768]{1,0:T(8,128)(2,1)S(1)} %fusion.4), channel_id=1, source_target_pairs={{0,2},{1,3},{4,0},{5,1},{8,4},{9,5},{12,8},{13,9},{14,12},{15,13},... | collective-permute-start | bytes 958472 | tf_op jit(solution)/shard_map/ppermute | solution.py:47
  (61 other events, 305.8 us)

commit v3 on v2

v3 whole, which is shorter than its diff:
```python
import functools

import jax
import jax.numpy as jnp
from jax import lax
from jax.experimental import pallas as pl
from jax.experimental.pallas import tpu as pltpu
from jax.sharding import PartitionSpec as P

H = 16
GRID = 16
LEAD = 16
RING = 8
VEC_ROWS = 16

f32 = jnp.float32
bf16 = jnp.bfloat16
eps_norm = 1e-05


def chip_at(place):
    if isinstance(place, int):
        return 2 * place if place < 4 else 2 * (7 - place) + 1
    return jnp.where(place < 4, 2 * place, 2 * (7 - place) + 1)


def place_of(chip):
    if isinstance(chip, int):
        return chip // 2 if chip % 2 == 0 else 7 - chip // 2
    return jnp.where(chip % 2 == 0, chip // 2, 7 - chip // 2)


def ring_route(step):
    return [
        (2 * chip_at(place) + core, 2 * chip_at((place + step) % RING) + core)
        for place in range(RING)
        for core in range(2)
    ]


CORE_ROUTE = [(index, index ^ 1) for index in range(2 * RING)]


def onward(block):
    return lax.ppermute(block, "dp", ring_route(1))


def backward(block):
    return lax.ppermute(block, "dp", ring_route(-1))


def across(block):
    return lax.ppermute(block, "dp", CORE_ROUTE)


def tie(*values):
    leaves, tree = jax.tree.flatten(values)
    arrays = iter(lax.optimization_barrier([leaf for leaf in leaves if isinstance(leaf, jax.Array)]))
    held = jax.tree.unflatten(tree, [next(arrays) if isinstance(leaf, jax.Array) else leaf for leaf in leaves])
    return held if len(held) > 1 else held[0]


def pack_first(qkv, out, vectors, ups):
    rows, width = out.shape
    chunks = qkv.shape[1] // width
    names, size = vectors.shape[0], ups.shape[1]

    def kernel(qkv_ref, out_ref, vec_ref, up_ref, packed_ref):
        me = lax.axis_index("dp")
        for chunk in range(chunks):
            packed_ref[chunk * rows : (chunk + 1) * rows, :] = qkv_ref[:, chunk * width : (chunk + 1) * width]
        packed_ref[chunks * rows : (chunks + 1) * rows, :] = out_ref[...]
        lane = lax.broadcasted_iota(jnp.int32, (names, width), 1)
        spread = jnp.concatenate([vec_ref[...].astype(f32)] * (width // rows), axis=1)
        small = jnp.where((lane >= me * rows) & (lane < (me + 1) * rows), spread, 0.0)
        lane = lax.broadcasted_iota(jnp.int32, (VEC_ROWS - names, width), 1)
        row = lax.broadcasted_iota(jnp.int32, (VEC_ROWS - names, width), 0)
        spread = jnp.concatenate([up_ref[...].astype(f32)] * (width // size), axis=1)
        at = row * width + lane
        last = jnp.where((at >= me * size) & (at < (me + 1) * size), spread, 0.0)
        packed_ref[(chunks + 1) * rows :, :] = jnp.concatenate([small, last], axis=0).astype(bf16)

    return pl.pallas_call(
        kernel,
        out_shape=jax.ShapeDtypeStruct(((chunks + 1) * rows + VEC_ROWS, width), bf16),
        compiler_params=pltpu.CompilerParams(vmem_limit_bytes=2 * 2**20),
        name="pack_first",
    )(qkv, out, vectors, ups)


def pack_second(up, down):
    rows, width = up.shape[0], down.shape[1]
    chunks = up.shape[1] // width

    def kernel(up_ref, down_ref, packed_ref):
        for chunk in range(chunks):
            packed_ref[chunk * rows : (chunk + 1) * rows, :] = up_ref[:, chunk * width : (chunk + 1) * width]
        packed_ref[chunks * rows :, :] = down_ref[...]

    return pl.pallas_call(
        kernel,
        out_shape=jax.ShapeDtypeStruct((chunks * rows + down.shape[0], width), bf16),
        compiler_params=pltpu.CompilerParams(vmem_limit_bytes=2 * 2**20),
        name="pack_second",
    )(up, down)


def half_of(rows):
    return rows // 32 * 16


def gather_start(shard):
    return {"step": 0, "here": {0: shard}, "peer": {}, "up": shard, "down": shard}


def gather_step(state):
    step = state["step"] + 1
    up, down = state["up"], state["down"]
    here, peer = dict(state["here"]), dict(state["peer"])
    if step < RING // 2:
        up, down = onward(up), backward(down)
    else:
        half = half_of(up.shape[0])
        up, down = onward(up[:half]), backward(down[half:])
    for place in here:
        if place not in peer:
            peer[place] = across(here[place])
    if step < RING // 2:
        here[RING - step], here[step] = up, down
    return {"step": step, "here": here, "peer": peer, "up": up, "down": down}


def gather_blocks(state):
    here, peer = state["here"], state["peer"]
    far = [state["up"], state["down"]]
    blocks = []
    for place in range(RING):
        if place == RING // 2:
            blocks += far + [across(block) for block in far]
        else:
            blocks += [here[place], peer[place]]
    return blocks


def assemble(blocks, vectors=False):
    rows, width = blocks[0].shape
    half = half_of(rows)
    count = len(blocks)

    def kernel(*refs):
        blocks_in, out, sems = refs[:count], refs[count], refs[-1]
        me = lax.axis_index("dp")
        core, place = lax.rem(me, 2), place_of(lax.div(me, 2))
        copies = []
        at = 0
        for step in range(RING):
            chip = chip_at(lax.rem(place + step, RING))
            parts = ((0, half), (half, rows - half)) if step == RING // 2 else ((0, rows),)
            for owner in (2 * chip + core, 2 * chip + 1 - core):
                for start, size in parts:
                    copies.append(
                        pltpu.make_async_copy(
                            blocks_in[at], out.at[owner, pl.ds(start, size)], sems.at[at]
                        )
                    )
                    at += 1
        for copy in copies:
            copy.start()
        for copy in copies:
            copy.wait()
        if vectors:
            total = jnp.zeros((VEC_ROWS, width), f32)
            for owner in range(2 * RING):
                total += out[owner, rows - VEC_ROWS :, :].astype(f32)
            refs[count + 1][...] = total

    shapes = [jax.ShapeDtypeStruct((2 * RING, rows, width), blocks[0].dtype)]
    if vectors:
        shapes.append(jax.ShapeDtypeStruct((VEC_ROWS, width), f32))
    outs = pl.pallas_call(
        kernel,
        out_shape=shapes,
        in_specs=[pl.BlockSpec(memory_space=pl.ANY)] * count,
        out_specs=[pl.BlockSpec(memory_space=pltpu.VMEM)] * len(shapes),
        scratch_shapes=[pltpu.SemaphoreType.DMA((count,))],
        compiler_params=pltpu.CompilerParams(vmem_limit_bytes=2**20),
        name="assemble",
    )(*blocks)
    return outs if vectors else outs[0]


def scatter_start(own, peer):
    return {"step": 0, "own": own, "peer": peer}


def hop_kernel(step, half, *refs):
    own_up, peer_up, own_down, peer_down = refs[:4]
    up_out, down_out = refs[-2:]
    top, bottom = slice(0, half), slice(half, None)
    local_up = lambda rows: own_up[0, rows, :].astype(f32) + peer_up[0, rows, :].astype(f32)
    local_down = lambda rows: own_down[0, rows, :].astype(f32) + peer_down[0, rows, :].astype(f32)
    if step == 1:
        up_out[...] = local_up(top).astype(bf16)
        down_out[...] = local_down(bottom).astype(bf16)
        return
    up_in, down_in = refs[4], refs[5]
    if step == 2:
        up_out[top, :] = (local_up(top) + up_in[...].astype(f32)).astype(bf16)
        up_out[bottom, :] = local_up(bottom).astype(bf16)
        down_out[top, :] = local_down(top).astype(bf16)
        down_out[bottom, :] = (local_down(bottom) + down_in[...].astype(f32)).astype(bf16)
        return
    up_out[...] = (local_up(slice(None)) + up_in[...].astype(f32)).astype(bf16)
    down_out[...] = (local_down(slice(None)) + down_in[...].astype(f32)).astype(bf16)


def scatter_step(state, held=()):
    step = state["step"]
    own, peer = state["own"], state["peer"]
    if step == 0:
        peer, held = tie(peer, held)
        return {"step": 1, "own": own, "peer": across(peer)}, held
    rows, width = own.shape[1:]
    half, far = half_of(rows), RING // 2
    at = lambda place: pl.BlockSpec((1, rows, width), lambda i: (place, 0, 0))
    whole = lambda size: pl.BlockSpec((size, width), lambda i: (0, 0))
    up_place, down_place = far + 1 - step, far - 1 + step
    before = [] if step == 1 else [state["up"], state["down"]]
    sizes = (half, rows - half) if step == 1 else (rows, rows)
    up, down = pl.pallas_call(
        functools.partial(hop_kernel, step, half),
        grid=(1,),
        in_specs=[at(up_place), at(up_place), at(down_place), at(down_place)] + [whole(b.shape[0]) for b in before],
        out_specs=[whole(size) for size in sizes],
        out_shape=[jax.ShapeDtypeStruct((size, width), bf16) for size in sizes],
        compiler_params=pltpu.CompilerParams(vmem_limit_bytes=8 * 2**20),
        name="hop",
    )(own, peer, own, peer, *before)
    up, down, held = tie(up, down, held)
    return {"step": step + 1, "own": own, "peer": peer, "up": onward(up), "down": backward(down)}, held


def scatter_sum(state, cuts):
    own, peer = state["own"], state["peer"]
    rows, width = own.shape[1:]
    shapes = [jax.ShapeDtypeStruct((count, chunks * width), f32) for _, count, chunks in cuts]

    def kernel(own_ref, peer_ref, up_ref, down_ref, *outs):
        for (first, count, chunks), out in zip(cuts, outs):
            for chunk in range(chunks):
                here = slice(first + chunk * count, first + (chunk + 1) * count)
                both = own_ref[0, here, :].astype(f32) + peer_ref[0, here, :].astype(f32)
                sent = up_ref[here, :].astype(f32) + down_ref[here, :].astype(f32)
                out[:, chunk * width : (chunk + 1) * width] = both + sent

    at = pl.BlockSpec((1, rows, width), lambda i: (0, 0, 0))
    whole = pl.BlockSpec((rows, width), lambda i: (0, 0))
    return pl.pallas_call(
        kernel,
        grid=(1,),
        in_specs=[at, at, whole, whole],
        out_specs=[pl.BlockSpec(shape.shape, lambda i: (0, 0)) for shape in shapes],
        out_shape=shapes,
        compiler_params=pltpu.CompilerParams(vmem_limit_bytes=12 * 2**20),
        name="scatter_sum",
    )(own, peer, state["up"], state["down"])


VMEM_LIMIT = 24 * 2**20
MLP_CHUNK = 32
ATTN_COST, MLP_COST = 24, 6
Q_BIAS, V_BIAS, OUT_BIAS, DOWN_BIAS, GAIN_ONE, SHIFT_ONE, GAIN_TWO, SHIFT_TWO, UP_BIAS = range(9)
NT = (((1,), (1,)), ((), ()))
TN = (((0,), (0,)), ((), ()))


def dot(first_mat, second_mat):
    return jnp.dot(first_mat, second_mat, preferred_element_type=f32)


def dot_nt(first_mat, second_mat):
    return lax.dot_general(first_mat, second_mat, NT, preferred_element_type=f32)


def dot_tn(first_mat, second_mat):
    return lax.dot_general(first_mat, second_mat, TN, preferred_element_type=f32)


def weight_part(w_ref, part):
    width = w_ref.shape[2]
    rows = width // LEAD
    return w_ref[:, part * rows : (part + 1) * rows, :].reshape(width, width)


def norm_parts(rows_in):
    average = jnp.mean(rows_in, axis=-1, keepdims=True)
    centred = rows_in - average
    inverse = lax.rsqrt(jnp.mean(centred * centred, axis=-1, keepdims=True) + eps_norm)
    return centred * inverse, inverse


def norm_back(rows_in, gain_row, grad_rows):
    unit, inverse = norm_parts(rows_in)
    scaled = grad_rows * gain_row
    mean_one = jnp.mean(scaled, axis=-1, keepdims=True)
    mean_two = jnp.mean(scaled * unit, axis=-1, keepdims=True)
    return (scaled - mean_one - unit * mean_two) * inverse, grad_rows * unit


def head_window(head, head_size, width):
    start = min(head * head_size // 128 * 128, width - 256)
    return start, head * head_size - start


def only_head(block, low, head_size):
    lane = lax.broadcasted_iota(jnp.int32, block.shape, 1)
    return jnp.where((lane >= low) & (lane < low + head_size), block, jnp.zeros_like(block))


def column_sum(rows_in):
    return jnp.sum(rows_in, axis=0, keepdims=True)


def attn_forward_kernel(
    image, heights_ref, widths_ref, x_ref, w_ref, vec_ref,
    middle_ref, second_ref, normed_ref, q_ref, k_ref, v_ref, probs_ref, attended_ref,
    vt_ref, at_ref,
):
    slots, width = x_ref.shape
    head_size = width // H
    step = 64
    for at in range(0, slots, step):
        unit, _ = norm_parts(x_ref[at : at + step, :].astype(f32))
        normed_ref[at : at + step, :] = (
            unit * vec_ref[GAIN_ONE : GAIN_ONE + 1, :] + vec_ref[SHIFT_ONE : SHIFT_ONE + 1, :]
        ).astype(bf16)
    normed = normed_ref[...]
    q_ref[...] = (dot(normed, weight_part(w_ref, 0)) + vec_ref[Q_BIAS : Q_BIAS + 1, :]).astype(bf16)
    k_ref[...] = dot(normed, weight_part(w_ref, 1)).astype(bf16)
    values = dot(normed, weight_part(w_ref, 2)) + vec_ref[V_BIAS : V_BIAS + 1, :]
    v_ref[...] = values.astype(bf16)
    vt_ref[...] = values.astype(bf16).T
    slot = lax.broadcasted_iota(jnp.int32, (slots, 128), 0)
    valid = (slot // GRID < heights_ref[image]) & (slot % GRID < widths_ref[image])
    mask = jnp.where(valid, 0.0, -1e30).astype(f32)
    scale = head_size ** (-0.5)
    for head in range(H):
        start, low = head_window(head, head_size, width)
        queries = only_head(q_ref[:, start : start + 256], low, head_size)
        scores = dot_nt(k_ref[:, start : start + 256], queries)
        for at in range(0, slots, 128):
            part = scores[:, at : at + 128] * scale + mask
            exponent = jnp.exp(part - jnp.max(part, axis=0, keepdims=True))
            inverse = 1.0 / jnp.sum(exponent, axis=0, keepdims=True)
            probs_ref[head, :, at : at + 128] = (exponent * inverse).astype(bf16)
        here = slice(head * head_size, (head + 1) * head_size)
        at_ref[here, :] = dot(vt_ref[here, :], probs_ref[head])
    attended_ref[...] = at_ref[...].T.astype(bf16)
    branch = dot(attended_ref[...], weight_part(w_ref, 3))
    middle_ref[...] = x_ref[...].astype(f32) + (branch + vec_ref[OUT_BIAS : OUT_BIAS + 1, :])
    for at in range(0, slots, step):
        unit, _ = norm_parts(middle_ref[at : at + step, :])
        second_ref[at : at + step, :] = (
            unit * vec_ref[GAIN_TWO : GAIN_TWO + 1, :] + vec_ref[SHIFT_TWO : SHIFT_TWO + 1, :]
        ).astype(bf16)


def attn_forward(layer_input, attn_w, vecs, heights, widths, image):
    slots, width = layer_input.shape
    wide = jax.ShapeDtypeStruct((slots, width), f32)
    low = jax.ShapeDtypeStruct((slots, width), bf16)
    here = pl.BlockSpec(memory_space=pltpu.VMEM)
    return pl.pallas_call(
        functools.partial(attn_forward_kernel, image),
        in_specs=[pl.BlockSpec(memory_space=pltpu.SMEM)] * 2 + [here] * 3,
        out_specs=[here] * 8,
        scratch_shapes=[pltpu.VMEM((width, slots), bf16), pltpu.VMEM((width, slots), f32)],
        out_shape=[wide, low, low, low, low, low, jax.ShapeDtypeStruct((H, slots, slots), bf16), low],
        compiler_params=pltpu.CompilerParams(vmem_limit_bytes=6 * 2**20),
        cost_estimate=pl.CostEstimate(
            flops=ATTN_COST * slots * width * width, bytes_accessed=attn_w.size * 2, transcendentals=slots * slots * H
        ),
        name="attn_forward",
    )(heights, widths, layer_input, attn_w, vecs)


def mlp_up_kernel(keep_slope, pieces, *refs):
    second_refs, (up_ref, vec_ref, act_ref) = refs[:pieces], refs[pieces : pieces + 3]
    slope_ref = refs[pieces + 3] if keep_slope else None
    pre_ref = refs[-1]
    index = pl.program_id(0)
    slots, width = second_refs[0].shape
    weight = up_ref[...].reshape(width, width)
    for piece, second_ref in enumerate(second_refs):
        pre_ref[piece * slots : (piece + 1) * slots, :] = dot(second_ref[...], weight)
    bias = vec_ref[pl.ds(UP_BIAS + index, 1), :]

    def gelu_rows(at, _):
        here = pl.ds(at * MLP_CHUNK, MLP_CHUNK)
        pre = pre_ref[here, :] + bias
        below = 0.5 * (1.0 + lax.erf(pre * (0.5**0.5)))
        act_ref[here, :] = (pre * below).astype(bf16)
        if keep_slope:
            bell = jnp.exp(-0.5 * pre * pre) * (0.5 / jnp.pi) ** 0.5
            slope_ref[here, :] = (below + pre * bell).astype(bf16)
        return 0

    lax.fori_loop(0, pre_ref.shape[0] // MLP_CHUNK, gelu_rows, 0)


def mlp_up(second, mlp_w, vecs, keep_slope):
    slots, width = second[0].shape
    count = slots * len(second)
    parts = mlp_w.shape[1] * LEAD // (2 * width)
    outs = 2 if keep_slope else 1
    return pl.pallas_call(
        functools.partial(mlp_up_kernel, keep_slope, len(second)),
        grid=(parts,),
        in_specs=[pl.BlockSpec((slots, width), lambda j: (0, 0))] * len(second)
        + [
            pl.BlockSpec((LEAD, width // LEAD, width), lambda j: (0, j, 0)),
            pl.BlockSpec(vecs.shape, lambda j: (0, 0)),
        ],
        out_specs=[pl.BlockSpec((count, width), lambda j: (0, j))] * outs,
        out_shape=[jax.ShapeDtypeStruct((count, width * parts), bf16)] * outs,
        scratch_shapes=[pltpu.VMEM((count, width), f32)],
        compiler_params=pltpu.CompilerParams(vmem_limit_bytes=14 * 2**20),
        cost_estimate=pl.CostEstimate(
            flops=MLP_COST * count * width * width * parts,
            bytes_accessed=mlp_w.size + count * width * 4 * parts,
            transcendentals=2 * count * width * parts,
        ),
        name="mlp_up",
    )(*second, mlp_w, vecs)


def mlp_down_kernel(pieces, act_ref, *refs):
    middle_refs, (down_ref, vec_ref, result_ref, acc_ref) = refs[:pieces], refs[pieces:]
    index = pl.program_id(0)
    slots, width = middle_refs[0].shape
    added = dot(act_ref[...], down_ref[...].reshape(width, width))

    @pl.when(index == 0)
    def _():
        for piece, middle_ref in enumerate(middle_refs):
            here = slice(piece * slots, (piece + 1) * slots)
            acc_ref[here, :] = added[here] + (middle_ref[...] + vec_ref[DOWN_BIAS : DOWN_BIAS + 1, :])

    @pl.when(index > 0)
    def _():
        acc_ref[...] += added

    @pl.when(index == pl.num_programs(0) - 1)
    def _():
        result_ref[...] = acc_ref[...].astype(bf16)


def mlp_down(activated, middle, mlp_w, vecs, image=0):
    slots, width = middle[0].shape
    count = slots * len(middle)
    parts = activated.shape[1] // width
    return pl.pallas_call(
        functools.partial(mlp_down_kernel, len(middle)),
        grid=(parts,),
        in_specs=[pl.BlockSpec((count, width), lambda j: (image, j))]
        + [pl.BlockSpec((slots, width), lambda j: (0, 0))] * len(middle)
        + [
            pl.BlockSpec((LEAD // parts, mlp_w.shape[1] // 2, width), lambda j: (j, 1, 0)),
            pl.BlockSpec(vecs.shape, lambda j: (0, 0)),
        ],
        out_specs=pl.BlockSpec((count, width), lambda j: (0, 0)),
        out_shape=jax.ShapeDtypeStruct((count, width), bf16),
        scratch_shapes=[pltpu.VMEM((count, width), f32)],
        compiler_params=pltpu.CompilerParams(vmem_limit_bytes=12 * 2**20),
        cost_estimate=pl.CostEstimate(
            flops=MLP_COST * count * width * width * parts,
            bytes_accessed=mlp_w.size + count * width * 10,
            transcendentals=0,
        ),
        name="mlp_down",
    )(activated, *middle, mlp_w, vecs)


def mlp_backward_kernel(pieces, slope_ref, *refs):
    upstream_refs, middle_refs, refs = refs[:pieces], refs[pieces : 2 * pieces], refs[2 * pieces :]
    (up_ref, down_ref, vec_ref), refs = refs[:3], refs[3:]
    grad_middle_refs, branch_refs, refs = refs[:pieces], refs[pieces : 2 * pieces], refs[2 * pieces :]
    grad_pre_ref, sums_ref, up_sum_ref, ga_ref, acc_ref = refs
    index = pl.program_id(0)
    slots, width = upstream_refs[0].shape
    count = slots * pieces
    weight = down_ref[...].reshape(width, width)
    for piece, upstream_ref in enumerate(upstream_refs):
        ga_ref[piece * slots : (piece + 1) * slots, :] = dot_nt(upstream_ref[...], weight)
    sums = jnp.zeros((1, width), f32)
    for at in range(0, count, MLP_CHUNK):
        here = slice(at, at + MLP_CHUNK)
        pre = (ga_ref[here, :] * slope_ref[here, :].astype(f32)).astype(bf16)
        grad_pre_ref[here, :] = pre
        sums += column_sum(pre.astype(f32))
    up_sum_ref[0] = sums
    added = dot_nt(grad_pre_ref[...], up_ref[...].reshape(width, width))

    @pl.when(index == 0)
    def _():
        acc_ref[...] = added

    @pl.when(index > 0)
    def _():
        acc_ref[...] += added

    @pl.when(index == pl.num_programs(0) - 1)
    def _():
        gain = vec_ref[GAIN_TWO : GAIN_TWO + 1, :]
        sums = [jnp.zeros((1, width), f32)] * 3
        for piece in range(pieces):
            for at in range(0, slots, MLP_CHUNK):
                here = slice(at, at + MLP_CHUNK)
                upstream = upstream_refs[piece][here, :].astype(f32)
                grad = acc_ref[piece * slots + at : piece * slots + at + MLP_CHUNK, :]
                grad_mid, gain_terms = norm_back(middle_refs[piece][here, :], gain, grad)
                total = upstream + grad_mid
                grad_middle_refs[piece][here, :] = total
                branch_refs[piece][here, :] = total.astype(bf16)
                sums = [old + column_sum(new) for old, new in zip(sums, (upstream, gain_terms, grad))]
        for row, value in enumerate(sums):
            sums_ref[row : row + 1, :] = value


def mlp_backward(upstream, slope, middle, mlp_w, vecs, image=0):
    slots, width = middle[0].shape
    pieces = len(middle)
    count = slots * pieces
    parts = mlp_w.shape[1] * LEAD // (2 * width)
    whole = pl.BlockSpec((slots, width), lambda j: (0, 0))
    chunk = pl.BlockSpec((count, width), lambda j: (0, j))
    outs = pl.pallas_call(
        functools.partial(mlp_backward_kernel, pieces),
        grid=(parts,),
        in_specs=[pl.BlockSpec((count, width), lambda j: (image, j))]
        + [whole] * 2 * pieces
        + [
            pl.BlockSpec((LEAD, width // LEAD, width), lambda j: (0, j, 0)),
            pl.BlockSpec((LEAD // parts, mlp_w.shape[1] // 2, width), lambda j: (j, 1, 0)),
            pl.BlockSpec(vecs.shape, lambda j: (0, 0)),
        ],
        out_specs=[whole] * 2 * pieces
        + [
            chunk,
            pl.BlockSpec((8, width), lambda j: (0, 0)),
            pl.BlockSpec((1, 1, width), lambda j: (j, 0, 0)),
        ],
        out_shape=[jax.ShapeDtypeStruct((slots, width), f32)] * pieces
        + [jax.ShapeDtypeStruct((slots, width), bf16)] * pieces
        + [
            jax.ShapeDtypeStruct((count, width * parts), bf16),
            jax.ShapeDtypeStruct((8, width), f32),
            jax.ShapeDtypeStruct((parts, 1, width), f32),
        ],
        scratch_shapes=[pltpu.VMEM((count, width), f32)] * 2,
        compiler_params=pltpu.CompilerParams(vmem_limit_bytes=20 * 2**20),
        cost_estimate=pl.CostEstimate(
            flops=2 * MLP_COST * count * width * width * parts,
            bytes_accessed=mlp_w.size * 2 + count * width * (10 + 4 * parts),
            transcendentals=0,
        ),
        name="mlp_backward",
    )(slope, *upstream, *middle, mlp_w, mlp_w, vecs)
    return outs[:pieces], outs[pieces : 2 * pieces], *outs[2 * pieces :]


def attn_backward_kernel(
    grad_middle_ref, branch_ref, x_ref, q_ref, k_ref, v_ref, probs_ref, w_ref, vec_ref,
    grad_in_ref, grad_low_ref, gq_ref, gk_ref, gv_ref, sums_ref,
    ga_ref, gat_ref, qt_ref, kt_ref, gqt_ref, gkt_ref, gvt_ref,
):
    slots, width = x_ref.shape
    head_size = width // H
    scale = head_size ** (-0.5)
    ga = dot_nt(branch_ref[...], weight_part(w_ref, 3)).astype(bf16)
    ga_ref[...] = ga
    gat_ref[...] = ga.T
    qt_ref[...] = q_ref[...].T
    kt_ref[...] = k_ref[...].T
    for head in range(H):
        start, low = head_window(head, head_size, width)
        here = slice(head * head_size, (head + 1) * head_size)
        own = only_head(ga_ref[:, start : start + 256], low, head_size)
        grad_probs = dot_nt(v_ref[:, start : start + 256], own)
        pieces = []
        for at in range(0, slots, 128):
            probs = probs_ref[head, :, at : at + 128].astype(f32)
            grad = grad_probs[:, at : at + 128]
            total = jnp.sum(probs * grad, axis=0, keepdims=True)
            pieces.append((probs * (grad - total)).astype(bf16))
        grad_scores = jnp.concatenate(pieces, axis=1)
        gvt_ref[here, :] = dot_nt(gat_ref[here, :], probs_ref[head])
        gqt_ref[here, :] = dot(kt_ref[here, :], grad_scores) * scale
        gkt_ref[here, :] = dot_nt(qt_ref[here, :], grad_scores) * scale
    gq_ref[...] = gqt_ref[...].T.astype(bf16)
    gk_ref[...] = gkt_ref[...].T.astype(bf16)
    gv_ref[...] = gvt_ref[...].T.astype(bf16)
    grad_normed = dot_nt(gq_ref[...], weight_part(w_ref, 0))
    grad_normed += dot_nt(gk_ref[...], weight_part(w_ref, 1))
    grad_normed += dot_nt(gv_ref[...], weight_part(w_ref, 2))
    grad_in_ref[...] = grad_normed
    gain = vec_ref[GAIN_ONE : GAIN_ONE + 1, :]
    sums = [jnp.zeros((1, width), f32)] * 5
    for at in range(0, slots, MLP_CHUNK):
        rows = slice(at, at + MLP_CHUNK)
        grad = grad_in_ref[rows, :]
        grad_norm, gain_terms = norm_back(x_ref[rows, :].astype(f32), gain, grad)
        total = grad_middle_ref[rows, :] + grad_norm
        grad_in_ref[rows, :] = total
        grad_low_ref[rows, :] = total.astype(bf16)
        terms = (
            gq_ref[rows, :].astype(f32), gv_ref[rows, :].astype(f32), branch_ref[rows, :].astype(f32),
            gain_terms, grad,
        )
        sums = [old + column_sum(new) for old, new in zip(sums, terms)]

    for row, value in enumerate(sums):
        sums_ref[row : row + 1, :] = value


def attn_backward(grad_middle, branch, layer_input, saved, attn_w, vecs):
    queries, key_rows, values, probs = saved
    slots, width = layer_input.shape
    low = jax.ShapeDtypeStruct((slots, width), bf16)
    here = pl.BlockSpec(memory_space=pltpu.VMEM)
    flipped = pltpu.VMEM((width, slots), bf16)
    flipped_wide = pltpu.VMEM((width, slots), f32)
    return pl.pallas_call(
        attn_backward_kernel,
        in_specs=[here] * 9,
        out_specs=[here] * 6,
        out_shape=[jax.ShapeDtypeStruct((slots, width), f32)] + [low] * 4 + [jax.ShapeDtypeStruct((8, width), f32)],
        scratch_shapes=[pltpu.VMEM((slots, width), bf16)] + [flipped] * 3 + [flipped_wide] * 3,
        compiler_params=pltpu.CompilerParams(vmem_limit_bytes=8 * 2**20),
        cost_estimate=pl.CostEstimate(
            flops=ATTN_COST * slots * width * width, bytes_accessed=attn_w.size * 2, transcendentals=0
        ),
        name="attn_backward",
    )(grad_middle, branch, layer_input, queries, key_rows, values, probs, attn_w, vecs)


def ring_slot(owner, me):
    there, here = place_of(lax.div(owner, 2)), place_of(lax.div(me, 2))
    return lax.rem(there - here + RING, RING)


def store_block(own_ref, peer_ref, owner, core, rows, value):
    me = lax.axis_index("dp")
    slot = ring_slot(owner, me)

    @pl.when(lax.rem(me, 2) == core)
    def _():
        own_ref[slot, rows, :] = value

    @pl.when(lax.rem(me, 2) != core)
    def _():
        peer_ref[slot, rows, :] = value


def scatter_shapes(rows, width):
    return [jax.ShapeDtypeStruct((RING, rows, width), bf16)] * 2


def joined(refs, scratch_ref):
    slots = refs[0].shape[0]
    for piece, ref in enumerate(refs):
        scratch_ref[piece * slots : (piece + 1) * slots, :] = ref[...]


def flipped(refs, scratch_ref):
    slots = refs[0].shape[0]
    for piece, ref in enumerate(refs):
        scratch_ref[:, piece * slots : (piece + 1) * slots] = ref[...].T


def grad_down_kernel(pieces, act_ref, *refs):
    upstream_refs, (own_ref, peer_ref, right_ref) = refs[:pieces], refs[pieces:]
    index = pl.program_id(0)
    rows = own_ref.shape[1]

    @pl.when(index == 0)
    def _():
        joined(upstream_refs, right_ref)

    value = dot_tn(act_ref[...], right_ref[...]).astype(bf16)
    for at in range(value.shape[0] // rows):
        owner = index * (value.shape[0] // rows) + at
        store_block(own_ref, peer_ref, owner, at % 2, slice(None), value[at * rows : (at + 1) * rows])


def grad_down_blocks(activated, upstream):
    slots, width = upstream[0].shape
    count, hidden = activated.shape
    parts = hidden // width
    rows = hidden // LEAD
    return pl.pallas_call(
        functools.partial(grad_down_kernel, len(upstream)),
        grid=(parts,),
        in_specs=[pl.BlockSpec((count, width), lambda j: (0, j))]
        + [pl.BlockSpec((slots, width), lambda j: (0, 0))] * len(upstream),
        out_specs=[pl.BlockSpec((RING, rows, width), lambda j: (0, 0, 0))] * 2,
        out_shape=scatter_shapes(rows, width),
        scratch_shapes=[pltpu.VMEM((count, width), bf16)],
        compiler_params=pltpu.CompilerParams(vmem_limit_bytes=18 * 2**20),
        cost_estimate=pl.CostEstimate(
            flops=MLP_COST * count * width * hidden, bytes_accessed=count * hidden * 2 + hidden * width * 2, transcendentals=0
        ),
        name="grad_down",
    )(activated, *upstream)


def grad_up_kernel(pieces, *refs):
    pre_refs, second_refs, attended_refs, branch_refs, (own_ref, peer_ref, left_ref, right_ref) = (
        *(refs[at * pieces : (at + 1) * pieces] for at in range(4)), refs[4 * pieces :]
    )
    index = pl.program_id(0)
    rows = second_refs[0].shape[1] // LEAD

    @pl.when(index == 0)
    def _():
        flipped(second_refs, left_ref)

    joined(pre_refs, right_ref)
    value = dot(left_ref[...], right_ref[...]).astype(bf16)
    for owner in range(LEAD):
        here = pl.ds(pl.multiple_of(index * rows, rows), rows)
        store_block(own_ref, peer_ref, owner, owner % 2, here, value[owner * rows : (owner + 1) * rows])

    @pl.when(index == pl.num_programs(0) - 1)
    def _():
        flipped(attended_refs, left_ref)
        joined(branch_refs, right_ref)
        last = dot(left_ref[...], right_ref[...]).astype(bf16)
        for owner in range(LEAD):
            here = pl.ds(own_ref.shape[1] - rows, rows)
            store_block(own_ref, peer_ref, owner, owner % 2, here, last[owner * rows : (owner + 1) * rows])


def grad_up_blocks(second, grad_pre, attended, branch):
    slots, width = second[0].shape
    count, hidden = slots * len(second), grad_pre[0].shape[1]
    parts = hidden // width
    rows = (hidden + width) // LEAD
    whole = [pl.BlockSpec((slots, width), lambda j: (0, 0))] * len(second)
    return pl.pallas_call(
        functools.partial(grad_up_kernel, len(second)),
        grid=(parts,),
        in_specs=[pl.BlockSpec((slots, width), lambda j: (0, j))] * len(second) + whole * 3,
        out_specs=[pl.BlockSpec((RING, rows, width), lambda j: (0, 0, 0))] * 2,
        out_shape=scatter_shapes(rows, width),
        scratch_shapes=[pltpu.VMEM((width, count), bf16), pltpu.VMEM((count, width), bf16)],
        compiler_params=pltpu.CompilerParams(vmem_limit_bytes=24 * 2**20),
        cost_estimate=pl.CostEstimate(
            flops=MLP_COST * count * width * hidden, bytes_accessed=count * hidden * 2 + hidden * width * 2, transcendentals=0
        ),
        name="grad_up",
    )(*grad_pre, *second, *attended, *branch)


def grad_qkv_kernel(pieces, *refs):
    left_refs, rights = refs[:pieces], refs[pieces : 4 * pieces]
    attn_sums, mlp_sums, up_sums = (refs[at * pieces : (at + 1) * pieces] for at in (4, 5, 6))
    own_ref, peer_ref, left_ref, right_ref, vec_ref = refs[7 * pieces :]
    width = left_refs[0].shape[1]
    rows = width // LEAD
    flipped(left_refs, left_ref)
    for part in range(3):
        joined(rights[part * pieces : (part + 1) * pieces], right_ref)
        value = dot(left_ref[...], right_ref[...]).astype(bf16)
        for owner in range(LEAD):
            here = slice(part * rows, (part + 1) * rows)
            store_block(own_ref, peer_ref, owner, owner % 2, here, value[owner * rows : (owner + 1) * rows])
    vec_ref[...] = jnp.zeros_like(vec_ref)
    for name, refs_of, row in (
        (Q_BIAS, attn_sums, 0), (V_BIAS, attn_sums, 1), (OUT_BIAS, attn_sums, 2), (DOWN_BIAS, mlp_sums, 0),
        (GAIN_ONE, attn_sums, 3), (SHIFT_ONE, attn_sums, 4), (GAIN_TWO, mlp_sums, 1), (SHIFT_TWO, mlp_sums, 2),
    ):
        vec_ref[name : name + 1, :] = sum(ref[row : row + 1, :] for ref in refs_of)
    for part in range(up_sums[0].shape[0]):
        vec_ref[UP_BIAS + part : UP_BIAS + part + 1, :] = sum(ref[part] for ref in up_sums)
    vectors = vec_ref[...].astype(bf16)
    here = slice(3 * rows, 3 * rows + VEC_ROWS)
    for slot in range(RING):
        own_ref[slot, here, :] = vectors
        peer_ref[slot, here, :] = vectors


def grad_qkv_blocks(normed, rights, attn_sums, mlp_sums, up_sums):
    slots, width = normed[0].shape
    count = slots * len(normed)
    arrays = [*normed, *(piece for right in rights for piece in right), *attn_sums, *mlp_sums, *up_sums]
    rows = 3 * width // LEAD + VEC_ROWS
    return pl.pallas_call(
        functools.partial(grad_qkv_kernel, len(normed)),
        in_specs=[pl.BlockSpec(memory_space=pltpu.VMEM)] * len(arrays),
        out_specs=[pl.BlockSpec(memory_space=pltpu.VMEM)] * 2,
        out_shape=scatter_shapes(rows, width),
        scratch_shapes=[
            pltpu.VMEM((width, count), bf16), pltpu.VMEM((count, width), bf16), pltpu.VMEM((VEC_ROWS, width), f32)
        ],
        compiler_params=pltpu.CompilerParams(vmem_limit_bytes=6 * 2**20),
        cost_estimate=pl.CostEstimate(
            flops=3 * MLP_COST * count * width * width, bytes_accessed=len(arrays) * slots * width * 2, transcendentals=0
        ),
        name="grad_qkv",
    )(*arrays)


VECS = ("q_bias", "v_bias", "out_bias", "down_bias", "gain_one", "shift_one", "gain_two", "shift_two")


def solution(mesh):
    dp_size = mesh.shape["dp"]
    ringed = dp_size == 2 * RING

    def gathered_whole(qkv, out, up, down, vectors):
        width = out.shape[1]
        gathered = [lax.all_gather(w, "dp", axis=0, tiled=True) for w in (qkv, out, up, down)]
        blocked = [w.reshape(LEAD, -1, w.shape[1]) for w in gathered]
        fold = lambda w: w.reshape(LEAD, w.shape[1], -1, width).transpose(0, 2, 1, 3).reshape(LEAD, -1, width)
        first = jnp.concatenate([fold(blocked[0]), blocked[1], jnp.zeros((LEAD, VEC_ROWS, width), bf16)], 1)
        whole = lambda name: lax.all_gather(vectors[name], "dp", axis=0, tiled=True)
        vecs = jnp.concatenate([jnp.stack([whole(name) for name in VECS]), whole("up_bias").reshape(-1, width)])
        vecs = jnp.pad(vecs.astype(f32), ((0, VEC_ROWS - vecs.shape[0]), (0, 0)))
        return first, jnp.concatenate([fold(blocked[2]), blocked[3]], 1), vecs

    def own_vectors(block):
        me = lax.axis_index("dp")
        width = block.shape[1]
        rows = width // LEAD
        small = lax.dynamic_slice(block, (0, me * rows), (len(VECS), rows))
        parts = (3 * LEAD + LEAD) * rows // width
        size = parts * rows
        in_row = width // size
        own = {name: small[at] for at, name in enumerate(VECS)}
        own["up_bias"] = lax.dynamic_slice(block, (len(VECS) + me // in_row, me % in_row * size), (1, size))[0]
        return own

    def shards(
        tokens, cotangent, heights, widths, qkv_weight, out_weight, up_weight, down_weight,
        q_bias, v_bias, out_bias, up_bias, down_bias, gain_one, shift_one, gain_two, shift_two,
    ):
        leading = lax.axis_index("section") == 0
        width = tokens.shape[1]
        images = heights.shape[0]
        each = range(images)
        rows = width // LEAD
        cut = lambda array: jnp.split(array, images)
        vectors = dict(
            q_bias=q_bias[0], v_bias=v_bias[0], out_bias=out_bias[0], up_bias=up_bias[0], down_bias=down_bias[0],
            gain_one=gain_one[0], shift_one=shift_one[0], gain_two=gain_two[0], shift_two=shift_two[0],
        )
        inputs, cotangents = cut(tokens), cut(cotangent)

        attention = lambda x, image: attn_forward(x, attn_w, vecs, heights, widths, image)
        if ringed:
            small = jnp.stack([vectors[name] for name in VECS])
            g = gather_start(pack_first(qkv_weight[0], out_weight[0], small, vectors["up_bias"][None]))
            m = gather_start(pack_second(up_weight[0], down_weight[0]))
            for _ in range(RING // 2 - 1):
                g, m = tie(gather_step(g), m)
            g, m = gather_step(g), gather_step(m)
            attn_w, vecs = assemble(gather_blocks(g), True)
            m, attn_w, vecs = tie(m, attn_w, vecs)
            m = gather_step(m)
            front = [attention(inputs[image], image)[:2] for image in each]
            m, front = tie(m, front)
            for _ in range(m["step"], RING // 2):
                m = gather_step(m)
            mlp_w = assemble(gather_blocks(m))
        else:
            attn_w, mlp_w, vecs = gathered_whole(
                qkv_weight[0], out_weight[0], up_weight[0], down_weight[0], vectors
            )
            front = [attention(inputs[image], image)[:2] for image in each]
        received = []
        for image in each:
            (activated,) = mlp_up(front[image][1:], mlp_w, vecs, False)
            sent = mlp_down(activated, front[image][:1], mlp_w, vecs)
            front, sent = tie(front, sent)
            received.append(lax.ppermute(sent, "section", [(0, 1)]))

        layer_input, kept = [], []
        for image in each:
            layer_input.append(jnp.where(leading, inputs[image], received[image]))
            kept.append(attention(layer_input[image], image))
            kept, received = tie(kept, received)
        middle, second, normed, queries, key_rows, values, probs, attended = zip(*kept)
        activated, slope = mlp_up(second, mlp_w, vecs, True)

        back_attn = lambda grad, branch, image: attn_backward(
            grad[image], branch[image], layer_input[image],
            (queries[image], key_rows[image], values[image], probs[image]), attn_w, vecs,
        )
        grad_middle, branch = mlp_backward(cotangents, slope, middle, mlp_w, vecs)[:2]
        arriving = []
        for image in each:
            to_send = back_attn(grad_middle, branch, image)[1]
            grad_middle, branch, activated, to_send = tie(grad_middle, branch, activated, to_send)
            arriving.append(lax.ppermute(to_send, "section", [(1, 0)]))
        upstream, back = [], []

        def back_one(image):
            upstream.append(jnp.where(leading, arriving[image], cotangents[image]))
            back.append(mlp_backward(upstream[image:], slope, middle[image : image + 1], mlp_w, vecs, image))

        back_one(0)
        back, arriving, activated = tie(back, arriving, activated)
        result = mlp_down(activated, middle, mlp_w, vecs)
        result, arriving, activated = tie(result, arriving, activated)
        if ringed:
            rest = [jnp.where(leading, arriving[image], cotangents[image]) for image in each[1:]]
            d = scatter_start(*grad_down_blocks(activated, upstream + rest))
            d, arriving = scatter_step(d, arriving)
            for image in each[1:]:
                back_one(image)
            d, back = tie(d, back)
            d, back = scatter_step(d, back)
            grad_middle, branch, grad_pre, mlp_sums, up_sums = zip(*back)
            grad_middle, branch = [g for (g,) in grad_middle], [g for (g,) in branch]
            u = scatter_start(*grad_up_blocks(second, grad_pre, attended, branch))
            d, u = tie(d, u)
            held = (grad_middle, branch)
            attn_back = []
            for image in each:
                if image < 2:
                    d, held = scatter_step(d, held)
                    u, held = scatter_step(u, held)
                attn_back.append(back_attn(*held, image))
                d, u, attn_back, held = tie(d, u, attn_back, held)
            d, attn_back = scatter_step(d, attn_back)
            u, attn_back = scatter_step(u, attn_back)
        else:
            for image in each[1:]:
                back_one(image)
            grad_middle, branch, grad_pre, mlp_sums, up_sums = zip(*back)
            grad_middle, branch = [g for (g,) in grad_middle], [g for (g,) in branch]
            attn_back = [back_attn(grad_middle, branch, image) for image in each]
        grad_input, _, gq, gk, gv, attn_sums = zip(*attn_back)
        if ringed:
            q = scatter_start(*grad_qkv_blocks(normed, (gq, gk, gv), attn_sums, mlp_sums, up_sums))
            parts = mlp_w.shape[1] // rows - 4
            ends = RING // 2 + 1
            q = scatter_step(scatter_step(q)[0])[0]
            d, q = tie(d, q)
            while min(d["step"], u["step"], q["step"]) < ends:
                d, u, q = (state if state["step"] == ends else scatter_step(state)[0] for state in (d, u, q))
            (g_down,) = scatter_sum(d, [(0, d["own"].shape[1], 1)])
            g_up, g_out = scatter_sum(u, [(0, rows, parts), (parts * rows, rows, 1)])
            g_qkv, vec_sums = scatter_sum(q, [(0, rows, 3), (3 * rows, VEC_ROWS, 1)])
            g_vecs = own_vectors(vec_sums)
        else:
            attn_sums = sum(attn_sums)
            sums = dict(zip(("q_bias", "v_bias", "out_bias", "gain_one", "shift_one"), attn_sums))
            sums |= dict(zip(("down_bias", "gain_two", "shift_two"), sum(mlp_sums)))
            sums["up_bias"] = sum(up_sums).reshape(-1)
            scatter = lambda a: lax.psum_scatter(a, "dp", scatter_dimension=0, tiled=True)
            whole = lambda pieces: jnp.concatenate(pieces)
            outer = lambda a, b: lax.dot_general(a, b, TN, preferred_element_type=f32)
            g_down = scatter(outer(activated, whole(upstream)))
            g_up = scatter(outer(whole(second), whole(grad_pre)))
            g_qkv = scatter(jnp.concatenate([outer(whole(normed), whole(part)) for part in (gq, gk, gv)], 1))
            g_out = scatter(outer(whole(attended), whole(branch)))
            g_vecs = {name: scatter(value) for name, value in sums.items()}
        return (
            result[None], jnp.concatenate(grad_input)[None],
            g_qkv[None], g_out[None], g_up[None], g_down[None],
            *(
                g_vecs[name][None]
                for name in (
                    "q_bias", "v_bias", "out_bias", "up_bias", "down_bias",
                    "gain_one", "shift_one", "gain_two", "shift_two",
                )
            ),
        )

    rows_spec = P("dp", None)
    three, two = P("section", "dp", None), P("section", "dp")
    return jax.shard_map(
        shards,
        mesh=mesh,
        in_specs=(rows_spec, rows_spec, P("dp"), P("dp")) + (three,) * 4 + (two,) * 9,
        out_specs=(three,) * 6 + (two,) * 9,
        check_vma=False,
    )
```

time: 399 us -> 303 us (0.76)
  waiting for transfers between devices: 118 us -> 84.8 us
  Pallas kernels: 152 us -> 132 us
  other arithmetic: 18.4 us -> 3.01 us
  starting transfers between devices: 69.6 us -> 54.5 us
  local copies, waits for them, and re-layouts: 34.8 us -> 23.3 us
    ppermute x2 -> x4, waiting for transfers between devices: 36.6 us -> 6.89 us  [the longest x2 5.05 us: shards(): arriving.append(lax.ppermute(to_send, 'section', [(1, 0)]))]
    ppermute x24 -> x20, starting transfers between devices: 38.3 us -> 13.2 us  [onward(): return lax.ppermute(block, 'dp', ring_route(1))]
    pallas_call x14 -> x39, Pallas kernels: 152 us -> 132 us  [the longest x4 31.8 us: attn_backward(): pl.pallas_call(attn_backward_kernel, in_specs=[here] * 9, out_specs=[here...]
    unnamed x62 -> x138, local copies, waits for them, and re-layouts: 30.4 us -> 19.9 us
    convert_element_type x12 -> x0, other arithmetic: 10.1 us -> none  [the longest x6 5.05 us: ring_scatter(): up = onward((local(step) + up.astype(f32)).astype(bf16))]
    ppermute x24 -> x20, starting transfers between devices: 20.9 us -> 30.1 us  [backward(): return lax.ppermute(block, 'dp', ring_route(-1))]
    ppermute x24 -> x20, waiting for transfers between devices: 29.8 us -> 26.7 us  [backward(): return lax.ppermute(block, 'dp', ring_route(-1))]
    ppermute x24 -> x20, waiting for transfers between devices: 50.1 us -> 47.9 us  [onward(): return lax.ppermute(block, 'dp', ring_route(1))]
  transfers between devices with their start and end apart: 80 -> 65, of which waited for: 35 -> 30; matrix products, arithmetic and copies ran while one was open for 6% -> 1% of each run, Pallas kernels for 10% -> 25%
where the time goes in v3:
time: 303 us; the launch traced here: 300 us
  Pallas kernels  132 us (44%)
  waiting for transfers between devices  84.8 us (28%)
  starting transfers between devices  54.5 us (18%)
  local copies, waits for them, and re-layouts  23.3 us (8%)
    ppermute x20, waiting for transfers between devices, onward(): return lax.ppermute(block, 'dp', ring_route(1))  47.9 us
    pallas_call x4, Pallas kernels, attn_backward(): pl.pallas_call(attn_backward_kernel, in_specs=[here] * 9, out_specs=[here...  31.8 us
    ppermute x20, starting transfers between devices, backward(): return lax.ppermute(block, 'dp', ring_route(-1))  30.1 us
    ppermute x20, waiting for transfers between devices, backward(): return lax.ppermute(block, 'dp', ring_route(-1))  26.7 us
    pallas_call x4, Pallas kernels, attn_forward(): pl.pallas_call(functools.partial(attn_forward_kernel, image), in_specs=[p...  26.4 us
    pallas_call x3, Pallas kernels, mlp_backward(): pl.pallas_call(functools.partial(mlp_backward_kernel, pieces), grid=(part...  20.8 us
    unnamed x138, local copies, waits for them, and re-layouts  19.9 us
    pallas_call x3, Pallas kernels, mlp_up(): pl.pallas_call(functools.partial(mlp_up_kernel, keep_slope, len(second)),...  14.8 us
  transfers between devices with their start and end apart: 65, of which 30 were waited for; matrix products, arithmetic and copies ran while one was open for 1% of the time, Pallas kernels for 25%

profile of v3, /device:TPU:0, one launch (start us, length us, event | category | flops | bytes accessed | tf_op | source)
XLA Modules:
  0.0 299.5 jit_solution(8367105437725408136)
XLA Ops:
  4.0 3.0 %collective-permute-start = (bf16[208,768]{1,0:T(8,128)(2,1)S(1)}, bf16[208,768]{1,0:T(8,128)(2,1)S(1)}, u32[]{:S(2)}, u32[]{:S(2)}) collective-permute-start(bf16[208,768]{1,0:T(8,128)(2,1)S(1)} %pack_first.1.refs_0_), channel_id=1, source_target_pairs={{0,2},{1,3},{4,0},{5,1},{8,4},{9,5},{12,8},{13,9},{14,12},{15,13},... | collective-permute-start | bytes 958472 | tf_op jit(solution)/shard_map/ppermute | solution.py:49
  9.1 5.5 %collective-permute-done.refs_2_ = bf16[208,768]{1,0:T(8,128)(2,1)S(1)} collective-permute-done((bf16[208,768]{1,0:T(8,128)(2,1)S(1)}, bf16[208,768]{1,0:T(8,128)(2,1)S(1)}, u32[]{:S(2)}, u32[]{:S(2)}) %collective-permute-start) | collective-permute-done | bytes 319520 | tf_op jit(solution)/shard_map/ppermute | solution.py:49
  16.0 1.6 collective-permute-start.3
  18.6 5.5 %collective-permute-done.3.refs_4_ = bf16[208,768]{1,0:T(8,128)(2,1)S(1)} collective-permute-done((bf16[208,768]{1,0:T(8,128)(2,1)S(1)}, bf16[208,768]{1,0:T(8,128)(2,1)S(1)}, u32[]{:S(2)}, u32[]{:S(2)}) %collective-permute-start.3) | collective-permute-done | bytes 319520 | tf_op jit(solution)/shard_map/ppermute | solution.py:49
  25.4 1.6 collective-permute-start.7
  28.0 4.4 %collective-permute-done.7.refs_6_ = bf16[208,768]{1,0:T(8,128)(2,1)S(1)} collective-permute-done((bf16[208,768]{1,0:T(8,128)(2,1)S(1)}, bf16[208,768]{1,0:T(8,128)(2,1)S(1)}, u32[]{:S(2)}, u32[]{:S(2)}) %collective-permute-start.7) | collective-permute-done | bytes 319520 | tf_op jit(solution)/shard_map/ppermute | solution.py:49
  32.4 2.5 collective-permute-done.8.refs_12_
  35.5 1.6 collective-permute-start.16
  39.2 2.7 collective-permute-done.15.refs_8_
  46.1 2.7 assemble.2
  52.7 6.9 %attn_forward.4 = (f32[256,768]{1,0:T(8,128)S(1)}, bf16[256,768]{1,0:T(8,128)(2,1)S(1)}, bf16[256,768]{1,0:T(8,128)(2,1)}, bf16[256,768]{1,0:T(8,128)(2,1)}, bf1...) custom-call(s32[2]{0:T(128)S(1)} %copy-done.32, ...), custom_call_target="tpu_custom_call" | custom-call | flops 3623878656 | bytes 5111808 | tf_op jit(solution)/shard_map/attn_forward/pallas_call | solution.py:373
  61.2 6.9 %attn_forward.5 = (f32[256,768]{1,0:T(8,128)S(1)}, bf16[256,768]{1,0:T(8,128)(2,1)S(1)}, bf16[256,768]{1,0:T(8,128)(2,1)}, bf16[256,768]{1,0:T(8,128)(2,1)}, bf1...) custom-call(s32[2]{0:T(128)S(1)} %copy-done.32, ...), custom_call_target="tpu_custom_call" | custom-call | flops 3623878656 | bytes 5111808 | tf_op jit(solution)/shard_map/attn_forward/pallas_call | solution.py:373
  72.0 1.6 collective-permute-start.25
  74.1 12.9 %collective-permute-done.27.refs_12_ = bf16[384,768]{1,0:T(8,128)(2,1)S(1)} collective-permute-done((bf16[384,768]{1,0:T(8,128)(2,1)}, bf16[384,768]{1,0:T(8,128)(2,1)S(1)}, u32[]{:S(2)}, u32[]{:S(2)}) %collective-permute-start.27) | collective-permute-done | bytes 589856 | tf_op jit(solution)/shard_map/ppermute | solution.py:45
  87.5 1.8 collective-permute-start.29
  90.5 4.8 %collective-permute-done.28.refs_8_ = bf16[192,768]{1,0:T(8,128)(2,1)} collective-permute-done((bf16[192,768]{1,0:T(8,128)(2,1)S(1)}, bf16[192,768]{1,0:T(8,128)(2,1)}, u32[]{:S(2)}, u32[]{:S(2)}) %collective-permute-start.28) | collective-permute-done | bytes 294944 | tf_op jit(solution)/shard_map/ppermute | solution.py:45
  95.3 2.1 collective-permute-done.29.refs_9_
  103.5 3.0 %assemble.3.refs_1_.refs_2_.refs_4_.refs_5_.refs_3_ = bf16[16,384,768]{2,1,0:T(8,128)(2,1)S(1)} custom-call(bf16[384,768]{1,0:T(8,128)(2,1)S(1)} %pack_second.1.refs_0_, bf16[384,768]{1,0:T(8,128)(2,1)S(1)} %collective-permute-done.13.refs_1_, bf16[384,768]{1,0:T(8,128)(2,1)S(1)} %collective-permute-done.11.refs_2_, bf16[384,768]{1,0:T(8,128)(2,1)S(1)} %copy-done.15, ...), custom_call_target="tpu_custom_call" | custom-call | tf_op jit(solution)/shard_map/assemble/pallas_call | solution.py:180
  106.6 3.4 %mlp_up.3.act_ref = bf16[256,3072]{1,0:T(8,128)(2,1)S(1)} custom-call(bf16[256,768]{1,0:T(8,128)(2,1)S(1)} %copy-done.43, bf16[16,384,768]{2,1,0:T(8,128)(2,1)S(1)} %assemble.3.refs_1_.refs_2_.refs_4_.refs_5_.refs_3_, f32[16,768]{1,0:T(8,128)S(1)} %copy-done.31), custom_call_target="tpu_custom_call" | custom-call | flops 3623878656 | bytes 7864320 | tf_op jit(solution)/shard_map/mlp_up/pallas_call | solution.py:416
  110.0 2.8 mlp_down.3
  112.8 3.5 %collective-permute-start.34 = (bf16[256,768]{1,0:T(8,128)(2,1)S(1)}, bf16[256,768]{1,0:T(8,128)(2,1)S(1)}, u32[]{:S(2)}, u32[]{:S(2)}) collective-permute-start(bf16[256,768]{1,0:T(8,128)(2,1)S(1)} %mlp_down.3), channel_id=1, source_target_pairs={{0,16},{1,17},{2,18},{3,19},{4,20},{5,21},{6,22},{7,23},{8,24},{9,... | collective-permute-start | bytes 1179656 | tf_op jit(solution)/shard_map/ppermute | solution.py:886
  116.4 3.4 %mlp_up.4.act_ref = bf16[256,3072]{1,0:T(8,128)(2,1)S(1)} custom-call(bf16[256,768]{1,0:T(8,128)(2,1)S(1)} %copy-done.45, bf16[16,384,768]{2,1,0:T(8,128)(2,1)S(1)} %assemble.3.refs_1_.refs_2_.refs_4_.refs_5_.refs_3_, f32[16,768]{1,0:T(8,128)S(1)} %copy-done.31), custom_call_target="tpu_custom_call" | custom-call | flops 3623878656 | bytes 7864320 | tf_op jit(solution)/shard_map/mlp_up/pallas_call | solution.py:416
  119.9 2.8 mlp_down.4
  124.0 1.8 collective-permute-done.34
  125.9 6.3 %attn_forward.6 = (f32[256,768]{1,0:T(8,128)S(1)}, bf16[256,768]{1,0:T(8,128)(2,1)S(1)}, bf16[256,768]{1,0:T(8,128)(2,1)S(1)}, bf16[256,768]{1,0:T(8,128)(2,1)S(...) custom-call(s32[2]{0:T(128)S(1)} %copy-done.32, ...), custom_call_target="tpu_custom_call" | custom-call | flops 3623878656 | bytes 5111808 | tf_op jit(solution)/shard_map/attn_forward/pallas_call | solution.py:373
  133.8 6.3 %attn_forward.7 = (f32[256,768]{1,0:T(8,128)S(1)}, bf16[256,768]{1,0:T(8,128)(2,1)S(1)}, bf16[256,768]{1,0:T(8,128)(2,1)S(1)}, bf16[256,768]{1,0:T(8,128)(2,1)S(...) custom-call(s32[2]{0:T(128)S(1)} %copy-done.32, ...), custom_call_target="tpu_custom_call" | custom-call | flops 3623878656 | bytes 5111808 | tf_op jit(solution)/shard_map/attn_forward/pallas_call | solution.py:373
  140.2 7.9 %mlp_up.5 = (bf16[512,3072]{1,0:T(8,128)(2,1)S(1)}, bf16[512,3072]{1,0:T(8,128)(2,1)S(1)}) custom-call(bf16[256,768]{1,0:T(8,128)(2,1)S(1)} %get-tuple-element.415.refs_0_.refs_2_, bf16[256,768]{1,0:T(8,128)(2,1)S(1)} %get-tuple-element.416.refs_1_.refs_3_, bf16[16,384,768]{2,1,0:T(8,128)(2,1)S(1)} %assemble.3.refs_1_.refs_2_.refs_4_.refs_5_.refs_3_, ...), custom_call_target="tpu_custom_call" | custom-call | flops 7247757312 | bytes 11010048 | tf_op jit(solution)/shard_map/mlp_up/pallas_call | solution.py:416
  148.1 9.5 %mlp_backward.3 = (f32[256,768]{1,0:T(8,128)S(1)}, f32[256,768]{1,0:T(8,128)S(1)}, bf16[256,768]{1,0:T(8,128)(2,1)S(1)}, bf16[256,768]{1,0:T(8,128)(2,1)S(1)}, b...) custom-call(bf16[512,3072]{1,0:T(8,128)(2,1)S(1)} %get-tuple-element.417.slope_ref, ...), custom_call_target="tpu_custom_call" | custom-call | flops 14495514624 | bytes 19660800 | tf_op jit(solution)/shard_map/mlp_backward/pallas_call | solution.py:537
  157.7 8.0 %attn_backward.4 = (f32[256,768]{1,0:T(8,128)}, bf16[256,768]{1,0:T(8,128)(2,1)S(1)}, bf16[256,768]{1,0:T(8,128)(2,1)}, bf16[256,768]{1,0:T(8,128)(2,1)}, bf16[256,768]{1,0:T(8,128)(2,1)}, /*index=5*/f32[8,768]{1,0:T(8,128)}) custom-call(f32[256,768]{1,0:T(8,128)S(1)} %get-tuple-element.420.grad_middle_ref, ...), custom_call_target="tpu_custom_call" | custom-call | flops 3623878656 | bytes 5111808 | tf_op jit(solution)/shard_map/attn_backward/pallas_call | solution.py:633
  165.7 1.6 collective-permute-start.36
  167.2 8.0 %attn_backward.5 = (f32[256,768]{1,0:T(8,128)}, bf16[256,768]{1,0:T(8,128)(2,1)S(1)}, bf16[256,768]{1,0:T(8,128)(2,1)}, bf16[256,768]{1,0:T(8,128)(2,1)}, bf16[256,768]{1,0:T(8,128)(2,1)}, /*index=5*/f32[8,768]{1,0:T(8,128)}) custom-call(f32[256,768]{1,0:T(8,128)S(1)} %get-tuple-element.436.grad_middle_ref, ...), custom_call_target="tpu_custom_call" | custom-call | flops 3623878656 | bytes 5111808 | tf_op jit(solution)/shard_map/attn_backward/pallas_call | solution.py:633
  177.9 5.7 %mlp_backward.4 = (f32[256,768]{1,0:T(8,128)S(1)}, bf16[256,768]{1,0:T(8,128)(2,1)S(1)}, bf16[256,3072]{1,0:T(8,128)(2,1)S(1)}, f32[8,768]{1,0:T(8,128)S(1)}, f32[4,1,768]{2,1,0:T(1,128)S(1)}) custom-call(bf16[512,3072]{1,0:T(8,128)(2,1)S(1)} %get-tuple-element.417.slope_ref, bf16[256,768]{1,0:T(8,128)(2,1)S(1)} %broadcast_select_fusion.2.refs_0_, ...), custom_call_target="tpu_custom_call" | custom-call | flops 7247757312 | bytes 14548992 | tf_op jit(solution)/shard_map/mlp_backward/pallas_call | solution.py:537
  183.6 3.7 %collective-permute-done.37 = bf16[256,768]{1,0:T(8,128)(2,1)S(1)} collective-permute-done((bf16[256,768]{1,0:T(8,128)(2,1)S(1)}, bf16[256,768]{1,0:T(8,128)(2,1)S(1)}, u32[]{:S(2)}, u32[]{:S(2)}) %collective-permute-start.37) | collective-permute-done | bytes 393248 | tf_op jit(solution)/shard_map/ppermute | solution.py:905
  187.3 5.3 %mlp_down.5 = bf16[512,768]{1,0:T(8,128)(2,1)} custom-call(bf16[512,3072]{1,0:T(8,128)(2,1)S(1)} %get-tuple-element.449.act_ref, f32[256,768]{1,0:T(8,128)S(1)} %get-tuple-element.418.refs_2_.refs_1_.refs_0_, f32[256,768]{1,0:T(8,128)S(1)} %get-tuple-element.419.refs_3_.refs_1_, bf16[16,384,768]{2,1,0:T(8,128)(2,1)S(1)} %assemble.3.refs_1_.refs_2_.refs_4_.refs_5_.refs_3_, ...), custom_call_target="tpu_custom_call" | custom-call | flops 7247757312 | bytes 8650752 | tf_op jit(solution)/shard_map/mlp_down/pallas_call | solution.py:462
  192.6 4.3 %grad_down.1 = (bf16[8,192,768]{2,1,0:T(8,128)(2,1)S(1)}, bf16[8,192,768]{2,1,0:T(8,128)(2,1)S(1)}) custom-call(bf16[512,3072]{1,0:T(8,128)(2,1)S(1)} %get-tuple-element.449.act_ref, bf16[256,768]{1,0:T(8,128)(2,1)S(1)} %broadcast_select_fusion.2.refs_0_, bf16[256,768]{1,0:T(8,128)(2,1)S(1)} %broadcast_select_fusion.1.refs_1_), custom_call_target="tpu_custom_call" | custom-call | flops 7247757312 | bytes 7864320 | tf_op jit(solution)/shard_map/grad_down/pallas_call | solution.py:701
  197.0 5.7 %mlp_backward.5 = (f32[256,768]{1,0:T(8,128)S(1)}, bf16[256,768]{1,0:T(8,128)(2,1)S(1)}, bf16[256,3072]{1,0:T(8,128)(2,1)S(1)}, f32[8,768]{1,0:T(8,128)S(1)}, f32[4,1,768]{2,1,0:T(1,128)S(1)}) custom-call(bf16[512,3072]{1,0:T(8,128)(2,1)S(1)} %get-tuple-element.417.slope_ref, bf16[256,768]{1,0:T(8,128)(2,1)S(1)} %broadcast_select_fusion.refs_0_, ...), custom_call_target="tpu_custom_call" | custom-call | flops 7247757312 | bytes 14548992 | tf_op jit(solution)/shard_map/mlp_backward/pallas_call | solution.py:537
  202.8 1.6 collective-permute-start.39
  205.4 5.6 %grad_up.1 = (bf16[8,240,768]{2,1,0:T(8,128)(2,1)S(1)}, bf16[8,240,768]{2,1,0:T(8,128)(2,1)S(1)}) custom-call(bf16[256,3072]{1,0:T(8,128)(2,1)S(1)} %copy-done.41, bf16[256,3072]{1,0:T(8,128)(2,1)S(1)} %get-tuple-element.482.refs_1_, bf16[256,768]{1,0:T(8,128)(2,1)S(1)} %copy-done.57, bf16[256,768]{1,0:T(8,128)(2,1)S(1)} %copy-done.61, ...), custom_call_target="tpu_custom_call" | custom-call | flops 7247757312 | bytes 7864320 | tf_op jit(solution)/shard_map/grad_up/pallas_call | solution.py:750
  213.8 7.9 %attn_backward.6 = (f32[256,768]{1,0:T(8,128)S(1)}, bf16[256,768]{1,0:T(8,128)(2,1)}, bf16[256,768]{1,0:T(8,128)(2,1)S(1)}, bf16[256,768]{1,0:T(8,128)(2,1)S(1)}...) custom-call(f32[256,768]{1,0:T(8,128)S(1)} %get-tuple-element.506.grad_middle_ref, ...), custom_call_target="tpu_custom_call" | custom-call | flops 3623878656 | bytes 5111808 | tf_op jit(solution)/shard_map/attn_backward/pallas_call | solution.py:633
  226.7 7.9 %attn_backward.7 = (f32[256,768]{1,0:T(8,128)S(1)}, bf16[256,768]{1,0:T(8,128)(2,1)}, bf16[256,768]{1,0:T(8,128)(2,1)S(1)}, bf16[256,768]{1,0:T(8,128)(2,1)S(1)}...) custom-call(f32[256,768]{1,0:T(8,128)S(1)} %get-tuple-element.538.grad_middle_ref, ...), custom_call_target="tpu_custom_call" | custom-call | flops 3623878656 | bytes 5111808 | tf_op jit(solution)/shard_map/attn_backward/pallas_call | solution.py:633
  236.8 3.4 %grad_qkv.1 = (bf16[8,160,768]{2,1,0:T(8,128)(2,1)S(1)}, bf16[8,160,768]{2,1,0:T(8,128)(2,1)S(1)}) custom-call(bf16[256,768]{1,0:T(8,128)(2,1)S(1)} %copy-done.53, bf16[256,768]{1,0:T(8,128)(2,1)S(1)} %copy-done.55, bf16[256,768]{1,0:T(8,128)(2,1)S(1)} %get-tuple-element.583.refs_2_, bf16[256,768]{1,0:T(8,128)(2,1)S(1)} %get-tuple-element.584.refs_3_, ...), custom_call_target="tpu_custom_call" | custom-call | flops 5435817984 | bytes 5505024 | tf_op jit(solution)/shard_map/grad_qkv/pallas_call | solution.py:798
  245.8 5.9 %collective-permute-done.59.refs_4_ = bf16[240,768]{1,0:T(8,128)(2,1)S(1)} collective-permute-done((bf16[240,768]{1,0:T(8,128)(2,1)S(1)}, bf16[240,768]{1,0:T(8,128)(2,1)S(1)}, u32[]{:S(2)}, u32[]{:S(2)}) %collective-permute-start.59) | collective-permute-done | bytes 368672 | tf_op jit(solution)/shard_map/ppermute | solution.py:45
  253.6 5.0 %collective-permute-done.48.down_ref = bf16[192,768]{1,0:T(8,128)(2,1)S(1)} collective-permute-done((bf16[192,768]{1,0:T(8,128)(2,1)S(1)}, bf16[192,768]{1,0:T(8,128)(2,1)S(1)}, u32[]{:S(2)}, u32[]{:S(2)}) %collective-permute-start.48) | collective-permute-done | bytes 294944 | tf_op jit(solution)/shard_map/ppermute | solution.py:49
  263.6 9.8 %collective-permute-done.53.refs_4_ = bf16[160,768]{1,0:T(8,128)(2,1)S(1)} collective-permute-done((bf16[160,768]{1,0:T(8,128)(2,1)S(1)}, bf16[160,768]{1,0:T(8,128)(2,1)S(1)}, u32[]{:S(2)}, u32[]{:S(2)}) %collective-permute-start.53) | collective-permute-done | bytes 245792 | tf_op jit(solution)/shard_map/ppermute | solution.py:45
  278.9 3.8 %collective-permute-done.55.refs_4_ = bf16[160,768]{1,0:T(8,128)(2,1)S(1)} collective-permute-done((bf16[160,768]{1,0:T(8,128)(2,1)S(1)}, bf16[160,768]{1,0:T(8,128)(2,1)S(1)}, u32[]{:S(2)}, u32[]{:S(2)}) %collective-permute-start.55) | collective-permute-done | bytes 245792 | tf_op jit(solution)/shard_map/ppermute | solution.py:45
  286.7 2.8 maximum_bitcast_fusion
  291.7 2.0 scatter_sum.4
  296.1 1.9 scatter_sum.3
  (276 shorter events, 79.0 us)
Async XLA Ops:
  4.0 10.6 %collective-permute-start = (bf16[208,768]{1,0:T(8,128)(2,1)S(1)}, bf16[208,768]{1,0:T(8,128)(2,1)S(1)}, u32[]{:S(2)}, u32[]{:S(2)}) collective-permute-start(bf16[208,768]{1,0:T(8,128)(2,1)S(1)} %pack_first.1.refs_0_), channel_id=1, source_target_pairs={{0,2},{1,3},{4,0},{5,1},{8,4},{9,5},{12,8},{13,9},{14,12},{15,13},... | collective-permute-start | bytes 958472 | tf_op jit(solution)/shard_map/ppermute | solution.py:49
  7.0 9.0 %collective-permute-start.1 = (bf16[208,768]{1,0:T(8,128)(2,1)S(1)}, bf16[208,768]{1,0:T(8,128)(2,1)S(1)}, u32[]{:S(2)}, u32[]{:S(2)}) collective-permute-start(bf16[208,768]{1,0:T(8,128)(2,1)S(1)} %pack_first.1.refs_0_), channel_id=1, source_target_pairs={{0,4},{1,5},{4,8},{5,9},{8,12},{9,13},{12,14},{13,15},{14,10},{15,... | collective-permute-start | bytes 958472 | tf_op jit(solution)/shard_map/ppermute | solution.py:45
  7.2 8.9 %collective-permute-start.2 = (bf16[208,768]{1,0:T(8,128)(2,1)S(1)}, bf16[208,768]{1,0:T(8,128)(2,1)S(1)}, u32[]{:S(2)}, u32[]{:S(2)}) collective-permute-start(bf16[208,768]{1,0:T(8,128)(2,1)S(1)} %pack_first.1.refs_0_), channel_id=1, source_target_pairs={{0,1},{1,0},{2,3},{3,2},{4,5},{5,4},{6,7},{7,6},{8,9},{9,8},{10,11... | collective-permute-start | bytes 958472 | tf_op jit(solution)/shard_map/ppermute | solution.py:53
  16.0 8.1 %collective-permute-start.3 = (bf16[208,768]{1,0:T(8,128)(2,1)S(1)}, bf16[208,768]{1,0:T(8,128)(2,1)S(1)}, u32[]{:S(2)}, u32[]{:S(2)}) collective-permute-start(bf16[208,768]{1,0:T(8,128)(2,1)S(1)} %collective-permute-done.refs_2_), channel_id=1, source_target_pairs={{0,2},{1,3},{4,0},{5,1},{8,4},{9,5},{12,8},{13,9},{14,12},{15,13},... | collective-permute-start | bytes 958472 | tf_op jit(solution)/shard_map/ppermute | solution.py:49
  27.0 7.9 %collective-permute-start.8 = (bf16[208,768]{1,0:T(8,128)(2,1)S(1)}, bf16[208,768]{1,0:T(8,128)(2,1)S(1)}, u32[]{:S(2)}, u32[]{:S(2)}) collective-permute-start(bf16[208,768]{1,0:T(8,128)(2,1)S(1)} %collective-permute-done.4.refs_14_), channel_id=1, source_target_pairs={{0,4},{1,5},{4,8},{5,9},{8,12},{9,13},{12,14},{13,15},{14,10},{15,... | collective-permute-start | bytes 958472 | tf_op jit(solution)/shard_map/ppermute | solution.py:45
  37.1 12.4 %collective-permute-start.11 = (bf16[384,768]{1,0:T(8,128)(2,1)S(1)}, bf16[384,768]{1,0:T(8,128)(2,1)S(1)}, u32[]{:S(2)}, u32[]{:S(2)}) collective-permute-start(bf16[384,768]{1,0:T(8,128)(2,1)S(1)} %pack_second.1.refs_0_), channel_id=1, source_target_pairs={{0,2},{1,3},{4,0},{5,1},{8,4},{9,5},{12,8},{13,9},{14,12},{15,13},... | collective-permute-start | bytes 1769480 | tf_op jit(solution)/shard_map/ppermute | solution.py:49
  38.7 11.3 %collective-permute-start.12 = (bf16[384,768]{1,0:T(8,128)(2,1)S(1)}, bf16[384,768]{1,0:T(8,128)(2,1)S(1)}, u32[]{:S(2)}, u32[]{:S(2)}) collective-permute-start(bf16[384,768]{1,0:T(8,128)(2,1)S(1)} %pack_second.1.refs_0_), channel_id=1, source_target_pairs={{0,4},{1,5},{4,8},{5,9},{8,12},{9,13},{12,14},{13,15},{14,10},{15,... | collective-permute-start | bytes 1769480 | tf_op jit(solution)/shard_map/ppermute | solution.py:45
  39.2 10.9 %collective-permute-start.13 = (bf16[384,768]{1,0:T(8,128)(2,1)S(1)}, bf16[384,768]{1,0:T(8,128)(2,1)S(1)}, u32[]{:S(2)}, u32[]{:S(2)}) collective-permute-start(bf16[384,768]{1,0:T(8,128)(2,1)S(1)} %pack_second.1.refs_0_), channel_id=1, source_target_pairs={{0,1},{1,0},{2,3},{3,2},{4,5},{5,4},{6,7},{7,6},{8,9},{9,8},{10,11... | collective-permute-start | bytes 1769480 | tf_op jit(solution)/shard_map/ppermute | solution.py:53
  50.0 19.8 %collective-permute-start.20 = (bf16[384,768]{1,0:T(8,128)(2,1)S(1)}, bf16[384,768]{1,0:T(8,128)(2,1)S(1)}, u32[]{:S(2)}, u32[]{:S(2)}) collective-permute-start(bf16[384,768]{1,0:T(8,128)(2,1)S(1)} %collective-permute-done.11.refs_2_), channel_id=1, source_target_pairs={{0,2},{1,3},{4,0},{5,1},{8,4},{9,5},{12,8},{13,9},{14,12},{15,13},... | collective-permute-start | bytes 1769480 | tf_op jit(solution)/shard_map/ppermute | solution.py:49
  51.4 18.5 %collective-permute-start.21 = (bf16[384,768]{1,0:T(8,128)(2,1)S(1)}, bf16[384,768]{1,0:T(8,128)(2,1)}, u32[]{:S(2)}, u32[]{:S(2)}) collective-permute-start(bf16[384,768]{1,0:T(8,128)(2,1)S(1)} %collective-permute-done.12.refs_16_), channel_id=1, source_target_pairs={{0,4},{1,5},{4,8},{5,9},{8,12},{9,13},{12,14},{13,15},{14,10},{15,... | collective-permute-start | bytes 1769480 | tf_op jit(solution)/shard_map/ppermute | solution.py:45
  52.2 17.7 %collective-permute-start.22 = (bf16[384,768]{1,0:T(8,128)(2,1)S(1)}, bf16[384,768]{1,0:T(8,128)(2,1)S(1)}, u32[]{:S(2)}, u32[]{:S(2)}) collective-permute-start(bf16[384,768]{1,0:T(8,128)(2,1)S(1)} %collective-permute-done.11.refs_2_), channel_id=1, source_target_pairs={{0,1},{1,0},{2,3},{3,2},{4,5},{5,4},{6,7},{7,6},{8,9},{9,8},{10,11... | collective-permute-start | bytes 1769480 | tf_op jit(solution)/shard_map/ppermute | solution.py:53
  52.2 18.5 %collective-permute-start.23 = (bf16[384,768]{1,0:T(8,128)(2,1)S(1)}, bf16[384,768]{1,0:T(8,128)(2,1)S(1)}, u32[]{:S(2)}, u32[]{:S(2)}) collective-permute-start(bf16[384,768]{1,0:T(8,128)(2,1)S(1)} %collective-permute-done.12.refs_16_), channel_id=1, source_target_pairs={{0,1},{1,0},{2,3},{3,2},{4,5},{5,4},{6,7},{7,6},{8,9},{9,8},{10,11... | collective-permute-start | bytes 1769480 | tf_op jit(solution)/shard_map/ppermute | solution.py:53
  71.5 15.5 %collective-permute-start.27 = (bf16[384,768]{1,0:T(8,128)(2,1)}, bf16[384,768]{1,0:T(8,128)(2,1)S(1)}, u32[]{:S(2)}, u32[]{:S(2)}) collective-permute-start(bf16[384,768]{1,0:T(8,128)(2,1)} %collective-permute-done.21.refs_14_), channel_id=1, source_target_pairs={{0,4},{1,5},{4,8},{5,9},{8,12},{9,13},{12,14},{13,15},{14,10},{15,... | collective-permute-start | bytes 1769480 | tf_op jit(solution)/shard_map/ppermute | solution.py:45
  72.0 15.5 %collective-permute-start.25 = (bf16[384,768]{1,0:T(8,128)(2,1)S(1)}, bf16[384,768]{1,0:T(8,128)(2,1)S(1)}, u32[]{:S(2)}, u32[]{:S(2)}) collective-permute-start(bf16[384,768]{1,0:T(8,128)(2,1)S(1)} %collective-permute-done.20.refs_4_), channel_id=1, source_target_pairs={{0,2},{1,3},{4,0},{5,1},{8,4},{9,5},{12,8},{13,9},{14,12},{15,13},... | collective-permute-start | bytes 1769480 | tf_op jit(solution)/shard_map/ppermute | solution.py:49
  73.6 15.8 %collective-permute-start.24 = (bf16[384,768]{1,0:T(8,128)(2,1)S(1)}, bf16[384,768]{1,0:T(8,128)(2,1)S(1)}, u32[]{:S(2)}, u32[]{:S(2)}) collective-permute-start(bf16[384,768]{1,0:T(8,128)(2,1)S(1)} %collective-permute-done.20.refs_4_), channel_id=1, source_target_pairs={{0,1},{1,0},{2,3},{3,2},{4,5},{5,4},{6,7},{7,6},{8,9},{9,8},{10,11... | collective-permute-start | bytes 1769480 | tf_op jit(solution)/shard_map/ppermute | solution.py:53
  73.6 25.0 %collective-permute-start.33 = (bf16[384,768]{1,0:T(8,128)(2,1)}, bf16[384,768]{1,0:T(8,128)(2,1)}, u32[]{:S(2)}, u32[]{:S(2)}) collective-permute-start(bf16[384,768]{1,0:T(8,128)(2,1)} %collective-permute-done.21.refs_14_), channel_id=1, source_target_pairs={{0,1},{1,0},{2,3},{3,2},{4,5},{5,4},{6,7},{7,6},{8,9},{9,8},{10,11... | collective-permute-start | bytes 1769480 | tf_op jit(solution)/shard_map/ppermute | solution.py:53
  87.0 8.2 %collective-permute-start.28 = (bf16[192,768]{1,0:T(8,128)(2,1)S(1)}, bf16[192,768]{1,0:T(8,128)(2,1)}, u32[]{:S(2)}, u32[]{:S(2)}) collective-permute-start(bf16[192,768]{1,0:T(8,128)(2,1)S(1)} %slice.48), channel_id=1, source_target_pairs={{0,4},{1,5},{4,8},{5,9},{8,12},{9,13},{12,14},{13,15},{14,10},{15,... | collective-permute-start | bytes 884744 | tf_op jit(solution)/shard_map/ppermute | solution.py:45
  87.5 11.1 %collective-permute-start.26 = (bf16[384,768]{1,0:T(8,128)(2,1)S(1)}, bf16[384,768]{1,0:T(8,128)(2,1)}, u32[]{:S(2)}, u32[]{:S(2)}) collective-permute-start(bf16[384,768]{1,0:T(8,128)(2,1)S(1)} %collective-permute-done.25.refs_6_), channel_id=1, source_target_pairs={{0,1},{1,0},{2,3},{3,2},{4,5},{5,4},{6,7},{7,6},{8,9},{9,8},{10,11... | collective-permute-start | bytes 1769480 | tf_op jit(solution)/shard_map/ppermute | solution.py:53
  87.5 9.8 %collective-permute-start.29 = (bf16[192,768]{1,0:T(8,128)(2,1)S(1)}, bf16[192,768]{1,0:T(8,128)(2,1)}, u32[]{:S(2)}, u32[]{:S(2)}) collective-permute-start(bf16[192,768]{1,0:T(8,128)(2,1)S(1)} %slice.49), channel_id=1, source_target_pairs={{0,2},{1,3},{4,0},{5,1},{8,4},{9,5},{12,8},{13,9},{14,12},{15,13},... | collective-permute-start | bytes 884744 | tf_op jit(solution)/shard_map/ppermute | solution.py:49
  90.2 9.0 %collective-permute-start.32 = (bf16[384,768]{1,0:T(8,128)(2,1)S(1)}, bf16[384,768]{1,0:T(8,128)(2,1)}, u32[]{:S(2)}, u32[]{:S(2)}) collective-permute-start(bf16[384,768]{1,0:T(8,128)(2,1)S(1)} %collective-permute-done.27.refs_12_), channel_id=1, source_target_pairs={{0,1},{1,0},{2,3},{3,2},{4,5},{5,4},{6,7},{7,6},{8,9},{9,8},{10,11... | collective-permute-start | bytes 1769480 | tf_op jit(solution)/shard_map/ppermute | solution.py:53
  112.8 13.0 %collective-permute-start.34 = (bf16[256,768]{1,0:T(8,128)(2,1)S(1)}, bf16[256,768]{1,0:T(8,128)(2,1)S(1)}, u32[]{:S(2)}, u32[]{:S(2)}) collective-permute-start(bf16[256,768]{1,0:T(8,128)(2,1)S(1)} %mlp_down.3), channel_id=1, source_target_pairs={{0,16},{1,17},{2,18},{3,19},{4,20},{5,21},{6,22},{7,23},{8,24},{9,... | collective-permute-start | bytes 1179656 | tf_op jit(solution)/shard_map/ppermute | solution.py:886
  122.7 11.1 %collective-permute-start.35 = (bf16[256,768]{1,0:T(8,128)(2,1)S(1)}, bf16[256,768]{1,0:T(8,128)(2,1)S(1)}, u32[]{:S(2)}, u32[]{:S(2)}) collective-permute-start(bf16[256,768]{1,0:T(8,128)(2,1)S(1)} %mlp_down.4), channel_id=1, source_target_pairs={{0,16},{1,17},{2,18},{3,19},{4,20},{5,21},{6,22},{7,23},{8,24},{9,... | collective-permute-start | bytes 1179656 | tf_op jit(solution)/shard_map/ppermute | solution.py:886
  165.7 12.2 %collective-permute-start.36 = (bf16[256,768]{1,0:T(8,128)(2,1)S(1)}, bf16[256,768]{1,0:T(8,128)(2,1)S(1)}, u32[]{:S(2)}, u32[]{:S(2)}) collective-permute-start(bf16[256,768]{1,0:T(8,128)(2,1)S(1)} %get-tuple-element.430), channel_id=1, source_target_pairs={{16,0},{17,1},{18,2},{19,3},{20,4},{21,5},{22,6},{23,7},{24,8},{25... | collective-permute-start | bytes 1179656 | tf_op jit(solution)/shard_map/ppermute | solution.py:905
  175.2 12.1 %collective-permute-start.37 = (bf16[256,768]{1,0:T(8,128)(2,1)S(1)}, bf16[256,768]{1,0:T(8,128)(2,1)S(1)}, u32[]{:S(2)}, u32[]{:S(2)}) collective-permute-start(bf16[256,768]{1,0:T(8,128)(2,1)S(1)} %get-tuple-element.444), channel_id=1, source_target_pairs={{16,0},{17,1},{18,2},{19,3},{20,4},{21,5},{22,6},{23,7},{24,8},{25... | collective-permute-start | bytes 1179656 | tf_op jit(solution)/shard_map/ppermute | solution.py:905
  202.8 8.1 %collective-permute-start.39 = (bf16[96,768]{1,0:T(8,128)(2,1)S(1)}, bf16[96,768]{1,0:T(8,128)(2,1)S(1)}, u32[]{:S(2)}, u32[]{:S(2)}) collective-permute-start(bf16[96,768]{1,0:T(8,128)(2,1)S(1)} %get-tuple-element.479), channel_id=1, source_target_pairs={{0,2},{1,3},{4,0},{5,1},{8,4},{9,5},{12,8},{13,9},{14,12},{15,13},... | collective-permute-start | bytes 442376 | tf_op jit(solution)/shard_map/ppermute | solution.py:49
  211.2 10.8 %collective-permute-start.43 = (bf16[8,240,768]{2,1,0:T(8,128)(2,1)S(1)}, bf16[8,240,768]{2,1,0:T(8,128)(2,1)S(1)}, u32[]{:S(2)}, u32[]{:S(2)}) collective-permute-start(bf16[8,240,768]{2,1,0:T(8,128)(2,1)S(1)} %get-tuple-element.505), channel_id=1, source_target_pairs={{0,1},{1,0},{2,3},{3,2},{4,5},{5,4},{6,7},{7,6},{8,9},{9,8},{10,11... | collective-permute-start | bytes 8847368 | tf_op jit(solution)/shard_map/ppermute | solution.py:53
  211.7 10.0 %collective-permute-start.41 = (bf16[192,768]{1,0:T(8,128)(2,1)S(1)}, bf16[192,768]{1,0:T(8,128)(2,1)S(1)}, u32[]{:S(2)}, u32[]{:S(2)}) collective-permute-start(bf16[192,768]{1,0:T(8,128)(2,1)S(1)} %get-tuple-element.497), channel_id=1, source_target_pairs={{0,2},{1,3},{4,0},{5,1},{8,4},{9,5},{12,8},{13,9},{14,12},{15,13},... | collective-permute-start | bytes 884744 | tf_op jit(solution)/shard_map/ppermute | solution.py:49
  213.3 8.7 %collective-permute-start.42 = (bf16[192,768]{1,0:T(8,128)(2,1)S(1)}, bf16[192,768]{1,0:T(8,128)(2,1)S(1)}, u32[]{:S(2)}, u32[]{:S(2)}) collective-permute-start(bf16[192,768]{1,0:T(8,128)(2,1)S(1)} %get-tuple-element.498), channel_id=1, source_target_pairs={{0,4},{1,5},{4,8},{5,9},{8,12},{9,13},{12,14},{13,15},{14,10},{15,... | collective-permute-start | bytes 884744 | tf_op jit(solution)/shard_map/ppermute | solution.py:45
  222.2 13.2 %collective-permute-start.44 = (bf16[192,768]{1,0:T(8,128)(2,1)S(1)}, bf16[192,768]{1,0:T(8,128)(2,1)S(1)}, u32[]{:S(2)}, u32[]{:S(2)}) collective-permute-start(bf16[192,768]{1,0:T(8,128)(2,1)S(1)} %get-tuple-element.523), channel_id=1, source_target_pairs={{0,2},{1,3},{4,0},{5,1},{8,4},{9,5},{12,8},{13,9},{14,12},{15,13},... | collective-permute-start | bytes 884744 | tf_op jit(solution)/shard_map/ppermute | solution.py:49
  223.6 11.9 %collective-permute-start.45 = (bf16[192,768]{1,0:T(8,128)(2,1)S(1)}, bf16[192,768]{1,0:T(8,128)(2,1)S(1)}, u32[]{:S(2)}, u32[]{:S(2)}) collective-permute-start(bf16[192,768]{1,0:T(8,128)(2,1)S(1)} %get-tuple-element.524), channel_id=1, source_target_pairs={{0,4},{1,5},{4,8},{5,9},{8,12},{9,13},{12,14},{13,15},{14,10},{15,... | collective-permute-start | bytes 884744 | tf_op jit(solution)/shard_map/ppermute | solution.py:45
  224.4 11.0 %collective-permute-start.46 = (bf16[128,768]{1,0:T(8,128)(2,1)S(1)}, bf16[128,768]{1,0:T(8,128)(2,1)S(1)}, u32[]{:S(2)}, u32[]{:S(2)}) collective-permute-start(bf16[128,768]{1,0:T(8,128)(2,1)S(1)} %get-tuple-element.531), channel_id=1, source_target_pairs={{0,2},{1,3},{4,0},{5,1},{8,4},{9,5},{12,8},{13,9},{14,12},{15,13},... | collective-permute-start | bytes 589832 | tf_op jit(solution)/shard_map/ppermute | solution.py:49
  225.8 9.7 %collective-permute-start.47 = (bf16[112,768]{1,0:T(8,128)(2,1)S(1)}, bf16[112,768]{1,0:T(8,128)(2,1)S(1)}, u32[]{:S(2)}, u32[]{:S(2)}) collective-permute-start(bf16[112,768]{1,0:T(8,128)(2,1)S(1)} %get-tuple-element.532), channel_id=1, source_target_pairs={{0,4},{1,5},{4,8},{5,9},{8,12},{9,13},{12,14},{13,15},{14,10},{15,... | collective-permute-start | bytes 516104 | tf_op jit(solution)/shard_map/ppermute | solution.py:45
  240.3 11.4 %collective-permute-start.59 = (bf16[240,768]{1,0:T(8,128)(2,1)S(1)}, bf16[240,768]{1,0:T(8,128)(2,1)S(1)}, u32[]{:S(2)}, u32[]{:S(2)}) collective-permute-start(bf16[240,768]{1,0:T(8,128)(2,1)S(1)} %get-tuple-element.610), channel_id=1, source_target_pairs={{0,4},{1,5},{4,8},{5,9},{8,12},{9,13},{12,14},{13,15},{14,10},{15,... | collective-permute-start | bytes 1105928 | tf_op jit(solution)/shard_map/ppermute | solution.py:45
  240.8 11.4 %collective-permute-start.60 = (bf16[240,768]{1,0:T(8,128)(2,1)S(1)}, bf16[240,768]{1,0:T(8,128)(2,1)S(1)}, u32[]{:S(2)}, u32[]{:S(2)}) collective-permute-start(bf16[240,768]{1,0:T(8,128)(2,1)S(1)} %get-tuple-element.611), channel_id=1, source_target_pairs={{0,2},{1,3},{4,0},{5,1},{8,4},{9,5},{12,8},{13,9},{14,12},{15,13},... | collective-permute-start | bytes 1105928 | tf_op jit(solution)/shard_map/ppermute | solution.py:49
  242.4 16.2 %collective-permute-start.48 = (bf16[192,768]{1,0:T(8,128)(2,1)S(1)}, bf16[192,768]{1,0:T(8,128)(2,1)S(1)}, u32[]{:S(2)}, u32[]{:S(2)}) collective-permute-start(bf16[192,768]{1,0:T(8,128)(2,1)S(1)} %get-tuple-element.579), channel_id=1, source_target_pairs={{0,2},{1,3},{4,0},{5,1},{8,4},{9,5},{12,8},{13,9},{14,12},{15,13},... | collective-permute-start | bytes 884744 | tf_op jit(solution)/shard_map/ppermute | solution.py:49
  243.7 17.1 %collective-permute-start.49 = (bf16[192,768]{1,0:T(8,128)(2,1)S(1)}, bf16[192,768]{1,0:T(8,128)(2,1)S(1)}, u32[]{:S(2)}, u32[]{:S(2)}) collective-permute-start(bf16[192,768]{1,0:T(8,128)(2,1)S(1)} %get-tuple-element.580), channel_id=1, source_target_pairs={{0,4},{1,5},{4,8},{5,9},{8,12},{9,13},{12,14},{13,15},{14,10},{15,... | collective-permute-start | bytes 884744 | tf_op jit(solution)/shard_map/ppermute | solution.py:45
  244.5 16.4 %collective-permute-start.51 = (bf16[80,768]{1,0:T(8,128)(2,1)S(1)}, bf16[80,768]{1,0:T(8,128)(2,1)S(1)}, u32[]{:S(2)}, u32[]{:S(2)}) collective-permute-start(bf16[80,768]{1,0:T(8,128)(2,1)S(1)} %get-tuple-element.597), channel_id=1, source_target_pairs={{0,2},{1,3},{4,0},{5,1},{8,4},{9,5},{12,8},{13,9},{14,12},{15,13},... | collective-permute-start | bytes 368648 | tf_op jit(solution)/shard_map/ppermute | solution.py:49
  251.7 9.1 %collective-permute-start.52 = (bf16[80,768]{1,0:T(8,128)(2,1)S(1)}, bf16[80,768]{1,0:T(8,128)(2,1)S(1)}, u32[]{:S(2)}, u32[]{:S(2)}) collective-permute-start(bf16[80,768]{1,0:T(8,128)(2,1)S(1)} %get-tuple-element.598), channel_id=1, source_target_pairs={{0,4},{1,5},{4,8},{5,9},{8,12},{9,13},{12,14},{13,15},{14,10},{15,... | collective-permute-start | bytes 368648 | tf_op jit(solution)/shard_map/ppermute | solution.py:45
  252.5 23.3 %collective-permute-start.61 = (bf16[240,768]{1,0:T(8,128)(2,1)S(1)}, bf16[240,768]{1,0:T(8,128)(2,1)S(1)}, u32[]{:S(2)}, u32[]{:S(2)}) collective-permute-start(bf16[240,768]{1,0:T(8,128)(2,1)S(1)} %get-tuple-element.612), channel_id=1, source_target_pairs={{0,4},{1,5},{4,8},{5,9},{8,12},{9,13},{12,14},{13,15},{14,10},{15,... | collective-permute-start | bytes 1105928 | tf_op jit(solution)/shard_map/ppermute | solution.py:45
  259.3 16.6 %collective-permute-start.62 = (bf16[240,768]{1,0:T(8,128)(2,1)S(1)}, bf16[240,768]{1,0:T(8,128)(2,1)S(1)}, u32[]{:S(2)}, u32[]{:S(2)}) collective-permute-start(bf16[240,768]{1,0:T(8,128)(2,1)S(1)} %get-tuple-element.613), channel_id=1, source_target_pairs={{0,2},{1,3},{4,0},{5,1},{8,4},{9,5},{12,8},{13,9},{14,12},{15,13},... | collective-permute-start | bytes 1105928 | tf_op jit(solution)/shard_map/ppermute | solution.py:49
  261.6 11.8 %collective-permute-start.53 = (bf16[160,768]{1,0:T(8,128)(2,1)S(1)}, bf16[160,768]{1,0:T(8,128)(2,1)S(1)}, u32[]{:S(2)}, u32[]{:S(2)}) collective-permute-start(bf16[160,768]{1,0:T(8,128)(2,1)S(1)} %get-tuple-element.603), channel_id=1, source_target_pairs={{0,4},{1,5},{4,8},{5,9},{8,12},{9,13},{12,14},{13,15},{14,10},{15,... | collective-permute-start | bytes 737288 | tf_op jit(solution)/shard_map/ppermute | solution.py:45
  262.0 11.6 %collective-permute-start.54 = (bf16[160,768]{1,0:T(8,128)(2,1)S(1)}, bf16[160,768]{1,0:T(8,128)(2,1)S(1)}, u32[]{:S(2)}, u32[]{:S(2)}) collective-permute-start(bf16[160,768]{1,0:T(8,128)(2,1)S(1)} %get-tuple-element.604), channel_id=1, source_target_pairs={{0,2},{1,3},{4,0},{5,1},{8,4},{9,5},{12,8},{13,9},{14,12},{15,13},... | collective-permute-start | bytes 737288 | tf_op jit(solution)/shard_map/ppermute | solution.py:49
  273.8 8.9 %collective-permute-start.55 = (bf16[160,768]{1,0:T(8,128)(2,1)S(1)}, bf16[160,768]{1,0:T(8,128)(2,1)S(1)}, u32[]{:S(2)}, u32[]{:S(2)}) collective-permute-start(bf16[160,768]{1,0:T(8,128)(2,1)S(1)} %get-tuple-element.605), channel_id=1, source_target_pairs={{0,4},{1,5},{4,8},{5,9},{8,12},{9,13},{12,14},{13,15},{14,10},{15,... | collective-permute-start | bytes 737288 | tf_op jit(solution)/shard_map/ppermute | solution.py:45
  274.8 8.9 %collective-permute-start.56 = (bf16[160,768]{1,0:T(8,128)(2,1)S(1)}, bf16[160,768]{1,0:T(8,128)(2,1)S(1)}, u32[]{:S(2)}, u32[]{:S(2)}) collective-permute-start(bf16[160,768]{1,0:T(8,128)(2,1)S(1)} %get-tuple-element.606), channel_id=1, source_target_pairs={{0,2},{1,3},{4,0},{5,1},{8,4},{9,5},{12,8},{13,9},{14,12},{15,13},... | collective-permute-start | bytes 737288 | tf_op jit(solution)/shard_map/ppermute | solution.py:49
  276.9 13.7 %collective-permute-start.63 = (bf16[240,768]{1,0:T(8,128)(2,1)}, bf16[240,768]{1,0:T(8,128)(2,1)S(1)}, u32[]{:S(2)}, u32[]{:S(2)}) collective-permute-start(bf16[240,768]{1,0:T(8,128)(2,1)} %get-tuple-element.614), channel_id=1, source_target_pairs={{0,4},{1,5},{4,8},{5,9},{8,12},{9,13},{12,14},{13,15},{14,10},{15,... | collective-permute-start | bytes 1105928 | tf_op jit(solution)/shard_map/ppermute | solution.py:45
  277.9 13.8 %collective-permute-start.64 = (bf16[240,768]{1,0:T(8,128)(2,1)}, bf16[240,768]{1,0:T(8,128)(2,1)}, u32[]{:S(2)}, u32[]{:S(2)}) collective-permute-start(bf16[240,768]{1,0:T(8,128)(2,1)} %get-tuple-element.615), channel_id=1, source_target_pairs={{0,2},{1,3},{4,0},{5,1},{8,4},{9,5},{12,8},{13,9},{14,12},{15,13},... | collective-permute-start | bytes 1105928 | tf_op jit(solution)/shard_map/ppermute | solution.py:49
  284.6 10.1 %collective-permute-start.57 = (bf16[160,768]{1,0:T(8,128)(2,1)}, bf16[160,768]{1,0:T(8,128)(2,1)}, u32[]{:S(2)}, u32[]{:S(2)}) collective-permute-start(bf16[160,768]{1,0:T(8,128)(2,1)} %get-tuple-element.607), channel_id=1, source_target_pairs={{0,4},{1,5},{4,8},{5,9},{8,12},{9,13},{12,14},{13,15},{14,10},{15,... | collective-permute-start | bytes 737288 | tf_op jit(solution)/shard_map/ppermute | solution.py:45
  286.1 8.6 %collective-permute-start.58 = (bf16[160,768]{1,0:T(8,128)(2,1)}, bf16[160,768]{1,0:T(8,128)(2,1)}, u32[]{:S(2)}, u32[]{:S(2)}) collective-permute-start(bf16[160,768]{1,0:T(8,128)(2,1)} %get-tuple-element.608), channel_id=1, source_target_pairs={{0,2},{1,3},{4,0},{5,1},{8,4},{9,5},{12,8},{13,9},{14,12},{15,13},... | collective-permute-start | bytes 737288 | tf_op jit(solution)/shard_map/ppermute | solution.py:49
  (86 other events, 669.0 us)
